TPU v7x, 32 devices: a whole 2x2x4 slice. The times are simulated.
32 devices in a mesh: seq: 8 (over z, core), chan: 4 (over y, x).
Axes of the slice: x: 2, y: 2, z: 4, core: 2. Of those that a mesh axis runs over, the one named last changes fastest.
Arguments:
- values: bfloat16 [2048, 4096], P('seq', 'chan'), may hold values from -6 to 6
- gates: bfloat16 [2048, 4096], P('seq', 'chan'), may hold values from -6 to 6
- filters: bfloat16 [1024, 4096], P(None, 'chan'), may hold values from -2 to 2
- skip: float32 [4096], P('chan'), may hold values from -4 to 4
- out_weight: bfloat16 [4096, 4096], P(('seq', 'chan')), may hold values from -0.09375 to 0.09375
Outputs:
- projected: bfloat16 [2048, 4096], P(('seq', 'chan'))
All inputs are finite; a program needn't handle non-finite values.
Results may differ from a plain program's by a relative error of at most 0.009.
Values may be sent and summed in bfloat16 or wider, within the bound.
No kernel may reach another device: no remote copies, remote signals or barrier semaphores. Data moves between devices by JAX's collectives and lax.ppermute only.
A program may use at most 192 MiB of HBM per device.

v0:
```python
import functools
import math

import jax
import jax.numpy as jnp
from jax import lax
from jax.experimental import pallas as pl
from jax.experimental.pallas import tpu as pltpu
from jax.sharding import PartitionSpec as P

AXES = ("seq", "chan")
F32 = jnp.float32
BF16 = jnp.bfloat16


def permute(value, move):
    pairs, chans = lax.axis_size("seq") // 2, lax.axis_size("chan")
    route = []
    for pair in range(pairs):
        for core in range(2):
            for chan in range(chans):
                target = move(pair, core, chan)
                if target is not None and 0 <= target[0] < pairs:
                    route.append(
                        (
                            (pair * 2 + core) * chans + chan,
                            (target[0] * 2 + target[1]) * chans + target[2],
                        )
                    )
    return lax.ppermute(value, AXES, route)


def tables(block):
    order = jnp.concatenate([jnp.arange(0, block, 2), jnp.arange(1, block, 2)])
    phase = (2 * order[:, None] + 1) * jnp.arange(block)[None, :] % (4 * block)
    angle = phase.astype(F32) * (math.pi / (2 * block))
    return jnp.concatenate([jnp.cos(angle), jnp.sin(angle)], axis=0)


def conv_kernel(lags, core_ref, table_ref, back_ref, skip_ref, gates_ref, filters_ref, *rest):
    *block_refs, out_ref = rest
    block = gates_ref.shape[0]
    half = block // 2
    odd = core_ref[0] == 1
    reach = lags // 2

    def transform(operand):
        return jnp.dot(table_ref[...], operand, preferred_element_type=F32)

    direct = block_refs[: reach + 1]
    crossed = block_refs[reach + 1 :]
    cos_parts, sin_parts = [], []
    for lag in range(lags + 1):
        if lag % 2 == 0:
            operand = direct[lag // 2][...]
        else:
            operand = jnp.where(odd, crossed[lag // 2][...], crossed[lag // 2 + 1][...])
        both = transform(operand)
        cos_parts.append(both[:block])
        sin_parts.append(both[block:])
    real = imag = 0.0
    for lag in range(lags):
        both = transform(filters_ref[lag * block : (lag + 1) * block, :])
        tap_cos, tap_sin = both[:block], both[block:]
        near_cos, near_sin = cos_parts[lag], sin_parts[lag]
        far_cos, far_sin = cos_parts[lag + 1], sin_parts[lag + 1]
        window_cos = jnp.concatenate(
            [near_cos[:half] + far_sin[:half], near_cos[half:] - far_sin[half:]], axis=0
        )
        window_sin = jnp.concatenate(
            [near_sin[:half] - far_cos[:half], near_sin[half:] + far_cos[half:]], axis=0
        )
        real = real + tap_cos * window_cos - tap_sin * window_sin
        imag = imag + tap_cos * window_sin + tap_sin * window_cos
    spectrum = jnp.concatenate([real, imag], axis=0).astype(BF16)
    filtered = jnp.dot(back_ref[...], spectrum, preferred_element_type=F32) * (1.0 / block)
    filtered = filtered + skip_ref[...] * direct[0][...].astype(F32)
    out_ref[...] = (gates_ref[...].astype(F32) * filtered).astype(BF16)


def convolve(core, gates, filters, skip, direct, crossed):
    block, width = gates.shape
    taps = filters.shape[0]
    lags = taps // block
    table = tables(block)
    tile = min(width, 256)

    def column(rows):
        return pl.BlockSpec((rows, tile), lambda i, *_: (0, i))

    def whole(rows, cols):
        return pl.BlockSpec((rows, cols), lambda i, *_: (0, 0))

    blocks = [*direct, *crossed]
    return pl.pallas_call(
        functools.partial(conv_kernel, lags),
        grid_spec=pltpu.PrefetchScalarGridSpec(
            num_scalar_prefetch=1,
            grid=(width // tile,),
            in_specs=[
                whole(2 * block, block),
                whole(block, 2 * block),
                column(1),
                column(block),
                column(taps),
                *[column(block) for _ in blocks],
            ],
            out_specs=column(block),
        ),
        out_shape=jax.ShapeDtypeStruct((block, width), BF16),
        compiler_params=pltpu.CompilerParams(vmem_limit_bytes=40 * 2**20),
        cost_estimate=pl.CostEstimate(
            flops=2 * (3 * lags + 3) * 2 * block * block * width,
            bytes_accessed=2 * width * (taps + (len(blocks) + 2) * block),
            transcendentals=0,
        ),
        name="conv",
    )(
        core.reshape(1),
        table.astype(BF16),
        table.T.astype(BF16),
        skip.reshape(1, width),
        gates,
        filters,
        *blocks,
    )


def project_kernel(count, offsets_ref, *refs):
    act_refs, piece_refs = refs[:count], refs[count : 2 * count]
    out_ref, held_ref = refs[2 * count :]
    rows = act_refs[0].shape[0]
    depth = piece_refs[0].shape[0] // 2

    @pl.when(pl.program_id(0) == 0)
    def _():
        for index, act in enumerate(act_refs):
            if depth % 128:
                held_ref[index * rows : (index + 1) * rows, :] = act[...]
                continue
            for slot in range(2 * count):
                start = pl.multiple_of(offsets_ref[slot], depth)
                held_ref[index * rows : (index + 1) * rows, slot * depth : (slot + 1) * depth] = (
                    act[:, pl.ds(start, depth)]
                )

    weight = jnp.concatenate([piece[...] for piece in piece_refs], axis=0)
    out_ref[...] = jnp.dot(held_ref[...], weight, preferred_element_type=F32)


def project(offsets, acts, pieces):
    count = len(acts)
    rows, depth = acts[0].shape
    cols = pieces[0].shape[1]
    tile = min(cols, 512)
    slot = depth // (2 * count)
    if slot % 128:
        acts = [
            jnp.concatenate(
                [
                    lax.dynamic_slice_in_dim(act, offsets[index], slot, axis=1)
                    for index in range(2 * count)
                ],
                axis=1,
            )
            for act in acts
        ]
    return pl.pallas_call(
        functools.partial(project_kernel, count),
        grid_spec=pltpu.PrefetchScalarGridSpec(
            num_scalar_prefetch=1,
            grid=(cols // tile,),
            in_specs=[
                *[pl.BlockSpec((rows, depth), lambda i, *_: (0, 0)) for _ in acts],
                *[
                    pl.BlockSpec((piece.shape[0], tile), lambda i, *_: (0, i))
                    for piece in pieces
                ],
            ],
            out_specs=pl.BlockSpec((count * rows, tile), lambda i, *_: (0, i)),
            scratch_shapes=[pltpu.VMEM((count * rows, depth), BF16)],
        ),
        out_shape=jax.ShapeDtypeStruct((count * rows, cols), F32),
        compiler_params=pltpu.CompilerParams(vmem_limit_bytes=40 * 2**20),
        cost_estimate=pl.CostEstimate(
            flops=2 * count * rows * depth * cols,
            bytes_accessed=2 * depth * cols + 6 * count * rows * cols,
            transcendentals=0,
        ),
        name="project",
    )(offsets, *acts, *pieces)


def body(values, gates, filters, skip, out_weight):
    pairs, chans = lax.axis_size("seq") // 2, lax.axis_size("chan")
    seq, chan = lax.axis_index("seq"), lax.axis_index("chan")
    pair, core = seq // 2, seq % 2
    block = values.shape[0]
    lags = filters.shape[0] // block
    own_rows, model = out_weight.shape
    half = model // 2

    mine = lax.dynamic_slice_in_dim(out_weight, core * half, half, axis=1)
    other = lax.dynamic_slice_in_dim(out_weight, (1 - core) * half, half, axis=1)

    direct = [values]
    for _ in range(lags // 2):
        direct.append(permute(direct[-1], lambda p, k, c: (p + 1, k, c)))
    crossed = [permute(held, lambda p, k, c: (p, 1 - k, c)) for held in direct]

    swapped = permute(other, lambda p, k, c: (p, 1 - k, c))
    pieces = [jnp.concatenate([mine, swapped], axis=0)]
    for step in range(1, chans):
        pieces.append(permute(pieces[0], lambda p, k, c, step=step: (p, k, c ^ step)))
    far_pieces = [permute(piece, lambda p, k, c: (p, 1 - k, c)) for piece in pieces]

    gated = convolve(core, gates, filters, skip, direct, crossed)

    rows = block // chans
    acts = []
    for step in range(chans):
        part = lax.dynamic_slice_in_dim(gated, (pair + step) % chans * rows, rows, axis=0)
        acts.append(permute(part, lambda p, k, c, step=step: (c, k, (p + step) % chans)))

    def offsets(first):
        return jnp.stack(
            [
                (which * chans + (chan ^ step)) * own_rows
                for step in range(chans)
                for which in (first, 1 - first)
            ]
        ).astype(jnp.int32)

    totals = []
    for first, weight in ((core, pieces), (1 - core, far_pieces)):
        partial = project(offsets(first), acts, weight).reshape(chans, rows, half)

        def share(target, partial=partial):
            return lax.dynamic_index_in_dim(
                partial, (chan - target) % chans, axis=0, keepdims=False
            )

        up = down = None
        for step in range(1, pairs):
            send_up = share(pairs + pair - step)
            send_down = share(pair - pairs + step)
            if step > 1:
                send_up = send_up + up.astype(F32)
                send_down = send_down + down.astype(F32)
            up = permute(
                send_up.astype(BF16),
                lambda p, k, c, step=step: (p + 1, k, c) if p < step else None,
            )
            down = permute(
                send_down.astype(BF16),
                lambda p, k, c, step=step: (p - 1, k, c) if pairs - 1 - p < step else None,
            )
        totals.append((share(pair) + up.astype(F32) + down.astype(F32)).astype(BF16))
    swap = core == 1
    return jnp.concatenate(
        [jnp.where(swap, totals[1], totals[0]), jnp.where(swap, totals[0], totals[1])], axis=1
    )


def solution(mesh):
    in_specs = (
        P("seq", "chan"),
        P("seq", "chan"),
        P(None, "chan"),
        P("chan"),
        P(("seq", "chan"), None),
    )
    out_specs = P(("seq", "chan"), None)
    return jax.shard_map(body, mesh=mesh, in_specs=in_specs, out_specs=out_specs, check_vma=False)
```

profile of v0, /device:TPU:4, one launch (start us, length us, event | category | flops | bytes accessed | tf_op | source)
XLA Modules:
  0.0 175.9 jit_solution(4288596693977491033)
XLA Ops:
  0.0 3.6 %collective-permute-start = (bf16[256,1024]{1,0:T(8,128)(2,1)}, bf16[256,1024]{1,0:T(8,128)(2,1)S(1)}, u32[]{:S(2)}, u32[]{:S(2)}) collective-permute-start(bf16[256,1024]{1,0:T(8,128)(2,1)} %rest_0_.1), channel_id=1, source_target_pairs={{0,8},{1,9},{2,10},{3,11},{4,12},{5,13},{6,14},{7,15},{8,16},{9,17... | collective-permute-start | bytes 1572872 | tf_op jit(solution)/shard_map/ppermute | solution.py:30
  5.6 9.5 %collective-permute-done.rest_1_ = bf16[256,1024]{1,0:T(8,128)(2,1)S(1)} collective-permute-done((bf16[256,1024]{1,0:T(8,128)(2,1)}, bf16[256,1024]{1,0:T(8,128)(2,1)S(1)}, u32[]{:S(2)}, u32[]{:S(2)}) %collective-permute-start) | collective-permute-done | bytes 524320 | tf_op jit(solution)/shard_map/ppermute | solution.py:30
  15.1 5.1 %collective-permute-start.1 = (bf16[256,1024]{1,0:T(8,128)(2,1)S(1)}, bf16[256,1024]{1,0:T(8,128)(2,1)}, u32[]{:S(2)}, u32[]{:S(2)}) collective-permute-start(bf16[256,1024]{1,0:T(8,128)(2,1)S(1)} %collective-permute-done.rest_1_), channel_id=1, source_target_pairs={{0,8},{1,9},{2,10},{3,11},{4,12},{5,13},{6,14},{7,15},{8,16},{9,17... | collective-permute-start | bytes 1572872 | tf_op jit(solution)/shard_map/ppermute | solution.py:30
  21.8 1.5 collective-permute-start.13
  24.6 5.0 %collective-permute-done.1.rest_2_ = bf16[256,1024]{1,0:T(8,128)(2,1)} collective-permute-done((bf16[256,1024]{1,0:T(8,128)(2,1)S(1)}, bf16[256,1024]{1,0:T(8,128)(2,1)}, u32[]{:S(2)}, u32[]{:S(2)}) %collective-permute-start.1) | collective-permute-done | bytes 524320 | tf_op jit(solution)/shard_map/ppermute | solution.py:30
  31.6 15.9 %collective-permute-done.15.refs_7_ = bf16[256,2048]{1,0:T(8,128)(2,1)} collective-permute-done((bf16[256,2048]{1,0:T(8,128)(2,1)S(1)}, bf16[256,2048]{1,0:T(8,128)(2,1)}, u32[]{:S(2)}, u32[]{:S(2)}) %collective-permute-start.15) | collective-permute-done | bytes 1048608 | tf_op jit(solution)/shard_map/ppermute | solution.py:30
  47.5 20.1 %collective-permute-done.13.refs_6_ = bf16[256,2048]{1,0:T(8,128)(2,1)} collective-permute-done((bf16[256,2048]{1,0:T(8,128)(2,1)S(1)}, bf16[256,2048]{1,0:T(8,128)(2,1)}, u32[]{:S(2)}, u32[]{:S(2)}) %collective-permute-start.13) | collective-permute-done | bytes 1048608 | tf_op jit(solution)/shard_map/ppermute | solution.py:30
  68.1 1.6 copy-done.4
  70.7 6.2 %conv.1 = bf16[256,1024]{1,0:T(8,128)(2,1)S(1)} custom-call(s32[1]{0:T(128)} %bitcast.8.core_ref, bf16[512,256]{1,0:T(8,128)(2,1)S(1)} %copy.6.table_ref, bf16[256,512]{1,0:T(8,128)(2,1)S(1)} %fusion.27.back_ref, f32[1,1024]{1,0:T(1,128)S(1)} %bitcast.78, bf16[256,1024]{1,0:T(8,128)(2,1)S(1)} %copy-done.5, bf16[1024,1024]{1,0:T(8,128)(2,1)S(1)} %copy-done.4, ...), custom_call_target="tpu_custom_call" | custom-call | flops 4026531840 | bytes 6291456 | tf_op jit(solution)/shard_map/conv/pallas_call | solution.py:95
  77.0 2.0 %collective-permute-start.8 = (bf16[64,1024]{1,0:T(8,128)(2,1)S(1)}, bf16[64,1024]{1,0:T(8,128)(2,1)S(1)}, u32[]{:S(2)}, u32[]{:S(2)}) collective-permute-start(bf16[64,1024]{1,0:T(8,128)(2,1)S(1)} %get-tuple-element.18), channel_id=1, source_target_pairs={{0,3},{1,11},{2,19},{3,27},{4,7},{5,15},{6,23},{7,31},{8,0},{9,8},... | collective-permute-start | bytes 393224 | tf_op jit(solution)/shard_map/ppermute | solution.py:30
  79.1 6.3 %collective-permute-done.8.refs_3_ = bf16[64,1024]{1,0:T(8,128)(2,1)S(1)} collective-permute-done((bf16[64,1024]{1,0:T(8,128)(2,1)S(1)}, bf16[64,1024]{1,0:T(8,128)(2,1)S(1)}, u32[]{:S(2)}, u32[]{:S(2)}) %collective-permute-start.8) | collective-permute-done | bytes 131104 | tf_op jit(solution)/shard_map/ppermute | solution.py:30
  86.1 6.4 %collective-permute-done.7.refs_2_ = bf16[64,1024]{1,0:T(8,128)(2,1)S(1)} collective-permute-done((bf16[64,1024]{1,0:T(8,128)(2,1)S(1)}, bf16[64,1024]{1,0:T(8,128)(2,1)S(1)}, u32[]{:S(2)}, u32[]{:S(2)}) %collective-permute-start.7) | collective-permute-done | bytes 131104 | tf_op jit(solution)/shard_map/ppermute | solution.py:30
  92.5 3.2 %collective-permute-start.6 = (bf16[64,1024]{1,0:T(8,128)(2,1)S(1)}, bf16[64,1024]{1,0:T(8,128)(2,1)S(1)}, u32[]{:S(2)}, u32[]{:S(2)}) collective-permute-start(bf16[64,1024]{1,0:T(8,128)(2,1)S(1)} %get-tuple-element.20), channel_id=1, source_target_pairs={{0,1},{1,9},{2,17},{3,25},{4,5},{5,13},{6,21},{7,29},{8,2},{9,10},... | collective-permute-start | bytes 393224 | tf_op jit(solution)/shard_map/ppermute | solution.py:30
  95.7 5.7 %collective-permute-done.6.refs_1_ = bf16[64,1024]{1,0:T(8,128)(2,1)S(1)} collective-permute-done((bf16[64,1024]{1,0:T(8,128)(2,1)S(1)}, bf16[64,1024]{1,0:T(8,128)(2,1)S(1)}, u32[]{:S(2)}, u32[]{:S(2)}) %collective-permute-start.6) | collective-permute-done | bytes 131104 | tf_op jit(solution)/shard_map/ppermute | solution.py:30
  101.4 8.0 %collective-permute-start.5 = (bf16[64,1024]{1,0:T(8,128)(2,1)S(1)}, bf16[64,1024]{1,0:T(8,128)(2,1)S(1)}, u32[]{:S(2)}, u32[]{:S(2)}) collective-permute-start(bf16[64,1024]{1,0:T(8,128)(2,1)S(1)} %get-tuple-element.21), channel_id=1, source_target_pairs={{0,0},{1,8},{2,16},{3,24},{4,4},{5,12},{6,20},{7,28},{8,1},{9,9},{... | collective-permute-start | bytes 393224 | tf_op jit(solution)/shard_map/ppermute | solution.py:30
  109.8 3.0 %collective-permute-done.5.refs_0_ = bf16[64,1024]{1,0:T(8,128)(2,1)S(1)} collective-permute-done((bf16[64,1024]{1,0:T(8,128)(2,1)S(1)}, bf16[64,1024]{1,0:T(8,128)(2,1)S(1)}, u32[]{:S(2)}, u32[]{:S(2)}) %collective-permute-start.5) | collective-permute-done | bytes 131104 | tf_op jit(solution)/shard_map/ppermute | solution.py:30
  114.4 4.5 %project.3 = f32[256,2048]{1,0:T(8,128)S(1)} custom-call(s32[8]{0:T(128)S(1)} %stack.47.offsets_ref, bf16[64,1024]{1,0:T(8,128)(2,1)S(1)} %copy-done.2, bf16[64,1024]{1,0:T(8,128)(2,1)S(1)} %collective-permute-done.6.refs_1_, bf16[64,1024]{1,0:T(8,128)(2,1)S(1)} %collective-permute-done.7.refs_2_, bf16[64,1024]{1,0:T(8,128)(2,1)S(1)} %collective-permute-done.8.refs_3_, ...), custom_call_target="tpu_custom_call" | custom-call | flops 1073741824 | bytes 7340032 | tf_op jit(solution)/shard_map/project/pallas_call | solution.py:168
  119.0 8.6 %collective-permute-start.23 = (bf16[64,2048]{1,0:T(8,128)(2,1)S(1)}, bf16[64,2048]{1,0:T(8,128)(2,1)S(1)}, u32[]{:S(2)}, u32[]{:S(2)}) collective-permute-start(bf16[64,2048]{1,0:T(8,128)(2,1)S(1)} %get-tuple-element.10), channel_id=1, source_target_pairs={{0,8},{1,9},{2,10},{3,11},{4,12},{5,13},{6,14},{7,15}} | collective-permute-start | bytes 786440 | tf_op jit(solution)/shard_map/ppermute | solution.py:30
  129.2 4.6 %project.2 = f32[256,2048]{1,0:T(8,128)S(1)} custom-call(s32[8]{0:T(128)S(1)} %stack.46.offsets_ref, bf16[64,1024]{1,0:T(8,128)(2,1)S(1)} %copy-done.3, bf16[64,1024]{1,0:T(8,128)(2,1)S(1)} %collective-permute-done.6.refs_1_, bf16[64,1024]{1,0:T(8,128)(2,1)S(1)} %collective-permute-done.7.refs_2_, bf16[64,1024]{1,0:T(8,128)(2,1)S(1)} %collective-permute-done.8.refs_3_, ...), custom_call_target="tpu_custom_call" | custom-call | flops 1073741824 | bytes 7340032 | tf_op jit(solution)/shard_map/project/pallas_call | solution.py:168
  135.3 3.4 %collective-permute-start.24 = (bf16[64,2048]{1,0:T(8,128)(2,1)S(1)}, bf16[64,2048]{1,0:T(8,128)(2,1)S(1)}, u32[]{:S(2)}, u32[]{:S(2)}) collective-permute-start(bf16[64,2048]{1,0:T(8,128)(2,1)S(1)} %fusion.2), channel_id=1, source_target_pairs={{0,8},{1,9},{2,10},{3,11},{4,12},{5,13},{6,14},{7,15},{8,16},{9,17... | collective-permute-start | bytes 786440 | tf_op jit(solution)/shard_map/ppermute | solution.py:30
  140.8 4.4 %collective-permute-start.18 = (bf16[64,2048]{1,0:T(8,128)(2,1)S(1)}, bf16[64,2048]{1,0:T(8,128)(2,1)S(1)}, u32[]{:S(2)}, u32[]{:S(2)}) collective-permute-start(bf16[64,2048]{1,0:T(8,128)(2,1)S(1)} %fusion.8), channel_id=1, source_target_pairs={{0,8},{1,9},{2,10},{3,11},{4,12},{5,13},{6,14},{7,15},{8,16},{9,17... | collective-permute-start | bytes 786440 | tf_op jit(solution)/shard_map/ppermute | solution.py:30
  145.5 4.4 %collective-permute-start.25 = (bf16[64,2048]{1,0:T(8,128)(2,1)S(1)}, bf16[64,2048]{1,0:T(8,128)(2,1)S(1)}, u32[]{:S(2)}, u32[]{:S(2)}) collective-permute-start(bf16[64,2048]{1,0:T(8,128)(2,1)S(1)} %get-tuple-element.8), channel_id=1, source_target_pairs={{0,8},{1,9},{2,10},{3,11},{4,12},{5,13},{6,14},{7,15},{8,16},{9,17... | collective-permute-start | bytes 786440 | tf_op jit(solution)/shard_map/ppermute | solution.py:30
  152.8 12.3 %collective-permute-start.19 = (bf16[64,2048]{1,0:T(8,128)(2,1)S(1)}, bf16[64,2048]{1,0:T(8,128)(2,1)}, u32[]{:S(2)}, u32[]{:S(2)}) collective-permute-start(bf16[64,2048]{1,0:T(8,128)(2,1)S(1)} %get-tuple-element.12), channel_id=1, source_target_pairs={{0,8},{1,9},{2,10},{3,11},{4,12},{5,13},{6,14},{7,15},{8,16},{9,17... | collective-permute-start | bytes 786440 | tf_op jit(solution)/shard_map/ppermute | solution.py:30
  168.2 5.3 %collective-permute-done.22 = bf16[64,2048]{1,0:T(8,128)(2,1)} collective-permute-done((bf16[64,2048]{1,0:T(8,128)(2,1)S(1)}, bf16[64,2048]{1,0:T(8,128)(2,1)}, u32[]{:S(2)}, u32[]{:S(2)}) %collective-permute-start.22) | collective-permute-done | bytes 262176 | tf_op jit(solution)/shard_map/ppermute | solution.py:30
  (79 shorter events, 24.2 us)
Async XLA Ops:
  0.0 15.1 %collective-permute-start = (bf16[256,1024]{1,0:T(8,128)(2,1)}, bf16[256,1024]{1,0:T(8,128)(2,1)S(1)}, u32[]{:S(2)}, u32[]{:S(2)}) collective-permute-start(bf16[256,1024]{1,0:T(8,128)(2,1)} %rest_0_.1), channel_id=1, source_target_pairs={{0,8},{1,9},{2,10},{3,11},{4,12},{5,13},{6,14},{7,15},{8,16},{9,17... | collective-permute-start | bytes 1572872 | tf_op jit(solution)/shard_map/ppermute | solution.py:30
  5.0 15.2 %collective-permute-start.9 = (bf16[128,2048]{1,0:T(8,128)(2,1)S(1)}, bf16[128,2048]{1,0:T(8,128)(2,1)S(1)}, u32[]{:S(2)}, u32[]{:S(2)}) collective-permute-start(bf16[128,2048]{1,0:T(8,128)(2,1)S(1)} %get-tuple-element.17), channel_id=1, source_target_pairs={{0,4},{1,5},{2,6},{3,7},{4,0},{5,1},{6,2},{7,3},{8,12},{9,13},{10,... | collective-permute-start | bytes 1572872 | tf_op jit(solution)/shard_map/ppermute | solution.py:30
  5.1 18.8 %collective-permute-start.2 = (bf16[256,1024]{1,0:T(8,128)(2,1)S(1)}, bf16[256,1024]{1,0:T(8,128)(2,1)S(1)}, u32[]{:S(2)}, u32[]{:S(2)}) collective-permute-start(bf16[256,1024]{1,0:T(8,128)(2,1)S(1)} %copy-done.6), channel_id=1, source_target_pairs={{0,4},{1,5},{2,6},{3,7},{4,0},{5,1},{6,2},{7,3},{8,12},{9,13},{10,... | collective-permute-start | bytes 1572872 | tf_op jit(solution)/shard_map/ppermute | solution.py:30
  15.1 14.6 %collective-permute-start.1 = (bf16[256,1024]{1,0:T(8,128)(2,1)S(1)}, bf16[256,1024]{1,0:T(8,128)(2,1)}, u32[]{:S(2)}, u32[]{:S(2)}) collective-permute-start(bf16[256,1024]{1,0:T(8,128)(2,1)S(1)} %collective-permute-done.rest_1_), channel_id=1, source_target_pairs={{0,8},{1,9},{2,10},{3,11},{4,12},{5,13},{6,14},{7,15},{8,16},{9,17... | collective-permute-start | bytes 1572872 | tf_op jit(solution)/shard_map/ppermute | solution.py:30
  20.3 27.2 %collective-permute-start.15 = (bf16[256,2048]{1,0:T(8,128)(2,1)S(1)}, bf16[256,2048]{1,0:T(8,128)(2,1)}, u32[]{:S(2)}, u32[]{:S(2)}) collective-permute-start(bf16[256,2048]{1,0:T(8,128)(2,1)S(1)} %pad_maximum_fusion.refs_4_), channel_id=1, source_target_pairs={{0,3},{1,2},{2,1},{3,0},{4,7},{5,6},{6,5},{7,4},{8,11},{9,10},{10,... | collective-permute-start | bytes 3145736 | tf_op jit(solution)/shard_map/ppermute | solution.py:30
  21.8 45.8 %collective-permute-start.13 = (bf16[256,2048]{1,0:T(8,128)(2,1)S(1)}, bf16[256,2048]{1,0:T(8,128)(2,1)}, u32[]{:S(2)}, u32[]{:S(2)}) collective-permute-start(bf16[256,2048]{1,0:T(8,128)(2,1)S(1)} %pad_maximum_fusion.refs_4_), channel_id=1, source_target_pairs={{0,2},{1,3},{2,0},{3,1},{4,6},{5,7},{6,4},{7,5},{8,10},{9,11},{10,... | collective-permute-start | bytes 3145736 | tf_op jit(solution)/shard_map/ppermute | solution.py:30
  23.3 44.3 %collective-permute-start.11 = (bf16[256,2048]{1,0:T(8,128)(2,1)S(1)}, bf16[256,2048]{1,0:T(8,128)(2,1)}, u32[]{:S(2)}, u32[]{:S(2)}) collective-permute-start(bf16[256,2048]{1,0:T(8,128)(2,1)S(1)} %pad_maximum_fusion.refs_4_), channel_id=1, source_target_pairs={{0,1},{1,0},{2,3},{3,2},{4,5},{5,4},{6,7},{7,6},{8,9},{9,8},{10,11... | collective-permute-start | bytes 3145736 | tf_op jit(solution)/shard_map/ppermute | solution.py:30
  29.7 38.4 %collective-permute-start.4 = (bf16[256,1024]{1,0:T(8,128)(2,1)}, bf16[256,1024]{1,0:T(8,128)(2,1)}, u32[]{:S(2)}, u32[]{:S(2)}) collective-permute-start(bf16[256,1024]{1,0:T(8,128)(2,1)} %collective-permute-done.1.rest_2_), channel_id=1, source_target_pairs={{0,4},{1,5},{2,6},{3,7},{4,0},{5,1},{6,2},{7,3},{8,12},{9,13},{10,... | collective-permute-start | bytes 1572872 | tf_op jit(solution)/shard_map/ppermute | solution.py:30
  31.1 96.4 %collective-permute-start.10 = (bf16[256,2048]{1,0:T(8,128)(2,1)S(1)}, bf16[256,2048]{1,0:T(8,128)(2,1)}, u32[]{:S(2)}, u32[]{:S(2)}) collective-permute-start(bf16[256,2048]{1,0:T(8,128)(2,1)S(1)} %pad_maximum_fusion.refs_4_), channel_id=1, source_target_pairs={{0,4},{1,5},{2,6},{3,7},{4,0},{5,1},{6,2},{7,3},{8,12},{9,13},{10,... | collective-permute-start | bytes 3145736 | tf_op jit(solution)/shard_map/ppermute | solution.py:30
  47.4 80.8 %collective-permute-start.16 = (bf16[256,2048]{1,0:T(8,128)(2,1)}, bf16[256,2048]{1,0:T(8,128)(2,1)}, u32[]{:S(2)}, u32[]{:S(2)}) collective-permute-start(bf16[256,2048]{1,0:T(8,128)(2,1)} %collective-permute-done.15.refs_7_), channel_id=1, source_target_pairs={{0,4},{1,5},{2,6},{3,7},{4,0},{5,1},{6,2},{7,3},{8,12},{9,13},{10,... | collective-permute-start | bytes 3145736 | tf_op jit(solution)/shard_map/ppermute | solution.py:30
  67.6 60.7 %collective-permute-start.14 = (bf16[256,2048]{1,0:T(8,128)(2,1)}, bf16[256,2048]{1,0:T(8,128)(2,1)}, u32[]{:S(2)}, u32[]{:S(2)}) collective-permute-start(bf16[256,2048]{1,0:T(8,128)(2,1)} %collective-permute-done.13.refs_6_), channel_id=1, source_target_pairs={{0,4},{1,5},{2,6},{3,7},{4,0},{5,1},{6,2},{7,3},{8,12},{9,13},{10,... | collective-permute-start | bytes 3145736 | tf_op jit(solution)/shard_map/ppermute | solution.py:30
  67.6 60.7 %collective-permute-start.12 = (bf16[256,2048]{1,0:T(8,128)(2,1)}, bf16[256,2048]{1,0:T(8,128)(2,1)}, u32[]{:S(2)}, u32[]{:S(2)}) collective-permute-start(bf16[256,2048]{1,0:T(8,128)(2,1)} %collective-permute-done.11.refs_5_), channel_id=1, source_target_pairs={{0,4},{1,5},{2,6},{3,7},{4,0},{5,1},{6,2},{7,3},{8,12},{9,13},{10,... | collective-permute-start | bytes 3145736 | tf_op jit(solution)/shard_map/ppermute | solution.py:30
  92.5 8.9 %collective-permute-start.6 = (bf16[64,1024]{1,0:T(8,128)(2,1)S(1)}, bf16[64,1024]{1,0:T(8,128)(2,1)S(1)}, u32[]{:S(2)}, u32[]{:S(2)}) collective-permute-start(bf16[64,1024]{1,0:T(8,128)(2,1)S(1)} %get-tuple-element.20), channel_id=1, source_target_pairs={{0,1},{1,9},{2,17},{3,25},{4,5},{5,13},{6,21},{7,29},{8,2},{9,10},... | collective-permute-start | bytes 393224 | tf_op jit(solution)/shard_map/ppermute | solution.py:30
  101.4 11.4 %collective-permute-start.5 = (bf16[64,1024]{1,0:T(8,128)(2,1)S(1)}, bf16[64,1024]{1,0:T(8,128)(2,1)S(1)}, u32[]{:S(2)}, u32[]{:S(2)}) collective-permute-start(bf16[64,1024]{1,0:T(8,128)(2,1)S(1)} %get-tuple-element.21), channel_id=1, source_target_pairs={{0,0},{1,8},{2,16},{3,24},{4,4},{5,12},{6,20},{7,28},{8,1},{9,9},{... | collective-permute-start | bytes 393224 | tf_op jit(solution)/shard_map/ppermute | solution.py:30
  119.0 16.3 %collective-permute-start.23 = (bf16[64,2048]{1,0:T(8,128)(2,1)S(1)}, bf16[64,2048]{1,0:T(8,128)(2,1)S(1)}, u32[]{:S(2)}, u32[]{:S(2)}) collective-permute-start(bf16[64,2048]{1,0:T(8,128)(2,1)S(1)} %get-tuple-element.10), channel_id=1, source_target_pairs={{0,8},{1,9},{2,10},{3,11},{4,12},{5,13},{6,14},{7,15}} | collective-permute-start | bytes 786440 | tf_op jit(solution)/shard_map/ppermute | solution.py:30
  127.6 17.6 %collective-permute-start.26 = (bf16[64,2048]{1,0:T(8,128)(2,1)S(1)}, bf16[64,2048]{1,0:T(8,128)(2,1)S(1)}, u32[]{:S(2)}, u32[]{:S(2)}) collective-permute-start(bf16[64,2048]{1,0:T(8,128)(2,1)S(1)} %get-tuple-element.11), channel_id=1, source_target_pairs={{24,16},{25,17},{26,18},{27,19},{28,20},{29,21},{30,22},{31,23}} | collective-permute-start | bytes 786440 | tf_op jit(solution)/shard_map/ppermute | solution.py:30
  135.3 10.1 %collective-permute-start.24 = (bf16[64,2048]{1,0:T(8,128)(2,1)S(1)}, bf16[64,2048]{1,0:T(8,128)(2,1)S(1)}, u32[]{:S(2)}, u32[]{:S(2)}) collective-permute-start(bf16[64,2048]{1,0:T(8,128)(2,1)S(1)} %fusion.2), channel_id=1, source_target_pairs={{0,8},{1,9},{2,10},{3,11},{4,12},{5,13},{6,14},{7,15},{8,16},{9,17... | collective-permute-start | bytes 786440 | tf_op jit(solution)/shard_map/ppermute | solution.py:30
  138.8 11.8 %collective-permute-start.20 = (bf16[64,2048]{1,0:T(8,128)(2,1)S(1)}, bf16[64,2048]{1,0:T(8,128)(2,1)S(1)}, u32[]{:S(2)}, u32[]{:S(2)}) collective-permute-start(bf16[64,2048]{1,0:T(8,128)(2,1)S(1)} %get-tuple-element.15), channel_id=1, source_target_pairs={{24,16},{25,17},{26,18},{27,19},{28,20},{29,21},{30,22},{31,23}} | collective-permute-start | bytes 786440 | tf_op jit(solution)/shard_map/ppermute | solution.py:30
  140.8 9.8 %collective-permute-start.18 = (bf16[64,2048]{1,0:T(8,128)(2,1)S(1)}, bf16[64,2048]{1,0:T(8,128)(2,1)S(1)}, u32[]{:S(2)}, u32[]{:S(2)}) collective-permute-start(bf16[64,2048]{1,0:T(8,128)(2,1)S(1)} %fusion.8), channel_id=1, source_target_pairs={{0,8},{1,9},{2,10},{3,11},{4,12},{5,13},{6,14},{7,15},{8,16},{9,17... | collective-permute-start | bytes 786440 | tf_op jit(solution)/shard_map/ppermute | solution.py:30
  145.5 20.9 %collective-permute-start.25 = (bf16[64,2048]{1,0:T(8,128)(2,1)S(1)}, bf16[64,2048]{1,0:T(8,128)(2,1)S(1)}, u32[]{:S(2)}, u32[]{:S(2)}) collective-permute-start(bf16[64,2048]{1,0:T(8,128)(2,1)S(1)} %get-tuple-element.8), channel_id=1, source_target_pairs={{0,8},{1,9},{2,10},{3,11},{4,12},{5,13},{6,14},{7,15},{8,16},{9,17... | collective-permute-start | bytes 786440 | tf_op jit(solution)/shard_map/ppermute | solution.py:30
  150.7 14.3 %collective-permute-start.21 = (bf16[64,2048]{1,0:T(8,128)(2,1)S(1)}, bf16[64,2048]{1,0:T(8,128)(2,1)S(1)}, u32[]{:S(2)}, u32[]{:S(2)}) collective-permute-start(bf16[64,2048]{1,0:T(8,128)(2,1)S(1)} %get-tuple-element.13), channel_id=1, source_target_pairs={{16,8},{17,9},{18,10},{19,11},{20,12},{21,13},{22,14},{23,15},{24,... | collective-permute-start | bytes 786440 | tf_op jit(solution)/shard_map/ppermute | solution.py:30
  151.5 15.4 %collective-permute-start.28 = (bf16[64,2048]{1,0:T(8,128)(2,1)S(1)}, bf16[64,2048]{1,0:T(8,128)(2,1)}, u32[]{:S(2)}, u32[]{:S(2)}) collective-permute-start(bf16[64,2048]{1,0:T(8,128)(2,1)S(1)} %fusion.1), channel_id=1, source_target_pairs={{8,0},{9,1},{10,2},{11,3},{12,4},{13,5},{14,6},{15,7},{16,8},{17,9... | collective-permute-start | bytes 786440 | tf_op jit(solution)/shard_map/ppermute | solution.py:30
  152.8 15.4 %collective-permute-start.19 = (bf16[64,2048]{1,0:T(8,128)(2,1)S(1)}, bf16[64,2048]{1,0:T(8,128)(2,1)}, u32[]{:S(2)}, u32[]{:S(2)}) collective-permute-start(bf16[64,2048]{1,0:T(8,128)(2,1)S(1)} %get-tuple-element.12), channel_id=1, source_target_pairs={{0,8},{1,9},{2,10},{3,11},{4,12},{5,13},{6,14},{7,15},{8,16},{9,17... | collective-permute-start | bytes 786440 | tf_op jit(solution)/shard_map/ppermute | solution.py:30
  165.1 8.4 %collective-permute-start.22 = (bf16[64,2048]{1,0:T(8,128)(2,1)S(1)}, bf16[64,2048]{1,0:T(8,128)(2,1)}, u32[]{:S(2)}, u32[]{:S(2)}) collective-permute-start(bf16[64,2048]{1,0:T(8,128)(2,1)S(1)} %fusion.7), channel_id=1, source_target_pairs={{8,0},{9,1},{10,2},{11,3},{12,4},{13,5},{14,6},{15,7},{16,8},{17,9... | collective-permute-start | bytes 786440 | tf_op jit(solution)/shard_map/ppermute | solution.py:30
  (15 other events, 198.7 us)
where the time goes:
time: 177 us; the launch traced here: 176 us
  waiting for transfers between devices  80.5 us (45%)
  starting transfers between devices  67.5 us (38%)
  Pallas kernels  15.4 us (9%)
  local copies, waits for them, and re-layouts  7.68 us (4%)
  other arithmetic  4.01 us (2%)
    ppermute x29, waiting for transfers between devices, permute(): return lax.ppermute(value, AXES, route)  80.5 us
    ppermute x29, starting transfers between devices, permute(): return lax.ppermute(value, AXES, route)  67.5 us
    pallas_call x2, Pallas kernels, project(): pl.pallas_call(functools.partial(project_kernel, count), grid_spec=pltpu....  9.13 us
    pallas_call x1, Pallas kernels, convolve(): pl.pallas_call(functools.partial(conv_kernel, lags), grid_spec=pltpu.Pref...  6.25 us
    unnamed x20, local copies, waits for them, and re-layouts  5.9 us
  transfers between devices with their start and end apart: 29, of which 13 were waited for; matrix products, arithmetic and copies ran while one was open for 2% of the time, Pallas kernels for 9%

commit v1 on v0

v1 whole, which is shorter than its diff:
```python
import functools
import math

import jax
import jax.numpy as jnp
import numpy as np
from jax import lax
from jax.experimental import pallas as pl
from jax.experimental.pallas import tpu as pltpu
from jax.sharding import PartitionSpec as P

AXES = ("seq", "chan")
F32 = jnp.float32
BF16 = jnp.bfloat16


def sizes():
    return lax.axis_size("seq") // 2, lax.axis_size("chan")


def place(pairs, chans, pair, core, chan):
    return (pair * 2 + core) * chans + chan


def permute(value, move):
    pairs, chans = sizes()
    route = []
    for pair in range(pairs):
        for core in range(2):
            for chan in range(chans):
                target = move(pair, core, chan)
                if target is not None and 0 <= target[0] < pairs:
                    route.append(
                        (place(pairs, chans, pair, core, chan), place(pairs, chans, *target))
                    )
    return lax.ppermute(value, AXES, route)


def table(block):
    order = np.concatenate([np.arange(0, block, 2), np.arange(1, block, 2)])
    phase = (2 * order[:, None] + 1) * np.arange(block)[None, :] % (4 * block)
    angle = phase * (math.pi / (2 * block))
    return np.concatenate([np.cos(angle), np.sin(angle)], axis=0)


def conv_kernel(lags, core_ref, table_ref, back_ref, skip_ref, gates_ref, filters_ref, *rest):
    *block_refs, out_ref = rest
    block = gates_ref.shape[0]
    half = block // 2
    odd = core_ref[0] == 1
    reach = lags // 2

    def transform(operand):
        return jnp.dot(table_ref[...], operand, preferred_element_type=F32)

    direct = block_refs[: reach + 1]
    crossed = block_refs[reach + 1 :]
    cos_parts, sin_parts = [], []
    for lag in range(lags + 1):
        if lag % 2 == 0:
            operand = direct[lag // 2][...]
        else:
            operand = jnp.where(odd, crossed[lag // 2][...], crossed[lag // 2 + 1][...])
        both = transform(operand)
        cos_parts.append(both[:block])
        sin_parts.append(both[block:])
    real = imag = 0.0
    for lag in range(lags):
        both = transform(filters_ref[lag * block : (lag + 1) * block, :])
        tap_cos, tap_sin = both[:block], both[block:]
        near_cos, near_sin = cos_parts[lag], sin_parts[lag]
        far_cos, far_sin = cos_parts[lag + 1], sin_parts[lag + 1]
        window_cos = jnp.concatenate(
            [near_cos[:half] + far_sin[:half], near_cos[half:] - far_sin[half:]], axis=0
        )
        window_sin = jnp.concatenate(
            [near_sin[:half] - far_cos[:half], near_sin[half:] + far_cos[half:]], axis=0
        )
        real = real + tap_cos * window_cos - tap_sin * window_sin
        imag = imag + tap_cos * window_sin + tap_sin * window_cos
    spectrum = jnp.concatenate([real, imag], axis=0).astype(BF16)
    filtered = jnp.dot(back_ref[...], spectrum, preferred_element_type=F32) * (1.0 / block)
    filtered = filtered + skip_ref[...] * direct[0][...].astype(F32)
    out_ref[...] = (gates_ref[...].astype(F32) * filtered).astype(BF16)


def convolve(core, gates, filters, skip, direct, crossed):
    block, width = gates.shape
    taps = filters.shape[0]
    lags = taps // block
    forth = table(block)
    tile = min(width, 256)

    def column(rows):
        return pl.BlockSpec((rows, tile), lambda i, *_: (0, i))

    def whole(rows, cols):
        return pl.BlockSpec((rows, cols), lambda i, *_: (0, 0))

    blocks = [*direct, *crossed]
    return pl.pallas_call(
        functools.partial(conv_kernel, lags),
        grid_spec=pltpu.PrefetchScalarGridSpec(
            num_scalar_prefetch=1,
            grid=(width // tile,),
            in_specs=[
                whole(2 * block, block),
                whole(block, 2 * block),
                column(1),
                column(block),
                column(taps),
                *[column(block) for _ in blocks],
            ],
            out_specs=column(block),
        ),
        out_shape=jax.ShapeDtypeStruct((block, width), BF16),
        cost_estimate=pl.CostEstimate(
            flops=2 * (3 * lags + 3) * 2 * block * block * width,
            bytes_accessed=2 * width * (taps + (len(blocks) + 2) * block),
            transcendentals=0,
        ),
        name="conv",
    )(
        core.reshape(1),
        jnp.asarray(forth, BF16),
        jnp.asarray(forth.T, BF16),
        skip.reshape(1, width),
        gates,
        filters,
        *blocks,
    )


def join_kernel(count, *refs):
    out_ref = refs[-1]
    start = 0
    for ref in refs[:count]:
        out_ref[start : start + ref.shape[0], :] = ref[...]
        start += ref.shape[0]


def join(parts, cols, deps=()):
    rows = sum(array.shape[0] for array, _ in parts)
    return pl.pallas_call(
        functools.partial(join_kernel, len(parts)),
        grid=(1,),
        in_specs=[
            *[
                pl.BlockSpec((array.shape[0], cols), lambda i, index=index: (0, index))
                for array, index in parts
            ],
            *[pl.BlockSpec(memory_space=pl.ANY) for _ in deps],
        ],
        out_specs=pl.BlockSpec((rows, cols), lambda i: (0, 0)),
        out_shape=jax.ShapeDtypeStruct((rows, cols), BF16),
        compiler_params=pltpu.CompilerParams(vmem_limit_bytes=12 * 2**20),
        name="join",
    )(*[array for array, _ in parts], *deps)


def part_kernel(many, index_ref, from_ref, *refs):
    for step, ref in enumerate(refs[-many:]):
        ref[...] = from_ref[index_ref[0] ^ step]


def part(index, array, deps):
    many, rows, depth = array.shape
    return pl.pallas_call(
        functools.partial(part_kernel, many),
        grid_spec=pltpu.PrefetchScalarGridSpec(
            num_scalar_prefetch=1,
            grid=(1,),
            in_specs=[pl.BlockSpec(array.shape, lambda i, *_: (0, 0, 0))]
            + [pl.BlockSpec(memory_space=pl.ANY)] * len(deps),
            out_specs=[pl.BlockSpec((rows, depth), lambda i, *_: (0, 0))] * many,
        ),
        out_shape=[jax.ShapeDtypeStruct((rows, depth), BF16)] * many,
        compiler_params=pltpu.CompilerParams(vmem_limit_bytes=12 * 2**20),
        name="part",
    )(index.reshape(1), array, *deps)


def fence_kernel(*refs):
    del refs


def fence(arrays, deps):
    anywhere = pl.BlockSpec(memory_space=pl.ANY)
    return pl.pallas_call(
        fence_kernel,
        in_specs=[anywhere] * (len(arrays) + len(deps)),
        out_specs=[anywhere] * len(arrays),
        out_shape=[jax.ShapeDtypeStruct(array.shape, array.dtype) for array in arrays],
        input_output_aliases={index: index for index in range(len(arrays))},
        name="fence",
    )(*arrays, *deps)


def arrange_kernel(slots, order_ref, *refs):
    out_ref = refs[-1]
    rows, depth = refs[0].shape
    width = depth // slots
    for index, ref in enumerate(refs[:-1]):
        here = slice(index * rows, (index + 1) * rows)
        if width % 128:
            out_ref[here, :] = ref[...]
            continue
        for slot in range(slots):
            start = pl.multiple_of(order_ref[slot] * width, width)
            out_ref[here, slot * width : (slot + 1) * width] = ref[:, pl.ds(start, width)]


def arrange(order, acts):
    slots = order.shape[0]
    rows, depth = acts[0].shape
    width = depth // slots
    if width % 128:
        acts = [
            jnp.concatenate(
                [
                    lax.dynamic_slice_in_dim(act, order[slot] * width, width, axis=1)
                    for slot in range(slots)
                ],
                axis=1,
            )
            for act in acts
        ]
    return pl.pallas_call(
        functools.partial(arrange_kernel, slots),
        grid_spec=pltpu.PrefetchScalarGridSpec(
            num_scalar_prefetch=1,
            grid=(1,),
            in_specs=[pl.BlockSpec((rows, depth), lambda i, *_: (0, 0)) for _ in acts],
            out_specs=pl.BlockSpec((rows * len(acts), depth), lambda i, *_: (0, 0)),
        ),
        out_shape=jax.ShapeDtypeStruct((rows * len(acts), depth), BF16),
        compiler_params=pltpu.CompilerParams(vmem_limit_bytes=12 * 2**20),
        name="arrange",
    )(order, *acts)


def project_kernel(spots, width, acts_ref, *refs):
    piece_refs = refs[:-2]
    send_ref, keep_ref = refs[-2:]
    rows = acts_ref.shape[0] // 2
    weight = jnp.concatenate(
        [piece_refs[piece][spot * width : (spot + 1) * width, :] for piece, spot in spots], axis=0
    )
    total = jnp.dot(acts_ref[...], weight, preferred_element_type=F32)
    send_ref[...] = total[:rows].astype(BF16)
    keep_ref[...] = total[rows:]


def project(acts, pieces, spots, width, cols):
    count, depth = acts.shape
    tile = min(cols, 512)
    return pl.pallas_call(
        functools.partial(project_kernel, spots, width),
        grid=(cols // tile,),
        in_specs=[
            pl.BlockSpec((count, depth), lambda i: (0, 0)),
            *[
                pl.BlockSpec(
                    (piece.shape[0], tile), lambda i, first=first * cols // tile: (0, first + i)
                )
                for piece, first in pieces
            ],
        ],
        out_specs=[pl.BlockSpec((count // 2, tile), lambda i: (0, i))] * 2,
        out_shape=[
            jax.ShapeDtypeStruct((count // 2, cols), BF16),
            jax.ShapeDtypeStruct((count // 2, cols), F32),
        ],
        compiler_params=pltpu.CompilerParams(vmem_limit_bytes=16 * 2**20),
        cost_estimate=pl.CostEstimate(
            flops=2 * count * depth * cols,
            bytes_accessed=2 * depth * cols + 6 * count * cols,
            transcendentals=0,
        ),
        name="project",
    )(acts, *[piece for piece, _ in pieces])


def body(values, gates, filters, skip, out_weight):
    pairs, chans = sizes()
    seq, chan = lax.axis_index("seq"), lax.axis_index("chan")
    pair, core = seq // 2, seq % 2
    block = values.shape[0]
    lags = filters.shape[0] // block
    own_rows, model = out_weight.shape
    half = model // 2
    rows = block // chans

    def swap(array):
        return permute(array, lambda p, k, c: (p, 1 - k, c))

    direct = [values]
    for _ in range(lags // 2):
        direct.append(permute(direct[-1], lambda p, k, c: (p + 1, k, c)))
    crossed = [
        permute(
            held,
            lambda p, k, c, first=index == 0, last=index == lags // 2: None
            if (first and k == 1) or (last and k == 0)
            else (p, 1 - k, c),
        )
        for index, held in enumerate(direct)
    ]

    bits = [1 << index for index in range(chans.bit_length() - 1)]
    parts, spots = [], []
    for which, order in enumerate((bits, bits[::-1])):
        held = join([(out_weight, which)], half, [crossed[0]])
        found = [0]
        for step, bit in enumerate(order):
            if step:
                held = join([(piece, 0) for piece in pieces], half)
            pieces = [held, permute(held, lambda p, k, c, bit=bit: (p, k, c ^ bit))]
            found = found + [mask ^ bit for mask in found]
        parts.append(pieces)
        each = len(found) // 2
        spots.append(
            [
                (2 * other + found.index(mask) // each, found.index(mask) % each)
                for other in range(2)
                for mask in range(chans)
            ]
        )

    gated = convolve(core, gates, filters, skip, direct, crossed)

    spread = lax.all_to_all(
        gated.reshape(chans, rows, gated.shape[1]), "chan", split_axis=0, concat_axis=0
    )
    flat = fence([piece for pieces in parts for piece in pieces], [gated])
    parts = [flat[:2], flat[2:]]
    swaps = [[swap(piece) for piece in pieces] for pieces in parts]
    parts = [[*pieces, *others] for pieces, others in zip(parts, swaps, strict=True)]
    acts = list(part(pair, spread, [other for others in swaps for other in others]))
    for step in range(1, pairs):
        acts[step] = permute(acts[step], lambda p, k, c, step=step: (p ^ step, k, c))

    count = pairs.bit_length() - 1
    steps = [1 << index for index in range(count)]
    ranks = sorted(range(pairs), key=lambda e: [not e & step for step in steps])
    order = jnp.stack(
        [which * chans + (chan ^ mask) for which in (core, 1 - core) for mask in range(chans)]
    ).astype(jnp.int32)
    acts = arrange(order, [acts[rank] for rank in ranks])

    chunks = 4
    cols = model // chunks
    outs = []
    for chunk in range(chunks):
        which = chunk // 2
        send, keep = project(
            acts, [(piece, chunk % 2) for piece in parts[which]], spots[which], own_rows, cols
        )
        for index, step in enumerate(steps):
            got = permute(send, lambda p, k, c, step=step: (p ^ step, k, c)).astype(F32)
            many = got.shape[0] // 2
            if index + 1 < count:
                send = (keep[:many] + got[:many]).astype(BF16)
                keep = keep[many:] + got[many:]
            else:
                keep = keep + got
        outs.append(keep.astype(BF16))
    return jnp.concatenate(outs, axis=1)


def solution(mesh):
    in_specs = (
        P("seq", "chan"),
        P("seq", "chan"),
        P(None, "chan"),
        P("chan"),
        P(("seq", "chan"), None),
    )
    out_specs = P(("seq", "chan"), None)
    return jax.shard_map(body, mesh=mesh, in_specs=in_specs, out_specs=out_specs, check_vma=False)
```

time: 177 us -> 126 us (0.71)
  the two profiles are of different devices: /device:TPU:4 before, /device:TPU:0 now
where the time goes in v1:
time: 126 us
  waiting for transfers between devices  62.6 us (50%)
  starting transfers between devices  36.4 us (29%)
  Pallas kernels  19 us (15%)
  local copies, waits for them, and re-layouts  5.97 us (5%)
  other arithmetic  1.35 us (1%)
    ppermute x24, waiting for transfers between devices, permute(): return lax.ppermute(value, AXES, route)  54.1 us
    ppermute x24, starting transfers between devices, permute(): return lax.ppermute(value, AXES, route)  32.2 us
    all_to_all x1, waiting for transfers between devices, body(): lax.all_to_all(gated.reshape(chans, rows, gated.shape[1]), 'chan', split_...  8.51 us
    pallas_call x4, Pallas kernels, project(): pl.pallas_call(functools.partial(project_kernel, spots, width), grid=(col...  7.8 us
    pallas_call x1, Pallas kernels, convolve(): pl.pallas_call(functools.partial(conv_kernel, lags), grid_spec=pltpu.Pref...  7.51 us
    unnamed x22, local copies, waits for them, and re-layouts  5.89 us
    all_to_all x1, starting transfers between devices, body(): lax.all_to_all(gated.reshape(chans, rows, gated.shape[1]), 'chan', split_...  4.13 us
  transfers between devices with their start and end apart: 25, of which 15 were waited for; matrix products, arithmetic and copies ran while one was open for 0% of the time, Pallas kernels for 11%

profile of v1, /device:TPU:0, one launch (start us, length us, event | category | flops | bytes accessed | tf_op | source)
XLA Modules:
  0.0 125.6 jit_solution(15974097047573848896)
XLA Ops:
  0.0 2.4 %collective-permute-start.2 = (bf16[256,1024]{1,0:T(8,128)(2,1)}, bf16[256,1024]{1,0:T(8,128)(2,1)S(1)}, u32[]{:S(2)}, u32[]{:S(2)}) collective-permute-start(bf16[256,1024]{1,0:T(8,128)(2,1)} %rest_0_.1), channel_id=1, source_target_pairs={{0,4},{1,5},{2,6},{3,7},{8,12},{9,13},{10,14},{11,15},{16,20},{17,... | collective-permute-start | bytes 1572872 | tf_op jit(solution)/shard_map/ppermute | solution.py:36
  2.4 5.1 %collective-permute-start = (bf16[256,1024]{1,0:T(8,128)(2,1)}, bf16[256,1024]{1,0:T(8,128)(2,1)}, u32[]{:S(2)}, u32[]{:S(2)}) collective-permute-start(bf16[256,1024]{1,0:T(8,128)(2,1)} %rest_0_.1), channel_id=1, source_target_pairs={{0,8},{1,9},{2,10},{3,11},{4,12},{5,13},{6,14},{7,15},{8,16},{9,17... | collective-permute-start | bytes 1572872 | tf_op jit(solution)/shard_map/ppermute | solution.py:36
  12.0 5.7 %collective-permute-done.rest_1_ = bf16[256,1024]{1,0:T(8,128)(2,1)} collective-permute-done((bf16[256,1024]{1,0:T(8,128)(2,1)}, bf16[256,1024]{1,0:T(8,128)(2,1)}, u32[]{:S(2)}, u32[]{:S(2)}) %collective-permute-start) | collective-permute-done | bytes 524320 | tf_op jit(solution)/shard_map/ppermute | solution.py:36
  17.7 5.2 %collective-permute-start.1 = (bf16[256,1024]{1,0:T(8,128)(2,1)}, bf16[256,1024]{1,0:T(8,128)(2,1)}, u32[]{:S(2)}, u32[]{:S(2)}) collective-permute-start(bf16[256,1024]{1,0:T(8,128)(2,1)} %collective-permute-done.rest_1_), channel_id=1, source_target_pairs={{0,8},{1,9},{2,10},{3,11},{4,12},{5,13},{6,14},{7,15},{8,16},{9,17... | collective-permute-start | bytes 1572872 | tf_op jit(solution)/shard_map/ppermute | solution.py:36
  26.2 6.0 %collective-permute-done.1.rest_2_ = bf16[256,1024]{1,0:T(8,128)(2,1)} collective-permute-done((bf16[256,1024]{1,0:T(8,128)(2,1)}, bf16[256,1024]{1,0:T(8,128)(2,1)}, u32[]{:S(2)}, u32[]{:S(2)}) %collective-permute-start.1) | collective-permute-done | bytes 524320 | tf_op jit(solution)/shard_map/ppermute | solution.py:36
  33.5 2.8 %collective-permute-done.4.rest_5_ = bf16[256,1024]{1,0:T(8,128)(2,1)} collective-permute-done((bf16[256,1024]{1,0:T(8,128)(2,1)}, bf16[256,1024]{1,0:T(8,128)(2,1)}, u32[]{:S(2)}, u32[]{:S(2)}) %collective-permute-start.4) | collective-permute-done | bytes 524320 | tf_op jit(solution)/shard_map/ppermute | solution.py:36
  36.3 7.5 %conv.1.refs_4_ = bf16[256,1024]{1,0:T(8,128)(2,1)} custom-call(s32[1]{0:T(128)} %bitcast.9.core_ref, bf16[512,256]{1,0:T(8,128)(2,1)} %constant.42.clone.table_ref, bf16[256,512]{1,0:T(8,128)(2,1)} %constant.43.clone.back_ref, f32[1,1024]{1,0:T(1,128)} %bitcast.13, bf16[256,1024]{1,0:T(8,128)(2,1)} %gates_ref.1, bf16[1024,1024]{1,0:T(8,128)(2,1)} %filters_ref.1, ...), custom_call_target="tpu_custom_call" | custom-call | flops 4026531840 | bytes 6291456 | tf_op jit(solution)/shard_map/conv/pallas_call | solution.py:101
  43.8 2.4 %collective-permute-done.6.refs_1_ = bf16[256,2048]{1,0:T(8,128)(2,1)S(1)} collective-permute-done((bf16[256,2048]{1,0:T(8,128)(2,1)S(1)}, bf16[256,2048]{1,0:T(8,128)(2,1)S(1)}, u32[]{:S(2)}, u32[]{:S(2)}) %collective-permute-start.6) | collective-permute-done | bytes 1048608 | tf_op jit(solution)/shard_map/ppermute | solution.py:36
  48.8 4.1 %all-to-all-start = ((bf16[4,64,1024]{2,1,0:T(8,128)(2,1)}), bf16[4,64,1024]{2,1,0:T(8,128)(2,1)}, u32[]{:S(2)}, u32[]{:S(2)}) async-start(bf16[4,64,1024]{2,1,0:T(8,128)(2,1)} %bitcast.12), calls=%async_computation | async-start | bytes 1048576 | tf_op jit(solution)/shard_map/all_to_all | solution.py:332
  52.9 8.5 %all-to-all-done.from_ref = bf16[4,64,1024]{2,1,0:T(8,128)(2,1)} async-done(((bf16[4,64,1024]{2,1,0:T(8,128)(2,1)}), bf16[4,64,1024]{2,1,0:T(8,128)(2,1)}, u32[]{:S(2)}, u32[]{:S(2)}) %all-to-all-start) | async-done | bytes 524320 | tf_op jit(solution)/shard_map/all_to_all | solution.py:332
  65.5 2.6 %collective-permute-start.13 = (bf16[64,1024]{1,0:T(8,128)(2,1)}, bf16[64,1024]{1,0:T(8,128)(2,1)S(1)}, u32[]{:S(2)}, u32[]{:S(2)}) collective-permute-start(bf16[64,1024]{1,0:T(8,128)(2,1)} %get-tuple-element.25), channel_id=1, source_target_pairs={{0,24},{1,25},{2,26},{3,27},{4,28},{5,29},{6,30},{7,31},{8,16},{9,... | collective-permute-start | bytes 393224 | tf_op jit(solution)/shard_map/ppermute | solution.py:36
  70.0 4.0 %collective-permute-done.13.refs_0_ = bf16[64,1024]{1,0:T(8,128)(2,1)S(1)} collective-permute-done((bf16[64,1024]{1,0:T(8,128)(2,1)}, bf16[64,1024]{1,0:T(8,128)(2,1)S(1)}, u32[]{:S(2)}, u32[]{:S(2)}) %collective-permute-start.13) | collective-permute-done | bytes 131104 | tf_op jit(solution)/shard_map/ppermute | solution.py:36
  74.0 2.5 %collective-permute-done.14.refs_1_ = bf16[64,1024]{1,0:T(8,128)(2,1)S(1)} collective-permute-done((bf16[64,1024]{1,0:T(8,128)(2,1)}, bf16[64,1024]{1,0:T(8,128)(2,1)S(1)}, u32[]{:S(2)}, u32[]{:S(2)}) %collective-permute-start.14) | collective-permute-done | bytes 131104 | tf_op jit(solution)/shard_map/ppermute | solution.py:36
  76.4 2.8 %collective-permute-done.15.refs_2_ = bf16[64,1024]{1,0:T(8,128)(2,1)} collective-permute-done((bf16[64,1024]{1,0:T(8,128)(2,1)}, bf16[64,1024]{1,0:T(8,128)(2,1)}, u32[]{:S(2)}, u32[]{:S(2)}) %collective-permute-start.15) | collective-permute-done | bytes 131104 | tf_op jit(solution)/shard_map/ppermute | solution.py:36
  83.3 1.9 %project.4 = (bf16[128,1024]{1,0:T(8,128)(2,1)S(1)}, f32[128,1024]{1,0:T(8,128)S(1)}) custom-call(bf16[256,1024]{1,0:T(8,128)(2,1)S(1)} %arrange.1.acts_ref, bf16[256,2048]{1,0:T(8,128)(2,1)S(1)} %copy-done.1, bf16[256,2048]{1,0:T(8,128)(2,1)S(1)} %copy-done.8, bf16[256,2048]{1,0:T(8,128)(2,1)} %collective-permute-done.9.refs_0_.refs_2_, ...), custom_call_target="tpu_custom_call" | custom-call | flops 536870912 | bytes 3670016 | tf_op jit(solution)/shard_map/project/pallas_call | solution.py:257
  85.3 2.0 %project.5 = (bf16[128,1024]{1,0:T(8,128)(2,1)S(1)}, f32[128,1024]{1,0:T(8,128)S(1)}) custom-call(bf16[256,1024]{1,0:T(8,128)(2,1)S(1)} %arrange.1.acts_ref, bf16[256,2048]{1,0:T(8,128)(2,1)S(1)} %copy-done.1, bf16[256,2048]{1,0:T(8,128)(2,1)S(1)} %copy-done.8, bf16[256,2048]{1,0:T(8,128)(2,1)} %collective-permute-done.9.refs_0_.refs_2_, ...), custom_call_target="tpu_custom_call" | custom-call | flops 536870912 | bytes 3670016 | tf_op jit(solution)/shard_map/project/pallas_call | solution.py:257
  87.4 2.0 %collective-permute-start.18 = (bf16[128,1024]{1,0:T(8,128)(2,1)S(1)}, bf16[128,1024]{1,0:T(8,128)(2,1)S(1)}, u32[]{:S(2)}, u32[]{:S(2)}) collective-permute-start(bf16[128,1024]{1,0:T(8,128)(2,1)S(1)} %get-tuple-element.32), channel_id=1, source_target_pairs={{0,8},{1,9},{2,10},{3,11},{4,12},{5,13},{6,14},{7,15},{8,0},{9,1},... | collective-permute-start | bytes 786440 | tf_op jit(solution)/shard_map/ppermute | solution.py:36
  91.4 1.9 %project.7 = (bf16[128,1024]{1,0:T(8,128)(2,1)S(1)}, f32[128,1024]{1,0:T(8,128)S(1)}) custom-call(bf16[256,1024]{1,0:T(8,128)(2,1)S(1)} %arrange.1.acts_ref, bf16[256,2048]{1,0:T(8,128)(2,1)S(1)} %copy-done.3, bf16[256,2048]{1,0:T(8,128)(2,1)} %get-tuple-element.24.refs_1_, bf16[256,2048]{1,0:T(8,128)(2,1)S(1)} %collective-permute-done.11.refs_2_, ...), custom_call_target="tpu_custom_call" | custom-call | flops 536870912 | bytes 3670016 | tf_op jit(solution)/shard_map/project/pallas_call | solution.py:257
  93.4 2.0 %collective-permute-start.22 = (bf16[128,1024]{1,0:T(8,128)(2,1)S(1)}, bf16[128,1024]{1,0:T(8,128)(2,1)S(1)}, u32[]{:S(2)}, u32[]{:S(2)}) collective-permute-start(bf16[128,1024]{1,0:T(8,128)(2,1)S(1)} %get-tuple-element.36), channel_id=1, source_target_pairs={{0,8},{1,9},{2,10},{3,11},{4,12},{5,13},{6,14},{7,15},{8,0},{9,1},... | collective-permute-start | bytes 786440 | tf_op jit(solution)/shard_map/ppermute | solution.py:36
  96.7 7.6 %collective-permute-done.18 = bf16[128,1024]{1,0:T(8,128)(2,1)S(1)} collective-permute-done((bf16[128,1024]{1,0:T(8,128)(2,1)S(1)}, bf16[128,1024]{1,0:T(8,128)(2,1)S(1)}, u32[]{:S(2)}, u32[]{:S(2)}) %collective-permute-start.18) | collective-permute-done | bytes 262176 | tf_op jit(solution)/shard_map/ppermute | solution.py:36
  105.2 6.6 %collective-permute-done.20 = bf16[128,1024]{1,0:T(8,128)(2,1)S(1)} collective-permute-done((bf16[128,1024]{1,0:T(8,128)(2,1)S(1)}, bf16[128,1024]{1,0:T(8,128)(2,1)S(1)}, u32[]{:S(2)}, u32[]{:S(2)}) %collective-permute-start.20) | collective-permute-done | bytes 262176 | tf_op jit(solution)/shard_map/ppermute | solution.py:36
  112.0 2.7 %collective-permute-done.22 = bf16[128,1024]{1,0:T(8,128)(2,1)S(1)} collective-permute-done((bf16[128,1024]{1,0:T(8,128)(2,1)S(1)}, bf16[128,1024]{1,0:T(8,128)(2,1)S(1)}, u32[]{:S(2)}, u32[]{:S(2)}) %collective-permute-start.22) | collective-permute-done | bytes 262176 | tf_op jit(solution)/shard_map/ppermute | solution.py:36
  115.1 5.4 %collective-permute-done.19 = bf16[64,1024]{1,0:T(8,128)(2,1)S(1)} collective-permute-done((bf16[64,1024]{1,0:T(8,128)(2,1)S(1)}, bf16[64,1024]{1,0:T(8,128)(2,1)S(1)}, u32[]{:S(2)}, u32[]{:S(2)}) %collective-permute-start.19) | collective-permute-done | bytes 131104 | tf_op jit(solution)/shard_map/ppermute | solution.py:36
  120.5 2.8 %collective-permute-done.21 = bf16[64,1024]{1,0:T(8,128)(2,1)S(1)} collective-permute-done((bf16[64,1024]{1,0:T(8,128)(2,1)S(1)}, bf16[64,1024]{1,0:T(8,128)(2,1)S(1)}, u32[]{:S(2)}, u32[]{:S(2)}) %collective-permute-start.21) | collective-permute-done | bytes 131104 | tf_op jit(solution)/shard_map/ppermute | solution.py:36
  (74 shorter events, 28.8 us)
Async XLA Ops:
  0.0 7.5 %collective-permute-start.2 = (bf16[256,1024]{1,0:T(8,128)(2,1)}, bf16[256,1024]{1,0:T(8,128)(2,1)S(1)}, u32[]{:S(2)}, u32[]{:S(2)}) collective-permute-start(bf16[256,1024]{1,0:T(8,128)(2,1)} %rest_0_.1), channel_id=1, source_target_pairs={{0,4},{1,5},{2,6},{3,7},{8,12},{9,13},{10,14},{11,15},{16,20},{17,... | collective-permute-start | bytes 1572872 | tf_op jit(solution)/shard_map/ppermute | solution.py:36
  2.4 15.3 %collective-permute-start = (bf16[256,1024]{1,0:T(8,128)(2,1)}, bf16[256,1024]{1,0:T(8,128)(2,1)}, u32[]{:S(2)}, u32[]{:S(2)}) collective-permute-start(bf16[256,1024]{1,0:T(8,128)(2,1)} %rest_0_.1), channel_id=1, source_target_pairs={{0,8},{1,9},{2,10},{3,11},{4,12},{5,13},{6,14},{7,15},{8,16},{9,17... | collective-permute-start | bytes 1572872 | tf_op jit(solution)/shard_map/ppermute | solution.py:36
  8.8 14.1 %collective-permute-start.5 = (bf16[128,2048]{1,0:T(8,128)(2,1)S(1)}, bf16[128,2048]{1,0:T(8,128)(2,1)S(1)}, u32[]{:S(2)}, u32[]{:S(2)}) collective-permute-start(bf16[128,2048]{1,0:T(8,128)(2,1)S(1)} %join.4.refs_0_), channel_id=1, source_target_pairs={{0,1},{1,0},{2,3},{3,2},{4,5},{5,4},{6,7},{7,6},{8,9},{9,8},{10,11... | collective-permute-start | bytes 1572872 | tf_op jit(solution)/shard_map/ppermute | solution.py:36
  10.4 14.2 %collective-permute-start.7 = (bf16[128,2048]{1,0:T(8,128)(2,1)S(1)}, bf16[128,2048]{1,0:T(8,128)(2,1)S(1)}, u32[]{:S(2)}, u32[]{:S(2)}) collective-permute-start(bf16[128,2048]{1,0:T(8,128)(2,1)S(1)} %join.6.refs_0_), channel_id=1, source_target_pairs={{0,2},{1,3},{2,0},{3,1},{4,6},{5,7},{6,4},{7,5},{8,10},{9,11},{10,... | collective-permute-start | bytes 1572872 | tf_op jit(solution)/shard_map/ppermute | solution.py:36
  17.7 14.5 %collective-permute-start.1 = (bf16[256,1024]{1,0:T(8,128)(2,1)}, bf16[256,1024]{1,0:T(8,128)(2,1)}, u32[]{:S(2)}, u32[]{:S(2)}) collective-permute-start(bf16[256,1024]{1,0:T(8,128)(2,1)} %collective-permute-done.rest_1_), channel_id=1, source_target_pairs={{0,8},{1,9},{2,10},{3,11},{4,12},{5,13},{6,14},{7,15},{8,16},{9,17... | collective-permute-start | bytes 1572872 | tf_op jit(solution)/shard_map/ppermute | solution.py:36
  23.0 23.3 %collective-permute-start.6 = (bf16[256,2048]{1,0:T(8,128)(2,1)S(1)}, bf16[256,2048]{1,0:T(8,128)(2,1)S(1)}, u32[]{:S(2)}, u32[]{:S(2)}) collective-permute-start(bf16[256,2048]{1,0:T(8,128)(2,1)S(1)} %join.5.refs_0_), channel_id=1, source_target_pairs={{0,2},{1,3},{2,0},{3,1},{4,6},{5,7},{6,4},{7,5},{8,10},{9,11},{10,... | collective-permute-start | bytes 3145736 | tf_op jit(solution)/shard_map/ppermute | solution.py:36
  24.6 23.1 %collective-permute-start.8 = (bf16[256,2048]{1,0:T(8,128)(2,1)S(1)}, bf16[256,2048]{1,0:T(8,128)(2,1)}, u32[]{:S(2)}, u32[]{:S(2)}) collective-permute-start(bf16[256,2048]{1,0:T(8,128)(2,1)S(1)} %join.7.refs_2_), channel_id=1, source_target_pairs={{0,1},{1,0},{2,3},{3,2},{4,5},{5,4},{6,7},{7,6},{8,9},{9,8},{10,11... | collective-permute-start | bytes 3145736 | tf_op jit(solution)/shard_map/ppermute | solution.py:36
  26.2 7.3 %collective-permute-start.3 = (bf16[256,1024]{1,0:T(8,128)(2,1)}, bf16[256,1024]{1,0:T(8,128)(2,1)}, u32[]{:S(2)}, u32[]{:S(2)}) collective-permute-start(bf16[256,1024]{1,0:T(8,128)(2,1)} %collective-permute-done.rest_1_), channel_id=1, source_target_pairs={{0,4},{1,5},{2,6},{3,7},{4,0},{5,1},{6,2},{7,3},{8,12},{9,13},{10,... | collective-permute-start | bytes 1572872 | tf_op jit(solution)/shard_map/ppermute | solution.py:36
  47.7 13.7 %collective-permute-start.10 = (bf16[256,2048]{1,0:T(8,128)(2,1)}, bf16[256,2048]{1,0:T(8,128)(2,1)S(1)}, u32[]{:S(2)}, u32[]{:S(2)}) collective-permute-start(bf16[256,2048]{1,0:T(8,128)(2,1)} %get-tuple-element.22.refs_1_), channel_id=1, source_target_pairs={{0,4},{1,5},{2,6},{3,7},{4,0},{5,1},{6,2},{7,3},{8,12},{9,13},{10,... | collective-permute-start | bytes 3145736 | tf_op jit(solution)/shard_map/ppermute | solution.py:36
  47.7 14.7 %collective-permute-start.11 = (bf16[256,2048]{1,0:T(8,128)(2,1)}, bf16[256,2048]{1,0:T(8,128)(2,1)S(1)}, u32[]{:S(2)}, u32[]{:S(2)}) collective-permute-start(bf16[256,2048]{1,0:T(8,128)(2,1)} %get-tuple-element.23.refs_0_), channel_id=1, source_target_pairs={{0,4},{1,5},{2,6},{3,7},{4,0},{5,1},{6,2},{7,3},{8,12},{9,13},{10,... | collective-permute-start | bytes 3145736 | tf_op jit(solution)/shard_map/ppermute | solution.py:36
  48.2 14.2 %collective-permute-start.12 = (bf16[256,2048]{1,0:T(8,128)(2,1)}, bf16[256,2048]{1,0:T(8,128)(2,1)S(1)}, u32[]{:S(2)}, u32[]{:S(2)}) collective-permute-start(bf16[256,2048]{1,0:T(8,128)(2,1)} %get-tuple-element.24.refs_1_), channel_id=1, source_target_pairs={{0,4},{1,5},{2,6},{3,7},{4,0},{5,1},{6,2},{7,3},{8,12},{9,13},{10,... | collective-permute-start | bytes 3145736 | tf_op jit(solution)/shard_map/ppermute | solution.py:36
  48.3 14.2 %collective-permute-start.9 = (bf16[256,2048]{1,0:T(8,128)(2,1)}, bf16[256,2048]{1,0:T(8,128)(2,1)}, u32[]{:S(2)}, u32[]{:S(2)}) collective-permute-start(bf16[256,2048]{1,0:T(8,128)(2,1)} %get-tuple-element.21.refs_0_), channel_id=1, source_target_pairs={{0,4},{1,5},{2,6},{3,7},{4,0},{5,1},{6,2},{7,3},{8,12},{9,13},{10,... | collective-permute-start | bytes 3145736 | tf_op jit(solution)/shard_map/ppermute | solution.py:36
  48.8 12.7 %all-to-all-start = ((bf16[4,64,1024]{2,1,0:T(8,128)(2,1)}), bf16[4,64,1024]{2,1,0:T(8,128)(2,1)}, u32[]{:S(2)}, u32[]{:S(2)}) async-start(bf16[4,64,1024]{2,1,0:T(8,128)(2,1)} %bitcast.12), calls=%async_computation | async-start | bytes 1048576 | tf_op jit(solution)/shard_map/all_to_all | solution.py:332
  65.5 8.4 %collective-permute-start.13 = (bf16[64,1024]{1,0:T(8,128)(2,1)}, bf16[64,1024]{1,0:T(8,128)(2,1)S(1)}, u32[]{:S(2)}, u32[]{:S(2)}) collective-permute-start(bf16[64,1024]{1,0:T(8,128)(2,1)} %get-tuple-element.25), channel_id=1, source_target_pairs={{0,24},{1,25},{2,26},{3,27},{4,28},{5,29},{6,30},{7,31},{8,16},{9,... | collective-permute-start | bytes 393224 | tf_op jit(solution)/shard_map/ppermute | solution.py:36
  68.1 8.3 %collective-permute-start.14 = (bf16[64,1024]{1,0:T(8,128)(2,1)}, bf16[64,1024]{1,0:T(8,128)(2,1)S(1)}, u32[]{:S(2)}, u32[]{:S(2)}) collective-permute-start(bf16[64,1024]{1,0:T(8,128)(2,1)} %get-tuple-element.26), channel_id=1, source_target_pairs={{0,8},{1,9},{2,10},{3,11},{4,12},{5,13},{6,14},{7,15},{8,0},{9,1},... | collective-permute-start | bytes 393224 | tf_op jit(solution)/shard_map/ppermute | solution.py:36
  68.1 11.1 %collective-permute-start.15 = (bf16[64,1024]{1,0:T(8,128)(2,1)}, bf16[64,1024]{1,0:T(8,128)(2,1)}, u32[]{:S(2)}, u32[]{:S(2)}) collective-permute-start(bf16[64,1024]{1,0:T(8,128)(2,1)} %get-tuple-element.27), channel_id=1, source_target_pairs={{0,16},{1,17},{2,18},{3,19},{4,20},{5,21},{6,22},{7,23},{8,24},{9,... | collective-permute-start | bytes 393224 | tf_op jit(solution)/shard_map/ppermute | solution.py:36
  85.2 10.1 %collective-permute-start.16 = (bf16[128,1024]{1,0:T(8,128)(2,1)S(1)}, bf16[128,1024]{1,0:T(8,128)(2,1)S(1)}, u32[]{:S(2)}, u32[]{:S(2)}) collective-permute-start(bf16[128,1024]{1,0:T(8,128)(2,1)S(1)} %get-tuple-element.30), channel_id=1, source_target_pairs={{0,8},{1,9},{2,10},{3,11},{4,12},{5,13},{6,14},{7,15},{8,0},{9,1},... | collective-permute-start | bytes 786440 | tf_op jit(solution)/shard_map/ppermute | solution.py:36
  87.4 17.0 %collective-permute-start.18 = (bf16[128,1024]{1,0:T(8,128)(2,1)S(1)}, bf16[128,1024]{1,0:T(8,128)(2,1)S(1)}, u32[]{:S(2)}, u32[]{:S(2)}) collective-permute-start(bf16[128,1024]{1,0:T(8,128)(2,1)S(1)} %get-tuple-element.32), channel_id=1, source_target_pairs={{0,8},{1,9},{2,10},{3,11},{4,12},{5,13},{6,14},{7,15},{8,0},{9,1},... | collective-permute-start | bytes 786440 | tf_op jit(solution)/shard_map/ppermute | solution.py:36
  91.3 20.6 %collective-permute-start.20 = (bf16[128,1024]{1,0:T(8,128)(2,1)S(1)}, bf16[128,1024]{1,0:T(8,128)(2,1)S(1)}, u32[]{:S(2)}, u32[]{:S(2)}) collective-permute-start(bf16[128,1024]{1,0:T(8,128)(2,1)S(1)} %get-tuple-element.34), channel_id=1, source_target_pairs={{0,8},{1,9},{2,10},{3,11},{4,12},{5,13},{6,14},{7,15},{8,0},{9,1},... | collective-permute-start | bytes 786440 | tf_op jit(solution)/shard_map/ppermute | solution.py:36
  93.4 21.4 %collective-permute-start.22 = (bf16[128,1024]{1,0:T(8,128)(2,1)S(1)}, bf16[128,1024]{1,0:T(8,128)(2,1)S(1)}, u32[]{:S(2)}, u32[]{:S(2)}) collective-permute-start(bf16[128,1024]{1,0:T(8,128)(2,1)S(1)} %get-tuple-element.36), channel_id=1, source_target_pairs={{0,8},{1,9},{2,10},{3,11},{4,12},{5,13},{6,14},{7,15},{8,0},{9,1},... | collective-permute-start | bytes 786440 | tf_op jit(solution)/shard_map/ppermute | solution.py:36
  95.4 19.6 %collective-permute-start.17 = (bf16[64,1024]{1,0:T(8,128)(2,1)S(1)}, bf16[64,1024]{1,0:T(8,128)(2,1)S(1)}, u32[]{:S(2)}, u32[]{:S(2)}) collective-permute-start(bf16[64,1024]{1,0:T(8,128)(2,1)S(1)} %fusion.9), channel_id=1, source_target_pairs={{0,16},{1,17},{2,18},{3,19},{4,20},{5,21},{6,22},{7,23},{8,24},{9,... | collective-permute-start | bytes 393224 | tf_op jit(solution)/shard_map/ppermute | solution.py:36
  104.5 16.0 %collective-permute-start.19 = (bf16[64,1024]{1,0:T(8,128)(2,1)S(1)}, bf16[64,1024]{1,0:T(8,128)(2,1)S(1)}, u32[]{:S(2)}, u32[]{:S(2)}) collective-permute-start(bf16[64,1024]{1,0:T(8,128)(2,1)S(1)} %fusion.6), channel_id=1, source_target_pairs={{0,16},{1,17},{2,18},{3,19},{4,20},{5,21},{6,22},{7,23},{8,24},{9,... | collective-permute-start | bytes 393224 | tf_op jit(solution)/shard_map/ppermute | solution.py:36
  111.9 11.4 %collective-permute-start.21 = (bf16[64,1024]{1,0:T(8,128)(2,1)S(1)}, bf16[64,1024]{1,0:T(8,128)(2,1)S(1)}, u32[]{:S(2)}, u32[]{:S(2)}) collective-permute-start(bf16[64,1024]{1,0:T(8,128)(2,1)S(1)} %fusion.3), channel_id=1, source_target_pairs={{0,16},{1,17},{2,18},{3,19},{4,20},{5,21},{6,22},{7,23},{8,24},{9,... | collective-permute-start | bytes 393224 | tf_op jit(solution)/shard_map/ppermute | solution.py:36
  114.8 9.9 %collective-permute-start.23 = (bf16[64,1024]{1,0:T(8,128)(2,1)S(1)}, bf16[64,1024]{1,0:T(8,128)(2,1)S(1)}, u32[]{:S(2)}, u32[]{:S(2)}) collective-permute-start(bf16[64,1024]{1,0:T(8,128)(2,1)S(1)} %fusion), channel_id=1, source_target_pairs={{0,16},{1,17},{2,18},{3,19},{4,20},{5,21},{6,22},{7,23},{8,24},{9,... | collective-permute-start | bytes 393224 | tf_op jit(solution)/shard_map/ppermute | solution.py:36
  (12 other events, 74.5 us)

commit v2 on v1

--- a/solution.py
+++ b/solution.py
@@ -44,7 +44,7 @@
 
 
 def conv_kernel(lags, core_ref, table_ref, back_ref, skip_ref, gates_ref, filters_ref, *rest):
-    *block_refs, out_ref = rest
+    block_refs, out_ref = rest[: lags + 2], rest[-1]
     block = gates_ref.shape[0]
     half = block // 2
     odd = core_ref[0] == 1
@@ -84,7 +84,7 @@
     out_ref[...] = (gates_ref[...].astype(F32) * filtered).astype(BF16)
 
 
-def convolve(core, gates, filters, skip, direct, crossed):
+def convolve(core, gates, filters, skip, direct, crossed, deps):
     block, width = gates.shape
     taps = filters.shape[0]
     lags = taps // block
@@ -110,6 +110,7 @@
                 column(block),
                 column(taps),
                 *[column(block) for _ in blocks],
+                *[pl.BlockSpec(memory_space=pl.ANY) for _ in deps],
             ],
             out_specs=column(block),
         ),
@@ -128,6 +129,7 @@
         gates,
         filters,
         *blocks,
+        *deps,
     )
 
 
@@ -158,26 +160,44 @@
     )(*[array for array, _ in parts], *deps)
 
 
-def part_kernel(many, index_ref, from_ref, *refs):
-    for step, ref in enumerate(refs[-many:]):
-        ref[...] = from_ref[index_ref[0] ^ step]
-
-
-def part(index, array, deps):
+def part_kernel(many, slots, order_ref, from_ref, *refs):
+    width = from_ref.shape[2] // slots
+    for step, ref in enumerate(refs):
+        here = order_ref[slots] ^ step
+        if width % 128:
+            ref[...] = from_ref[here]
+            continue
+        for slot in range(slots):
+            start = pl.multiple_of(order_ref[slot] * width, width)
+            ref[:, slot * width : (slot + 1) * width] = from_ref[here, :, pl.ds(start, width)]
+
+
+def part(order, array):
     many, rows, depth = array.shape
-    return pl.pallas_call(
-        functools.partial(part_kernel, many),
-        grid_spec=pltpu.PrefetchScalarGridSpec(
-            num_scalar_prefetch=1,
-            grid=(1,),
-            in_specs=[pl.BlockSpec(array.shape, lambda i, *_: (0, 0, 0))]
-            + [pl.BlockSpec(memory_space=pl.ANY)] * len(deps),
-            out_specs=[pl.BlockSpec((rows, depth), lambda i, *_: (0, 0))] * many,
-        ),
-        out_shape=[jax.ShapeDtypeStruct((rows, depth), BF16)] * many,
-        compiler_params=pltpu.CompilerParams(vmem_limit_bytes=12 * 2**20),
-        name="part",
-    )(index.reshape(1), array, *deps)
+    slots = order.shape[0] - 1
+    width = depth // slots
+    if width % 128:
+        array = jnp.concatenate(
+            [
+                lax.dynamic_slice_in_dim(array, order[slot] * width, width, axis=2)
+                for slot in range(slots)
+            ],
+            axis=2,
+        )
+    return list(
+        pl.pallas_call(
+            functools.partial(part_kernel, many, slots),
+            grid_spec=pltpu.PrefetchScalarGridSpec(
+                num_scalar_prefetch=1,
+                grid=(1,),
+                in_specs=[pl.BlockSpec(array.shape, lambda i, *_: (0, 0, 0))],
+                out_specs=[pl.BlockSpec((rows, depth), lambda i, *_: (0, 0))] * many,
+            ),
+            out_shape=[jax.ShapeDtypeStruct((rows, depth), BF16)] * many,
+            compiler_params=pltpu.CompilerParams(vmem_limit_bytes=12 * 2**20),
+            name="part",
+        )(order, array)
+    )
 
 
 def fence_kernel(*refs):
@@ -196,69 +216,28 @@
     )(*arrays, *deps)
 
 
-def arrange_kernel(slots, order_ref, *refs):
-    out_ref = refs[-1]
-    rows, depth = refs[0].shape
-    width = depth // slots
-    for index, ref in enumerate(refs[:-1]):
-        here = slice(index * rows, (index + 1) * rows)
-        if width % 128:
-            out_ref[here, :] = ref[...]
-            continue
-        for slot in range(slots):
-            start = pl.multiple_of(order_ref[slot] * width, width)
-            out_ref[here, slot * width : (slot + 1) * width] = ref[:, pl.ds(start, width)]
-
-
-def arrange(order, acts):
-    slots = order.shape[0]
-    rows, depth = acts[0].shape
-    width = depth // slots
-    if width % 128:
-        acts = [
-            jnp.concatenate(
-                [
-                    lax.dynamic_slice_in_dim(act, order[slot] * width, width, axis=1)
-                    for slot in range(slots)
-                ],
-                axis=1,
-            )
-            for act in acts
-        ]
-    return pl.pallas_call(
-        functools.partial(arrange_kernel, slots),
-        grid_spec=pltpu.PrefetchScalarGridSpec(
-            num_scalar_prefetch=1,
-            grid=(1,),
-            in_specs=[pl.BlockSpec((rows, depth), lambda i, *_: (0, 0)) for _ in acts],
-            out_specs=pl.BlockSpec((rows * len(acts), depth), lambda i, *_: (0, 0)),
-        ),
-        out_shape=jax.ShapeDtypeStruct((rows * len(acts), depth), BF16),
-        compiler_params=pltpu.CompilerParams(vmem_limit_bytes=12 * 2**20),
-        name="arrange",
-    )(order, *acts)
-
-
-def project_kernel(spots, width, acts_ref, *refs):
-    piece_refs = refs[:-2]
+def project_kernel(count, spots, width, *refs):
+    act_refs, piece_refs = refs[:count], refs[count:-2]
     send_ref, keep_ref = refs[-2:]
-    rows = acts_ref.shape[0] // 2
+    rows = send_ref.shape[0]
     weight = jnp.concatenate(
         [piece_refs[piece][spot * width : (spot + 1) * width, :] for piece, spot in spots], axis=0
     )
-    total = jnp.dot(acts_ref[...], weight, preferred_element_type=F32)
+    acts = jnp.concatenate([act[...] for act in act_refs], axis=0)
+    total = jnp.dot(acts, weight, preferred_element_type=F32)
     send_ref[...] = total[:rows].astype(BF16)
     keep_ref[...] = total[rows:]
 
 
 def project(acts, pieces, spots, width, cols):
-    count, depth = acts.shape
+    rows, depth = acts[0].shape
+    count = rows * len(acts)
     tile = min(cols, 512)
     return pl.pallas_call(
-        functools.partial(project_kernel, spots, width),
+        functools.partial(project_kernel, len(acts), spots, width),
         grid=(cols // tile,),
         in_specs=[
-            pl.BlockSpec((count, depth), lambda i: (0, 0)),
+            *[pl.BlockSpec((rows, depth), lambda i: (0, 0)) for _ in acts],
             *[
                 pl.BlockSpec(
                     (piece.shape[0], tile), lambda i, first=first * cols // tile: (0, first + i)
@@ -278,7 +257,7 @@
             transcendentals=0,
         ),
         name="project",
-    )(acts, *[piece for piece, _ in pieces])
+    )(*acts, *[piece for piece, _ in pieces])
 
 
 def body(values, gates, filters, skip, out_weight):
@@ -327,26 +306,24 @@
             ]
         )
 
-    gated = convolve(core, gates, filters, skip, direct, crossed)
+    gated = convolve(core, gates, filters, skip, direct, crossed, [])
 
     spread = lax.all_to_all(
         gated.reshape(chans, rows, gated.shape[1]), "chan", split_axis=0, concat_axis=0
     )
     flat = fence([piece for pieces in parts for piece in pieces], [gated])
-    parts = [flat[:2], flat[2:]]
-    swaps = [[swap(piece) for piece in pieces] for pieces in parts]
-    parts = [[*pieces, *others] for pieces, others in zip(parts, swaps, strict=True)]
-    acts = list(part(pair, spread, [other for others in swaps for other in others]))
+    swaps = [swap(piece) for piece in flat]
+    parts = [[*flat[at : at + 2], *swaps[at : at + 2]] for at in (0, 2)]
+    (spread,) = fence([spread], swaps)
+    order = [which * chans + (chan ^ mask) for which in (core, 1 - core) for mask in range(chans)]
+    acts = part(jnp.stack([*order, pair]).astype(jnp.int32), spread)
     for step in range(1, pairs):
         acts[step] = permute(acts[step], lambda p, k, c, step=step: (p ^ step, k, c))
 
     count = pairs.bit_length() - 1
     steps = [1 << index for index in range(count)]
     ranks = sorted(range(pairs), key=lambda e: [not e & step for step in steps])
-    order = jnp.stack(
-        [which * chans + (chan ^ mask) for which in (core, 1 - core) for mask in range(chans)]
-    ).astype(jnp.int32)
-    acts = arrange(order, [acts[rank] for rank in ranks])
+    acts = [acts[rank] for rank in ranks]
 
     chunks = 4
     cols = model // chunks

time: 126 us -> 122 us (0.968)
  local copies, waits for them, and re-layouts: 5.97 us -> 3.87 us
  Pallas kernels: 19 us -> 17.6 us
    unnamed x22 -> x26, local copies, waits for them, and re-layouts: 5.89 us -> 3.78 us
    pallas_call x6 -> x5, Pallas kernels: 11.3 us -> 9.89 us  [the longest x4 8.18 us: project(): pl.pallas_call(functools.partial(project_kernel, len(acts), spots, width)...]
where the time goes in v2:
time: 122 us
  waiting for transfers between devices  62.2 us (51%)
  starting transfers between devices  36.4 us (30%)
  Pallas kernels  17.6 us (14%)
  local copies, waits for them, and re-layouts  3.87 us (3%)
  other arithmetic  1.28 us (1%)
    ppermute x24, waiting for transfers between devices, permute(): return lax.ppermute(value, AXES, route)  53.8 us
    ppermute x24, starting transfers between devices, permute(): return lax.ppermute(value, AXES, route)  32.2 us
    all_to_all x1, waiting for transfers between devices, body(): lax.all_to_all(gated.reshape(chans, rows, gated.shape[1]), 'chan', split_...  8.41 us
    pallas_call x4, Pallas kernels, project(): pl.pallas_call(functools.partial(project_kernel, len(acts), spots, width)...  8.18 us
    pallas_call x1, Pallas kernels, convolve(): pl.pallas_call(functools.partial(conv_kernel, lags), grid_spec=pltpu.Pref...  7.52 us
    all_to_all x1, starting transfers between devices, body(): lax.all_to_all(gated.reshape(chans, rows, gated.shape[1]), 'chan', split_...  4.14 us
    unnamed x26, local copies, waits for them, and re-layouts  3.78 us
  transfers between devices with their start and end apart: 25, of which 15 were waited for; matrix products, arithmetic and copies ran while one was open for 0% of the time, Pallas kernels for 11%

profile of v2, /device:TPU:0, one launch (start us, length us, event | category | flops | bytes accessed | tf_op | source)
XLA Modules:
  0.0 121.7 jit_solution(17080842902398191534)
XLA Ops:
  0.0 2.4 %collective-permute-start.2 = (bf16[256,1024]{1,0:T(8,128)(2,1)}, bf16[256,1024]{1,0:T(8,128)(2,1)S(1)}, u32[]{:S(2)}, u32[]{:S(2)}) collective-permute-start(bf16[256,1024]{1,0:T(8,128)(2,1)} %rest_0_.1), channel_id=1, source_target_pairs={{0,4},{1,5},{2,6},{3,7},{8,12},{9,13},{10,14},{11,15},{16,20},{17,... | collective-permute-start | bytes 1572872 | tf_op jit(solution)/shard_map/ppermute | solution.py:36
  2.4 5.1 %collective-permute-start = (bf16[256,1024]{1,0:T(8,128)(2,1)}, bf16[256,1024]{1,0:T(8,128)(2,1)}, u32[]{:S(2)}, u32[]{:S(2)}) collective-permute-start(bf16[256,1024]{1,0:T(8,128)(2,1)} %rest_0_.1), channel_id=1, source_target_pairs={{0,8},{1,9},{2,10},{3,11},{4,12},{5,13},{6,14},{7,15},{8,16},{9,17... | collective-permute-start | bytes 1572872 | tf_op jit(solution)/shard_map/ppermute | solution.py:36
  12.0 5.7 %collective-permute-done.rest_1_ = bf16[256,1024]{1,0:T(8,128)(2,1)} collective-permute-done((bf16[256,1024]{1,0:T(8,128)(2,1)}, bf16[256,1024]{1,0:T(8,128)(2,1)}, u32[]{:S(2)}, u32[]{:S(2)}) %collective-permute-start) | collective-permute-done | bytes 524320 | tf_op jit(solution)/shard_map/ppermute | solution.py:36
  17.7 5.2 %collective-permute-start.1 = (bf16[256,1024]{1,0:T(8,128)(2,1)}, bf16[256,1024]{1,0:T(8,128)(2,1)}, u32[]{:S(2)}, u32[]{:S(2)}) collective-permute-start(bf16[256,1024]{1,0:T(8,128)(2,1)} %collective-permute-done.rest_1_), channel_id=1, source_target_pairs={{0,8},{1,9},{2,10},{3,11},{4,12},{5,13},{6,14},{7,15},{8,16},{9,17... | collective-permute-start | bytes 1572872 | tf_op jit(solution)/shard_map/ppermute | solution.py:36
  26.2 5.9 %collective-permute-done.1.rest_2_ = bf16[256,1024]{1,0:T(8,128)(2,1)} collective-permute-done((bf16[256,1024]{1,0:T(8,128)(2,1)}, bf16[256,1024]{1,0:T(8,128)(2,1)}, u32[]{:S(2)}, u32[]{:S(2)}) %collective-permute-start.1) | collective-permute-done | bytes 524320 | tf_op jit(solution)/shard_map/ppermute | solution.py:36
  33.5 2.8 %collective-permute-done.4.rest_5_ = bf16[256,1024]{1,0:T(8,128)(2,1)} collective-permute-done((bf16[256,1024]{1,0:T(8,128)(2,1)}, bf16[256,1024]{1,0:T(8,128)(2,1)}, u32[]{:S(2)}, u32[]{:S(2)}) %collective-permute-start.4) | collective-permute-done | bytes 524320 | tf_op jit(solution)/shard_map/ppermute | solution.py:36
  36.3 7.5 %conv.1.refs_4_ = bf16[256,1024]{1,0:T(8,128)(2,1)} custom-call(s32[1]{0:T(128)} %bitcast.9.core_ref, bf16[512,256]{1,0:T(8,128)(2,1)} %constant.42.clone.table_ref, bf16[256,512]{1,0:T(8,128)(2,1)} %constant.43.clone.back_ref, f32[1,1024]{1,0:T(1,128)} %bitcast.12, bf16[256,1024]{1,0:T(8,128)(2,1)} %gates_ref.1, bf16[1024,1024]{1,0:T(8,128)(2,1)} %filters_ref.1, ...), custom_call_target="tpu_custom_call" | custom-call | flops 4026531840 | bytes 6291456 | tf_op jit(solution)/shard_map/conv/pallas_call | solution.py:101
  43.8 2.4 %collective-permute-done.6.refs_1_ = bf16[256,2048]{1,0:T(8,128)(2,1)S(1)} collective-permute-done((bf16[256,2048]{1,0:T(8,128)(2,1)S(1)}, bf16[256,2048]{1,0:T(8,128)(2,1)S(1)}, u32[]{:S(2)}, u32[]{:S(2)}) %collective-permute-start.6) | collective-permute-done | bytes 1048608 | tf_op jit(solution)/shard_map/ppermute | solution.py:36
  48.8 4.1 %all-to-all-start = ((bf16[4,64,1024]{2,1,0:T(8,128)(2,1)}), bf16[4,64,1024]{2,1,0:T(8,128)(2,1)}, u32[]{:S(2)}, u32[]{:S(2)}) async-start(bf16[4,64,1024]{2,1,0:T(8,128)(2,1)} %bitcast.11), calls=%async_computation | async-start | bytes 1048576 | tf_op jit(solution)/shard_map/all_to_all | solution.py:311
  53.1 8.4 %all-to-all-done.refs_0_ = bf16[4,64,1024]{2,1,0:T(8,128)(2,1)} async-done(((bf16[4,64,1024]{2,1,0:T(8,128)(2,1)}), bf16[4,64,1024]{2,1,0:T(8,128)(2,1)}, u32[]{:S(2)}, u32[]{:S(2)}) %all-to-all-start) | async-done | bytes 524320 | tf_op jit(solution)/shard_map/all_to_all | solution.py:311
  64.5 2.6 %collective-permute-start.13 = (bf16[64,1024]{1,0:T(8,128)(2,1)S(1)}, bf16[64,1024]{1,0:T(8,128)(2,1)S(1)}, u32[]{:S(2)}, u32[]{:S(2)}) collective-permute-start(bf16[64,1024]{1,0:T(8,128)(2,1)S(1)} %get-tuple-element.25), channel_id=1, source_target_pairs={{0,24},{1,25},{2,26},{3,27},{4,28},{5,29},{6,30},{7,31},{8,16},{9,... | collective-permute-start | bytes 393224 | tf_op jit(solution)/shard_map/ppermute | solution.py:36
  69.0 3.8 %collective-permute-done.13.refs_0_ = bf16[64,1024]{1,0:T(8,128)(2,1)S(1)} collective-permute-done((bf16[64,1024]{1,0:T(8,128)(2,1)S(1)}, bf16[64,1024]{1,0:T(8,128)(2,1)S(1)}, u32[]{:S(2)}, u32[]{:S(2)}) %collective-permute-start.13) | collective-permute-done | bytes 131104 | tf_op jit(solution)/shard_map/ppermute | solution.py:36
  72.8 2.5 %collective-permute-done.14.refs_1_ = bf16[64,1024]{1,0:T(8,128)(2,1)S(1)} collective-permute-done((bf16[64,1024]{1,0:T(8,128)(2,1)S(1)}, bf16[64,1024]{1,0:T(8,128)(2,1)S(1)}, u32[]{:S(2)}, u32[]{:S(2)}) %collective-permute-start.14) | collective-permute-done | bytes 131104 | tf_op jit(solution)/shard_map/ppermute | solution.py:36
  75.3 2.7 %collective-permute-done.15.refs_2_ = bf16[64,1024]{1,0:T(8,128)(2,1)S(1)} collective-permute-done((bf16[64,1024]{1,0:T(8,128)(2,1)S(1)}, bf16[64,1024]{1,0:T(8,128)(2,1)S(1)}, u32[]{:S(2)}, u32[]{:S(2)}) %collective-permute-start.15) | collective-permute-done | bytes 131104 | tf_op jit(solution)/shard_map/ppermute | solution.py:36
  79.2 2.1 %project.4 = (bf16[128,1024]{1,0:T(8,128)(2,1)S(1)}, f32[128,1024]{1,0:T(8,128)S(1)}) custom-call(bf16[64,1024]{1,0:T(8,128)(2,1)S(1)} %collective-permute-done.13.refs_0_, bf16[64,1024]{1,0:T(8,128)(2,1)S(1)} %collective-permute-done.14.refs_1_, bf16[64,1024]{1,0:T(8,128)(2,1)S(1)} %collective-permute-done.15.refs_2_, ...), custom_call_target="tpu_custom_call" | custom-call | flops 536870912 | bytes 3670016 | tf_op jit(solution)/shard_map/project/pallas_call | solution.py:236
  81.4 2.2 %project.5 = (bf16[128,1024]{1,0:T(8,128)(2,1)S(1)}, f32[128,1024]{1,0:T(8,128)S(1)}) custom-call(bf16[64,1024]{1,0:T(8,128)(2,1)S(1)} %collective-permute-done.13.refs_0_, bf16[64,1024]{1,0:T(8,128)(2,1)S(1)} %collective-permute-done.14.refs_1_, bf16[64,1024]{1,0:T(8,128)(2,1)S(1)} %collective-permute-done.15.refs_2_, ...), custom_call_target="tpu_custom_call" | custom-call | flops 536870912 | bytes 3670016 | tf_op jit(solution)/shard_map/project/pallas_call | solution.py:236
  85.6 1.9 %project.6 = (bf16[128,1024]{1,0:T(8,128)(2,1)S(1)}, f32[128,1024]{1,0:T(8,128)S(1)}) custom-call(bf16[64,1024]{1,0:T(8,128)(2,1)S(1)} %collective-permute-done.13.refs_0_, bf16[64,1024]{1,0:T(8,128)(2,1)S(1)} %collective-permute-done.14.refs_1_, bf16[64,1024]{1,0:T(8,128)(2,1)S(1)} %collective-permute-done.15.refs_2_, ...), custom_call_target="tpu_custom_call" | custom-call | flops 536870912 | bytes 3670016 | tf_op jit(solution)/shard_map/project/pallas_call | solution.py:236
  87.8 1.9 %project.7 = (bf16[128,1024]{1,0:T(8,128)(2,1)S(1)}, f32[128,1024]{1,0:T(8,128)S(1)}) custom-call(bf16[64,1024]{1,0:T(8,128)(2,1)S(1)} %collective-permute-done.13.refs_0_, bf16[64,1024]{1,0:T(8,128)(2,1)S(1)} %collective-permute-done.14.refs_1_, bf16[64,1024]{1,0:T(8,128)(2,1)S(1)} %collective-permute-done.15.refs_2_, ...), custom_call_target="tpu_custom_call" | custom-call | flops 536870912 | bytes 3670016 | tf_op jit(solution)/shard_map/project/pallas_call | solution.py:236
  89.7 1.9 %collective-permute-start.22 = (bf16[128,1024]{1,0:T(8,128)(2,1)S(1)}, bf16[128,1024]{1,0:T(8,128)(2,1)S(1)}, u32[]{:S(2)}, u32[]{:S(2)}) collective-permute-start(bf16[128,1024]{1,0:T(8,128)(2,1)S(1)} %get-tuple-element.36), channel_id=1, source_target_pairs={{0,8},{1,9},{2,10},{3,11},{4,12},{5,13},{6,14},{7,15},{8,0},{9,1},... | collective-permute-start | bytes 786440 | tf_op jit(solution)/shard_map/ppermute | solution.py:36
  93.0 7.5 %collective-permute-done.18 = bf16[128,1024]{1,0:T(8,128)(2,1)S(1)} collective-permute-done((bf16[128,1024]{1,0:T(8,128)(2,1)S(1)}, bf16[128,1024]{1,0:T(8,128)(2,1)S(1)}, u32[]{:S(2)}, u32[]{:S(2)}) %collective-permute-start.18) | collective-permute-done | bytes 262176 | tf_op jit(solution)/shard_map/ppermute | solution.py:36
  101.3 6.6 %collective-permute-done.20 = bf16[128,1024]{1,0:T(8,128)(2,1)S(1)} collective-permute-done((bf16[128,1024]{1,0:T(8,128)(2,1)S(1)}, bf16[128,1024]{1,0:T(8,128)(2,1)S(1)}, u32[]{:S(2)}, u32[]{:S(2)}) %collective-permute-start.20) | collective-permute-done | bytes 262176 | tf_op jit(solution)/shard_map/ppermute | solution.py:36
  108.1 2.7 %collective-permute-done.22 = bf16[128,1024]{1,0:T(8,128)(2,1)S(1)} collective-permute-done((bf16[128,1024]{1,0:T(8,128)(2,1)S(1)}, bf16[128,1024]{1,0:T(8,128)(2,1)S(1)}, u32[]{:S(2)}, u32[]{:S(2)}) %collective-permute-start.22) | collective-permute-done | bytes 262176 | tf_op jit(solution)/shard_map/ppermute | solution.py:36
  111.2 5.5 %collective-permute-done.19 = bf16[64,1024]{1,0:T(8,128)(2,1)S(1)} collective-permute-done((bf16[64,1024]{1,0:T(8,128)(2,1)S(1)}, bf16[64,1024]{1,0:T(8,128)(2,1)S(1)}, u32[]{:S(2)}, u32[]{:S(2)}) %collective-permute-start.19) | collective-permute-done | bytes 131104 | tf_op jit(solution)/shard_map/ppermute | solution.py:36
  116.7 2.7 %collective-permute-done.21 = bf16[64,1024]{1,0:T(8,128)(2,1)S(1)} collective-permute-done((bf16[64,1024]{1,0:T(8,128)(2,1)S(1)}, bf16[64,1024]{1,0:T(8,128)(2,1)S(1)}, u32[]{:S(2)}, u32[]{:S(2)}) %collective-permute-start.21) | collective-permute-done | bytes 131104 | tf_op jit(solution)/shard_map/ppermute | solution.py:36
  (78 shorter events, 25.0 us)
Async XLA Ops:
  0.0 7.5 %collective-permute-start.2 = (bf16[256,1024]{1,0:T(8,128)(2,1)}, bf16[256,1024]{1,0:T(8,128)(2,1)S(1)}, u32[]{:S(2)}, u32[]{:S(2)}) collective-permute-start(bf16[256,1024]{1,0:T(8,128)(2,1)} %rest_0_.1), channel_id=1, source_target_pairs={{0,4},{1,5},{2,6},{3,7},{8,12},{9,13},{10,14},{11,15},{16,20},{17,... | collective-permute-start | bytes 1572872 | tf_op jit(solution)/shard_map/ppermute | solution.py:36
  2.4 15.3 %collective-permute-start = (bf16[256,1024]{1,0:T(8,128)(2,1)}, bf16[256,1024]{1,0:T(8,128)(2,1)}, u32[]{:S(2)}, u32[]{:S(2)}) collective-permute-start(bf16[256,1024]{1,0:T(8,128)(2,1)} %rest_0_.1), channel_id=1, source_target_pairs={{0,8},{1,9},{2,10},{3,11},{4,12},{5,13},{6,14},{7,15},{8,16},{9,17... | collective-permute-start | bytes 1572872 | tf_op jit(solution)/shard_map/ppermute | solution.py:36
  8.8 14.1 %collective-permute-start.5 = (bf16[128,2048]{1,0:T(8,128)(2,1)S(1)}, bf16[128,2048]{1,0:T(8,128)(2,1)S(1)}, u32[]{:S(2)}, u32[]{:S(2)}) collective-permute-start(bf16[128,2048]{1,0:T(8,128)(2,1)S(1)} %join.4.refs_0_), channel_id=1, source_target_pairs={{0,1},{1,0},{2,3},{3,2},{4,5},{5,4},{6,7},{7,6},{8,9},{9,8},{10,11... | collective-permute-start | bytes 1572872 | tf_op jit(solution)/shard_map/ppermute | solution.py:36
  10.4 14.2 %collective-permute-start.7 = (bf16[128,2048]{1,0:T(8,128)(2,1)S(1)}, bf16[128,2048]{1,0:T(8,128)(2,1)S(1)}, u32[]{:S(2)}, u32[]{:S(2)}) collective-permute-start(bf16[128,2048]{1,0:T(8,128)(2,1)S(1)} %join.6.refs_0_), channel_id=1, source_target_pairs={{0,2},{1,3},{2,0},{3,1},{4,6},{5,7},{6,4},{7,5},{8,10},{9,11},{10,... | collective-permute-start | bytes 1572872 | tf_op jit(solution)/shard_map/ppermute | solution.py:36
  17.7 14.5 %collective-permute-start.1 = (bf16[256,1024]{1,0:T(8,128)(2,1)}, bf16[256,1024]{1,0:T(8,128)(2,1)}, u32[]{:S(2)}, u32[]{:S(2)}) collective-permute-start(bf16[256,1024]{1,0:T(8,128)(2,1)} %collective-permute-done.rest_1_), channel_id=1, source_target_pairs={{0,8},{1,9},{2,10},{3,11},{4,12},{5,13},{6,14},{7,15},{8,16},{9,17... | collective-permute-start | bytes 1572872 | tf_op jit(solution)/shard_map/ppermute | solution.py:36
  23.0 23.3 %collective-permute-start.6 = (bf16[256,2048]{1,0:T(8,128)(2,1)S(1)}, bf16[256,2048]{1,0:T(8,128)(2,1)S(1)}, u32[]{:S(2)}, u32[]{:S(2)}) collective-permute-start(bf16[256,2048]{1,0:T(8,128)(2,1)S(1)} %join.5.refs_0_), channel_id=1, source_target_pairs={{0,2},{1,3},{2,0},{3,1},{4,6},{5,7},{6,4},{7,5},{8,10},{9,11},{10,... | collective-permute-start | bytes 3145736 | tf_op jit(solution)/shard_map/ppermute | solution.py:36
  24.7 23.1 %collective-permute-start.8 = (bf16[256,2048]{1,0:T(8,128)(2,1)S(1)}, bf16[256,2048]{1,0:T(8,128)(2,1)}, u32[]{:S(2)}, u32[]{:S(2)}) collective-permute-start(bf16[256,2048]{1,0:T(8,128)(2,1)S(1)} %join.7.refs_2_), channel_id=1, source_target_pairs={{0,1},{1,0},{2,3},{3,2},{4,5},{5,4},{6,7},{7,6},{8,9},{9,8},{10,11... | collective-permute-start | bytes 3145736 | tf_op jit(solution)/shard_map/ppermute | solution.py:36
  26.2 7.3 %collective-permute-start.3 = (bf16[256,1024]{1,0:T(8,128)(2,1)}, bf16[256,1024]{1,0:T(8,128)(2,1)}, u32[]{:S(2)}, u32[]{:S(2)}) collective-permute-start(bf16[256,1024]{1,0:T(8,128)(2,1)} %collective-permute-done.rest_1_), channel_id=1, source_target_pairs={{0,4},{1,5},{2,6},{3,7},{4,0},{5,1},{6,2},{7,3},{8,12},{9,13},{10,... | collective-permute-start | bytes 1572872 | tf_op jit(solution)/shard_map/ppermute | solution.py:36
  47.8 13.7 %collective-permute-start.10 = (bf16[256,2048]{1,0:T(8,128)(2,1)}, bf16[256,2048]{1,0:T(8,128)(2,1)}, u32[]{:S(2)}, u32[]{:S(2)}) collective-permute-start(bf16[256,2048]{1,0:T(8,128)(2,1)} %get-tuple-element.22.refs_5_), channel_id=1, source_target_pairs={{0,4},{1,5},{2,6},{3,7},{4,0},{5,1},{6,2},{7,3},{8,12},{9,13},{10,... | collective-permute-start | bytes 3145736 | tf_op jit(solution)/shard_map/ppermute | solution.py:36
  47.8 13.7 %collective-permute-start.11 = (bf16[256,2048]{1,0:T(8,128)(2,1)}, bf16[256,2048]{1,0:T(8,128)(2,1)S(1)}, u32[]{:S(2)}, u32[]{:S(2)}) collective-permute-start(bf16[256,2048]{1,0:T(8,128)(2,1)} %get-tuple-element.23.refs_4_), channel_id=1, source_target_pairs={{0,4},{1,5},{2,6},{3,7},{4,0},{5,1},{6,2},{7,3},{8,12},{9,13},{10,... | collective-permute-start | bytes 3145736 | tf_op jit(solution)/shard_map/ppermute | solution.py:36
  48.3 13.2 %collective-permute-start.12 = (bf16[256,2048]{1,0:T(8,128)(2,1)}, bf16[256,2048]{1,0:T(8,128)(2,1)S(1)}, u32[]{:S(2)}, u32[]{:S(2)}) collective-permute-start(bf16[256,2048]{1,0:T(8,128)(2,1)} %get-tuple-element.24.refs_5_), channel_id=1, source_target_pairs={{0,4},{1,5},{2,6},{3,7},{4,0},{5,1},{6,2},{7,3},{8,12},{9,13},{10,... | collective-permute-start | bytes 3145736 | tf_op jit(solution)/shard_map/ppermute | solution.py:36
  48.3 13.2 %collective-permute-start.9 = (bf16[256,2048]{1,0:T(8,128)(2,1)}, bf16[256,2048]{1,0:T(8,128)(2,1)}, u32[]{:S(2)}, u32[]{:S(2)}) collective-permute-start(bf16[256,2048]{1,0:T(8,128)(2,1)} %get-tuple-element.21.refs_4_), channel_id=1, source_target_pairs={{0,4},{1,5},{2,6},{3,7},{4,0},{5,1},{6,2},{7,3},{8,12},{9,13},{10,... | collective-permute-start | bytes 3145736 | tf_op jit(solution)/shard_map/ppermute | solution.py:36
  48.8 12.7 %all-to-all-start = ((bf16[4,64,1024]{2,1,0:T(8,128)(2,1)}), bf16[4,64,1024]{2,1,0:T(8,128)(2,1)}, u32[]{:S(2)}, u32[]{:S(2)}) async-start(bf16[4,64,1024]{2,1,0:T(8,128)(2,1)} %bitcast.11), calls=%async_computation | async-start | bytes 1048576 | tf_op jit(solution)/shard_map/all_to_all | solution.py:311
  64.5 8.3 %collective-permute-start.13 = (bf16[64,1024]{1,0:T(8,128)(2,1)S(1)}, bf16[64,1024]{1,0:T(8,128)(2,1)S(1)}, u32[]{:S(2)}, u32[]{:S(2)}) collective-permute-start(bf16[64,1024]{1,0:T(8,128)(2,1)S(1)} %get-tuple-element.25), channel_id=1, source_target_pairs={{0,24},{1,25},{2,26},{3,27},{4,28},{5,29},{6,30},{7,31},{8,16},{9,... | collective-permute-start | bytes 393224 | tf_op jit(solution)/shard_map/ppermute | solution.py:36
  67.1 8.1 %collective-permute-start.14 = (bf16[64,1024]{1,0:T(8,128)(2,1)S(1)}, bf16[64,1024]{1,0:T(8,128)(2,1)S(1)}, u32[]{:S(2)}, u32[]{:S(2)}) collective-permute-start(bf16[64,1024]{1,0:T(8,128)(2,1)S(1)} %get-tuple-element.26), channel_id=1, source_target_pairs={{0,8},{1,9},{2,10},{3,11},{4,12},{5,13},{6,14},{7,15},{8,0},{9,1},... | collective-permute-start | bytes 393224 | tf_op jit(solution)/shard_map/ppermute | solution.py:36
  67.1 10.8 %collective-permute-start.15 = (bf16[64,1024]{1,0:T(8,128)(2,1)S(1)}, bf16[64,1024]{1,0:T(8,128)(2,1)S(1)}, u32[]{:S(2)}, u32[]{:S(2)}) collective-permute-start(bf16[64,1024]{1,0:T(8,128)(2,1)S(1)} %get-tuple-element.27), channel_id=1, source_target_pairs={{0,16},{1,17},{2,18},{3,19},{4,20},{5,21},{6,22},{7,23},{8,24},{9,... | collective-permute-start | bytes 393224 | tf_op jit(solution)/shard_map/ppermute | solution.py:36
  81.3 10.2 %collective-permute-start.16 = (bf16[128,1024]{1,0:T(8,128)(2,1)S(1)}, bf16[128,1024]{1,0:T(8,128)(2,1)S(1)}, u32[]{:S(2)}, u32[]{:S(2)}) collective-permute-start(bf16[128,1024]{1,0:T(8,128)(2,1)S(1)} %get-tuple-element.30), channel_id=1, source_target_pairs={{0,8},{1,9},{2,10},{3,11},{4,12},{5,13},{6,14},{7,15},{8,0},{9,1},... | collective-permute-start | bytes 786440 | tf_op jit(solution)/shard_map/ppermute | solution.py:36
  83.7 16.8 %collective-permute-start.18 = (bf16[128,1024]{1,0:T(8,128)(2,1)S(1)}, bf16[128,1024]{1,0:T(8,128)(2,1)S(1)}, u32[]{:S(2)}, u32[]{:S(2)}) collective-permute-start(bf16[128,1024]{1,0:T(8,128)(2,1)S(1)} %get-tuple-element.32), channel_id=1, source_target_pairs={{0,8},{1,9},{2,10},{3,11},{4,12},{5,13},{6,14},{7,15},{8,0},{9,1},... | collective-permute-start | bytes 786440 | tf_op jit(solution)/shard_map/ppermute | solution.py:36
  87.5 20.4 %collective-permute-start.20 = (bf16[128,1024]{1,0:T(8,128)(2,1)S(1)}, bf16[128,1024]{1,0:T(8,128)(2,1)S(1)}, u32[]{:S(2)}, u32[]{:S(2)}) collective-permute-start(bf16[128,1024]{1,0:T(8,128)(2,1)S(1)} %get-tuple-element.34), channel_id=1, source_target_pairs={{0,8},{1,9},{2,10},{3,11},{4,12},{5,13},{6,14},{7,15},{8,0},{9,1},... | collective-permute-start | bytes 786440 | tf_op jit(solution)/shard_map/ppermute | solution.py:36
  89.7 21.1 %collective-permute-start.22 = (bf16[128,1024]{1,0:T(8,128)(2,1)S(1)}, bf16[128,1024]{1,0:T(8,128)(2,1)S(1)}, u32[]{:S(2)}, u32[]{:S(2)}) collective-permute-start(bf16[128,1024]{1,0:T(8,128)(2,1)S(1)} %get-tuple-element.36), channel_id=1, source_target_pairs={{0,8},{1,9},{2,10},{3,11},{4,12},{5,13},{6,14},{7,15},{8,0},{9,1},... | collective-permute-start | bytes 786440 | tf_op jit(solution)/shard_map/ppermute | solution.py:36
  91.7 19.4 %collective-permute-start.17 = (bf16[64,1024]{1,0:T(8,128)(2,1)S(1)}, bf16[64,1024]{1,0:T(8,128)(2,1)S(1)}, u32[]{:S(2)}, u32[]{:S(2)}) collective-permute-start(bf16[64,1024]{1,0:T(8,128)(2,1)S(1)} %fusion.9), channel_id=1, source_target_pairs={{0,16},{1,17},{2,18},{3,19},{4,20},{5,21},{6,22},{7,23},{8,24},{9,... | collective-permute-start | bytes 393224 | tf_op jit(solution)/shard_map/ppermute | solution.py:36
  100.6 16.1 %collective-permute-start.19 = (bf16[64,1024]{1,0:T(8,128)(2,1)S(1)}, bf16[64,1024]{1,0:T(8,128)(2,1)S(1)}, u32[]{:S(2)}, u32[]{:S(2)}) collective-permute-start(bf16[64,1024]{1,0:T(8,128)(2,1)S(1)} %fusion.6), channel_id=1, source_target_pairs={{0,16},{1,17},{2,18},{3,19},{4,20},{5,21},{6,22},{7,23},{8,24},{9,... | collective-permute-start | bytes 393224 | tf_op jit(solution)/shard_map/ppermute | solution.py:36
  108.0 11.5 %collective-permute-start.21 = (bf16[64,1024]{1,0:T(8,128)(2,1)S(1)}, bf16[64,1024]{1,0:T(8,128)(2,1)S(1)}, u32[]{:S(2)}, u32[]{:S(2)}) collective-permute-start(bf16[64,1024]{1,0:T(8,128)(2,1)S(1)} %fusion.3), channel_id=1, source_target_pairs={{0,16},{1,17},{2,18},{3,19},{4,20},{5,21},{6,22},{7,23},{8,24},{9,... | collective-permute-start | bytes 393224 | tf_op jit(solution)/shard_map/ppermute | solution.py:36
  110.9 10.0 %collective-permute-start.23 = (bf16[64,1024]{1,0:T(8,128)(2,1)S(1)}, bf16[64,1024]{1,0:T(8,128)(2,1)S(1)}, u32[]{:S(2)}, u32[]{:S(2)}) collective-permute-start(bf16[64,1024]{1,0:T(8,128)(2,1)S(1)} %fusion), channel_id=1, source_target_pairs={{0,16},{1,17},{2,18},{3,19},{4,20},{5,21},{6,22},{7,23},{8,24},{9,... | collective-permute-start | bytes 393224 | tf_op jit(solution)/shard_map/ppermute | solution.py:36
  (14 other events, 91.9 us)

commit v3 on v2

--- a/solution.py
+++ b/solution.py
@@ -44,7 +44,7 @@
 
 
 def conv_kernel(lags, core_ref, table_ref, back_ref, skip_ref, gates_ref, filters_ref, *rest):
-    block_refs, out_ref = rest[: lags + 2], rest[-1]
+    block_refs, out_refs = rest[: lags + 2], rest[-2:]
     block = gates_ref.shape[0]
     half = block // 2
     odd = core_ref[0] == 1
@@ -81,7 +81,12 @@
     spectrum = jnp.concatenate([real, imag], axis=0).astype(BF16)
     filtered = jnp.dot(back_ref[...], spectrum, preferred_element_type=F32) * (1.0 / block)
     filtered = filtered + skip_ref[...] * direct[0][...].astype(F32)
-    out_ref[...] = (gates_ref[...].astype(F32) * filtered).astype(BF16)
+    result = (gates_ref[...].astype(F32) * filtered).astype(BF16)
+    chans, few, _ = out_refs[0].shape
+    for chan in range(chans):
+        for which, ref in enumerate(out_refs):
+            start = (2 * chan + which) * few
+            ref[chan] = result[start : start + few]
 
 
 def convolve(core, gates, filters, skip, direct, crossed, deps):
@@ -89,7 +94,9 @@
     taps = filters.shape[0]
     lags = taps // block
     forth = table(block)
-    tile = min(width, 256)
+    _, chans = sizes()
+    few = block // chans // 2
+    tile = min(width, 512)
 
     def column(rows):
         return pl.BlockSpec((rows, tile), lambda i, *_: (0, i))
@@ -112,9 +119,9 @@
                 *[column(block) for _ in blocks],
                 *[pl.BlockSpec(memory_space=pl.ANY) for _ in deps],
             ],
-            out_specs=column(block),
+            out_specs=[pl.BlockSpec((chans, few, tile), lambda i, *_: (0, 0, i))] * 2,
         ),
-        out_shape=jax.ShapeDtypeStruct((block, width), BF16),
+        out_shape=[jax.ShapeDtypeStruct((chans, few, width), BF16)] * 2,
         cost_estimate=pl.CostEstimate(
             flops=2 * (3 * lags + 3) * 2 * block * block * width,
             bytes_accessed=2 * width * (taps + (len(blocks) + 2) * block),
@@ -212,40 +219,42 @@
         out_specs=[anywhere] * len(arrays),
         out_shape=[jax.ShapeDtypeStruct(array.shape, array.dtype) for array in arrays],
         input_output_aliases={index: index for index in range(len(arrays))},
+        compiler_params=pltpu.CompilerParams(vmem_limit_bytes=2**20),
         name="fence",
     )(*arrays, *deps)
 
 
-def project_kernel(count, spots, width, *refs):
+def project_kernel(count, firsts, tile, spots, width, *refs):
     act_refs, piece_refs = refs[:count], refs[count:-2]
     send_ref, keep_ref = refs[-2:]
-    rows = send_ref.shape[0]
-    weight = jnp.concatenate(
-        [piece_refs[piece][spot * width : (spot + 1) * width, :] for piece, spot in spots], axis=0
-    )
+    rows, cols = send_ref.shape
     acts = jnp.concatenate([act[...] for act in act_refs], axis=0)
-    total = jnp.dot(acts, weight, preferred_element_type=F32)
-    send_ref[...] = total[:rows].astype(BF16)
-    keep_ref[...] = total[rows:]
+    for start in range(0, cols, tile):
+        weight = jnp.concatenate(
+            [
+                piece_refs[piece][
+                    spot * width : (spot + 1) * width,
+                    firsts[piece] * cols + start : firsts[piece] * cols + start + tile,
+                ]
+                for piece, spot in spots
+            ],
+            axis=0,
+        )
+        total = jnp.dot(acts, weight, preferred_element_type=F32)
+        send_ref[:, start : start + tile] = total[:rows].astype(BF16)
+        keep_ref[:, start : start + tile] = total[rows:]
 
 
 def project(acts, pieces, spots, width, cols):
     rows, depth = acts[0].shape
     count = rows * len(acts)
     tile = min(cols, 512)
+    firsts = [first for _, first in pieces]
+    held = pl.BlockSpec(memory_space=pltpu.VMEM)
     return pl.pallas_call(
-        functools.partial(project_kernel, len(acts), spots, width),
-        grid=(cols // tile,),
-        in_specs=[
-            *[pl.BlockSpec((rows, depth), lambda i: (0, 0)) for _ in acts],
-            *[
-                pl.BlockSpec(
-                    (piece.shape[0], tile), lambda i, first=first * cols // tile: (0, first + i)
-                )
-                for piece, first in pieces
-            ],
-        ],
-        out_specs=[pl.BlockSpec((count // 2, tile), lambda i: (0, i))] * 2,
+        functools.partial(project_kernel, len(acts), firsts, tile, spots, width),
+        in_specs=[held] * (len(acts) + len(pieces)),
+        out_specs=[held] * 2,
         out_shape=[
             jax.ShapeDtypeStruct((count // 2, cols), BF16),
             jax.ShapeDtypeStruct((count // 2, cols), F32),
@@ -308,41 +317,44 @@
 
     gated = convolve(core, gates, filters, skip, direct, crossed, [])
 
-    spread = lax.all_to_all(
-        gated.reshape(chans, rows, gated.shape[1]), "chan", split_axis=0, concat_axis=0
-    )
-    flat = fence([piece for pieces in parts for piece in pieces], [gated])
+    spreads = [lax.all_to_all(some, "chan", split_axis=0, concat_axis=0) for some in gated]
+
+    flat = fence([piece for pieces in parts for piece in pieces], gated[:1])
     swaps = [swap(piece) for piece in flat]
     parts = [[*flat[at : at + 2], *swaps[at : at + 2]] for at in (0, 2)]
-    (spread,) = fence([spread], swaps)
+    spreads = [fence([some], swaps)[0] for some in spreads]
     order = [which * chans + (chan ^ mask) for which in (core, 1 - core) for mask in range(chans)]
-    acts = part(jnp.stack([*order, pair]).astype(jnp.int32), spread)
-    for step in range(1, pairs):
-        acts[step] = permute(acts[step], lambda p, k, c, step=step: (p ^ step, k, c))
+    order = jnp.stack([*order, pair]).astype(jnp.int32)
+    acts = []
+    for spread in spreads:
+        some = part(order, spread)
+        for step in range(1, pairs):
+            some[step] = permute(some[step], lambda p, k, c, step=step: (p ^ step, k, c))
+        acts.append(some)
 
     count = pairs.bit_length() - 1
     steps = [1 << index for index in range(count)]
     ranks = sorted(range(pairs), key=lambda e: [not e & step for step in steps])
-    acts = [acts[rank] for rank in ranks]
-
-    chunks = 4
-    cols = model // chunks
+    acts = [[some[rank] for rank in ranks] for some in acts]
+
     outs = []
-    for chunk in range(chunks):
-        which = chunk // 2
-        send, keep = project(
-            acts, [(piece, chunk % 2) for piece in parts[which]], spots[which], own_rows, cols
-        )
-        for index, step in enumerate(steps):
-            got = permute(send, lambda p, k, c, step=step: (p ^ step, k, c)).astype(F32)
-            many = got.shape[0] // 2
-            if index + 1 < count:
-                send = (keep[:many] + got[:many]).astype(BF16)
-                keep = keep[many:] + got[many:]
-            else:
-                keep = keep + got
-        outs.append(keep.astype(BF16))
-    return jnp.concatenate(outs, axis=1)
+    for some in acts:
+        row = []
+        for which in range(2):
+            send, keep = project(
+                some, [(piece, 0) for piece in parts[which]], spots[which], own_rows, half
+            )
+            for index, step in enumerate(steps):
+                got = permute(send, lambda p, k, c, step=step: (p ^ step, k, c)).astype(F32)
+                many = got.shape[0] // 2
+                if index + 1 < count:
+                    send = (keep[:many] + got[:many]).astype(BF16)
+                    keep = keep[many:] + got[many:]
+                else:
+                    keep = keep + got
+            row.append(keep.astype(BF16))
+        outs.append(jnp.concatenate(row, axis=1))
+    return jnp.concatenate(outs, axis=0)
 
 
 def solution(mesh):

time: 122 us -> 120 us (0.984)
  waiting for transfers between devices: 62.2 us -> 48 us
  starting transfers between devices: 36.4 us -> 45.4 us
  Pallas kernels: 17.6 us -> 19.1 us
    ppermute x24 -> x27, waiting for transfers between devices: 53.8 us -> 42.3 us  [permute(): return lax.ppermute(value, AXES, route)]
    ppermute x24 -> x27, starting transfers between devices: 32.2 us -> 38.6 us  [permute(): return lax.ppermute(value, AXES, route)]
    all_to_all x1 -> x2, waiting for transfers between devices: 8.41 us -> 5.66 us  [body(): lax.all_to_all(some, 'chan', split_axis=0, concat_axis=0)]
    all_to_all x1 -> x2, starting transfers between devices: 4.14 us -> 6.81 us  [body(): lax.all_to_all(some, 'chan', split_axis=0, concat_axis=0)]
    pallas_call x4, Pallas kernels: 8.18 us -> 9.87 us  [project(): pl.pallas_call(functools.partial(project_kernel, len(acts), firsts, tile,...]
    unnamed x26 -> x14, local copies, waits for them, and re-layouts: 3.78 us -> 3.96 us
  transfers between devices with their start and end apart: 25 -> 29, of which waited for: 15 -> 14; matrix products, arithmetic and copies ran while one was open for 0% -> 1% of each run, Pallas kernels for 11% -> 15%
where the time goes in v3:
time: 120 us; the launch traced here: 119 us
  waiting for transfers between devices  48 us (40%)
  starting transfers between devices  45.4 us (38%)
  Pallas kernels  19.1 us (16%)
  local copies, waits for them, and re-layouts  4.04 us (3%)
  other arithmetic  2.18 us (2%)
    ppermute x27, waiting for transfers between devices, permute(): return lax.ppermute(value, AXES, route)  42.3 us
    ppermute x27, starting transfers between devices, permute(): return lax.ppermute(value, AXES, route)  38.6 us
    pallas_call x4, Pallas kernels, project(): pl.pallas_call(functools.partial(project_kernel, len(acts), firsts, tile,...  9.87 us
    pallas_call x1, Pallas kernels, convolve(): pl.pallas_call(functools.partial(conv_kernel, lags), grid_spec=pltpu.Pref...  7.12 us
    all_to_all x2, starting transfers between devices, body(): lax.all_to_all(some, 'chan', split_axis=0, concat_axis=0)  6.81 us
    all_to_all x2, waiting for transfers between devices, body(): lax.all_to_all(some, 'chan', split_axis=0, concat_axis=0)  5.66 us
    unnamed x14, local copies, waits for them, and re-layouts  3.96 us
  transfers between devices with their start and end apart: 29, of which 14 were waited for; matrix products, arithmetic and copies ran while one was open for 1% of the time, Pallas kernels for 15%

profile of v3, /device:TPU:0, one launch (start us, length us, event | category | flops | bytes accessed | tf_op | source)
XLA Modules:
  0.0 119.0 jit_solution(12253969036662475816)
XLA Ops:
  0.0 2.4 %collective-permute-start.2 = (bf16[256,1024]{1,0:T(8,128)(2,1)}, bf16[256,1024]{1,0:T(8,128)(2,1)S(1)}, u32[]{:S(2)}, u32[]{:S(2)}) collective-permute-start(bf16[256,1024]{1,0:T(8,128)(2,1)} %rest_0_.1), channel_id=1, source_target_pairs={{0,4},{1,5},{2,6},{3,7},{8,12},{9,13},{10,14},{11,15},{16,20},{17,... | collective-permute-start | bytes 1572872 | tf_op jit(solution)/shard_map/ppermute | solution.py:36
  2.4 5.1 %collective-permute-start = (bf16[256,1024]{1,0:T(8,128)(2,1)}, bf16[256,1024]{1,0:T(8,128)(2,1)}, u32[]{:S(2)}, u32[]{:S(2)}) collective-permute-start(bf16[256,1024]{1,0:T(8,128)(2,1)} %rest_0_.1), channel_id=1, source_target_pairs={{0,8},{1,9},{2,10},{3,11},{4,12},{5,13},{6,14},{7,15},{8,16},{9,17... | collective-permute-start | bytes 1572872 | tf_op jit(solution)/shard_map/ppermute | solution.py:36
  12.0 5.7 %collective-permute-done.rest_1_ = bf16[256,1024]{1,0:T(8,128)(2,1)} collective-permute-done((bf16[256,1024]{1,0:T(8,128)(2,1)}, bf16[256,1024]{1,0:T(8,128)(2,1)}, u32[]{:S(2)}, u32[]{:S(2)}) %collective-permute-start) | collective-permute-done | bytes 524320 | tf_op jit(solution)/shard_map/ppermute | solution.py:36
  17.7 5.2 %collective-permute-start.1 = (bf16[256,1024]{1,0:T(8,128)(2,1)}, bf16[256,1024]{1,0:T(8,128)(2,1)}, u32[]{:S(2)}, u32[]{:S(2)}) collective-permute-start(bf16[256,1024]{1,0:T(8,128)(2,1)} %collective-permute-done.rest_1_), channel_id=1, source_target_pairs={{0,8},{1,9},{2,10},{3,11},{4,12},{5,13},{6,14},{7,15},{8,16},{9,17... | collective-permute-start | bytes 1572872 | tf_op jit(solution)/shard_map/ppermute | solution.py:36
  26.2 5.9 %collective-permute-done.1.rest_2_ = bf16[256,1024]{1,0:T(8,128)(2,1)} collective-permute-done((bf16[256,1024]{1,0:T(8,128)(2,1)}, bf16[256,1024]{1,0:T(8,128)(2,1)}, u32[]{:S(2)}, u32[]{:S(2)}) %collective-permute-start.1) | collective-permute-done | bytes 524320 | tf_op jit(solution)/shard_map/ppermute | solution.py:36
  33.5 2.8 %collective-permute-done.4.rest_5_ = bf16[256,1024]{1,0:T(8,128)(2,1)} collective-permute-done((bf16[256,1024]{1,0:T(8,128)(2,1)}, bf16[256,1024]{1,0:T(8,128)(2,1)}, u32[]{:S(2)}, u32[]{:S(2)}) %collective-permute-start.4) | collective-permute-done | bytes 524320 | tf_op jit(solution)/shard_map/ppermute | solution.py:36
  36.3 7.1 %conv.1 = (bf16[4,32,1024]{2,1,0:T(8,128)(2,1)}, bf16[4,32,1024]{2,1,0:T(8,128)(2,1)}) custom-call(s32[1]{0:T(128)} %bitcast.9.core_ref, bf16[512,256]{1,0:T(8,128)(2,1)} %constant.42.clone.table_ref, bf16[256,512]{1,0:T(8,128)(2,1)} %constant.43.clone.back_ref, f32[1,1024]{1,0:T(1,128)} %bitcast.11, bf16[256,1024]{1,0:T(8,128)(2,1)} %gates_ref.1, ...), custom_call_target="tpu_custom_call" | custom-call | flops 4026531840 | bytes 6291456 | tf_op jit(solution)/shard_map/conv/pallas_call | solution.py:108
  43.4 2.9 %collective-permute-done.6.refs_1_ = bf16[256,2048]{1,0:T(8,128)(2,1)S(1)} collective-permute-done((bf16[256,2048]{1,0:T(8,128)(2,1)S(1)}, bf16[256,2048]{1,0:T(8,128)(2,1)S(1)}, u32[]{:S(2)}, u32[]{:S(2)}) %collective-permute-start.6) | collective-permute-done | bytes 1048608 | tf_op jit(solution)/shard_map/ppermute | solution.py:36
  50.7 3.4 %all-to-all-start.1 = ((bf16[4,32,1024]{2,1,0:T(8,128)(2,1)}), bf16[4,32,1024]{2,1,0:T(8,128)(2,1)S(1)}, u32[]{:S(2)}, u32[]{:S(2)}) async-start(bf16[4,32,1024]{2,1,0:T(8,128)(2,1)} %get-tuple-element.40), calls=%async_computation.1 | async-start | bytes 524288 | tf_op jit(solution)/shard_map/all_to_all | solution.py:320
  54.2 5.7 %all-to-all-done.1.refs_0_ = bf16[4,32,1024]{2,1,0:T(8,128)(2,1)S(1)} async-done(((bf16[4,32,1024]{2,1,0:T(8,128)(2,1)}), bf16[4,32,1024]{2,1,0:T(8,128)(2,1)S(1)}, u32[]{:S(2)}, u32[]{:S(2)}) %all-to-all-start.1) | async-done | bytes 262176 | tf_op jit(solution)/shard_map/all_to_all | solution.py:320
  61.2 2.5 %collective-permute-start.20 = (bf16[32,1024]{1,0:T(8,128)(2,1)}, bf16[32,1024]{1,0:T(8,128)(2,1)S(1)}, u32[]{:S(2)}, u32[]{:S(2)}) collective-permute-start(bf16[32,1024]{1,0:T(8,128)(2,1)} %get-tuple-element.41), channel_id=1, source_target_pairs={{0,24},{1,25},{2,26},{3,27},{4,28},{5,29},{6,30},{7,31},{8,16},{9,... | collective-permute-start | bytes 196616 | tf_op jit(solution)/shard_map/ppermute | solution.py:36
  65.6 3.4 %all-to-all-start = ((bf16[4,32,1024]{2,1,0:T(8,128)(2,1)}), bf16[4,32,1024]{2,1,0:T(8,128)(2,1)S(1)}, u32[]{:S(2)}, u32[]{:S(2)}) async-start(bf16[4,32,1024]{2,1,0:T(8,128)(2,1)} %get-tuple-element.27.refs_4_), calls=%async_computation | async-start | bytes 524288 | tf_op jit(solution)/shard_map/all_to_all | solution.py:320
  69.3 3.3 %project.7 = (bf16[64,2048]{1,0:T(8,128)(2,1)}, f32[64,2048]{1,0:T(8,128)S(1)}) custom-call(bf16[32,1024]{1,0:T(8,128)(2,1)S(1)} %collective-permute-done.20.refs_0_, bf16[32,1024]{1,0:T(8,128)(2,1)} %collective-permute-done.21.refs_1_, bf16[32,1024]{1,0:T(8,128)(2,1)} %collective-permute-done.22.refs_2_, bf16[32,1024]{1,0:T(8,128)(2,1)S(1)} %get-tuple-element.44.refs_3_, ...), custom_call_target="tpu_custom_call" | custom-call | flops 536870912 | bytes 5767168 | tf_op jit(solution)/shard_map/project/pallas_call | solution.py:254
  78.2 2.2 %collective-permute-start.15 = (bf16[32,1024]{1,0:T(8,128)(2,1)S(1)}, bf16[32,1024]{1,0:T(8,128)(2,1)S(1)}, u32[]{:S(2)}, u32[]{:S(2)}) collective-permute-start(bf16[32,1024]{1,0:T(8,128)(2,1)S(1)} %get-tuple-element.34), channel_id=1, source_target_pairs={{0,16},{1,17},{2,18},{3,19},{4,20},{5,21},{6,22},{7,23},{8,24},{9,... | collective-permute-start | bytes 196616 | tf_op jit(solution)/shard_map/ppermute | solution.py:36
  80.4 2.0 %project.6 = (bf16[64,2048]{1,0:T(8,128)(2,1)S(1)}, f32[64,2048]{1,0:T(8,128)S(1)}) custom-call(bf16[32,1024]{1,0:T(8,128)(2,1)S(1)} %collective-permute-done.20.refs_0_, bf16[32,1024]{1,0:T(8,128)(2,1)} %collective-permute-done.21.refs_1_, bf16[32,1024]{1,0:T(8,128)(2,1)} %collective-permute-done.22.refs_2_, ...), custom_call_target="tpu_custom_call" | custom-call | flops 536870912 | bytes 5767168 | tf_op jit(solution)/shard_map/project/pallas_call | solution.py:254
  82.5 3.0 %collective-permute-done.13.refs_0_ = bf16[32,1024]{1,0:T(8,128)(2,1)S(1)} collective-permute-done((bf16[32,1024]{1,0:T(8,128)(2,1)S(1)}, bf16[32,1024]{1,0:T(8,128)(2,1)S(1)}, u32[]{:S(2)}, u32[]{:S(2)}) %collective-permute-start.13) | collective-permute-done | bytes 65568 | tf_op jit(solution)/shard_map/ppermute | solution.py:36
  86.2 2.6 %project.5 = (bf16[64,2048]{1,0:T(8,128)(2,1)S(1)}, f32[64,2048]{1,0:T(8,128)S(1)}) custom-call(bf16[32,1024]{1,0:T(8,128)(2,1)S(1)} %collective-permute-done.13.refs_0_, bf16[32,1024]{1,0:T(8,128)(2,1)S(1)} %collective-permute-done.14.refs_1_, bf16[32,1024]{1,0:T(8,128)(2,1)S(1)} %collective-permute-done.15.refs_2_, ...), custom_call_target="tpu_custom_call" | custom-call | flops 536870912 | bytes 5767168 | tf_op jit(solution)/shard_map/project/pallas_call | solution.py:254
  88.8 2.8 %collective-permute-start.18 = (bf16[64,2048]{1,0:T(8,128)(2,1)S(1)}, bf16[64,2048]{1,0:T(8,128)(2,1)S(1)}, u32[]{:S(2)}, u32[]{:S(2)}) collective-permute-start(bf16[64,2048]{1,0:T(8,128)(2,1)S(1)} %get-tuple-element.39), channel_id=1, source_target_pairs={{0,8},{1,9},{2,10},{3,11},{4,12},{5,13},{6,14},{7,15},{8,0},{9,1},... | collective-permute-start | bytes 786440 | tf_op jit(solution)/shard_map/ppermute | solution.py:36
  91.6 1.9 %project.4 = (bf16[64,2048]{1,0:T(8,128)(2,1)S(1)}, f32[64,2048]{1,0:T(8,128)S(1)}) custom-call(bf16[32,1024]{1,0:T(8,128)(2,1)S(1)} %collective-permute-done.13.refs_0_, bf16[32,1024]{1,0:T(8,128)(2,1)S(1)} %collective-permute-done.14.refs_1_, bf16[32,1024]{1,0:T(8,128)(2,1)S(1)} %collective-permute-done.15.refs_2_, ...), custom_call_target="tpu_custom_call" | custom-call | flops 536870912 | bytes 5767168 | tf_op jit(solution)/shard_map/project/pallas_call | solution.py:254
  94.7 2.7 %collective-permute-start.26 = (bf16[32,2048]{1,0:T(8,128)(2,1)S(1)}, bf16[32,2048]{1,0:T(8,128)(2,1)S(1)}, u32[]{:S(2)}, u32[]{:S(2)}) collective-permute-start(bf16[32,2048]{1,0:T(8,128)(2,1)S(1)} %fusion), channel_id=1, source_target_pairs={{0,16},{1,17},{2,18},{3,19},{4,20},{5,21},{6,22},{7,23},{8,24},{9,... | collective-permute-start | bytes 393224 | tf_op jit(solution)/shard_map/ppermute | solution.py:36
  97.9 5.9 %collective-permute-done.18 = bf16[64,2048]{1,0:T(8,128)(2,1)S(1)} collective-permute-done((bf16[64,2048]{1,0:T(8,128)(2,1)S(1)}, bf16[64,2048]{1,0:T(8,128)(2,1)S(1)}, u32[]{:S(2)}, u32[]{:S(2)}) %collective-permute-start.18) | collective-permute-done | bytes 262176 | tf_op jit(solution)/shard_map/ppermute | solution.py:36
  104.0 4.1 %collective-permute-done.16 = bf16[64,2048]{1,0:T(8,128)(2,1)S(1)} collective-permute-done((bf16[64,2048]{1,0:T(8,128)(2,1)S(1)}, bf16[64,2048]{1,0:T(8,128)(2,1)S(1)}, u32[]{:S(2)}, u32[]{:S(2)}) %collective-permute-start.16) | collective-permute-done | bytes 262176 | tf_op jit(solution)/shard_map/ppermute | solution.py:36
  108.7 5.3 %collective-permute-done.24 = bf16[32,2048]{1,0:T(8,128)(2,1)S(1)} collective-permute-done((bf16[32,2048]{1,0:T(8,128)(2,1)S(1)}, bf16[32,2048]{1,0:T(8,128)(2,1)S(1)}, u32[]{:S(2)}, u32[]{:S(2)}) %collective-permute-start.24) | collective-permute-done | bytes 131104 | tf_op jit(solution)/shard_map/ppermute | solution.py:36
  114.0 2.7 %collective-permute-done.19 = bf16[32,2048]{1,0:T(8,128)(2,1)S(1)} collective-permute-done((bf16[32,2048]{1,0:T(8,128)(2,1)S(1)}, bf16[32,2048]{1,0:T(8,128)(2,1)S(1)}, u32[]{:S(2)}, u32[]{:S(2)}) %collective-permute-start.19) | collective-permute-done | bytes 131104 | tf_op jit(solution)/shard_map/ppermute | solution.py:36
  (76 shorter events, 27.9 us)
Async XLA Ops:
  2.4 15.3 %collective-permute-start = (bf16[256,1024]{1,0:T(8,128)(2,1)}, bf16[256,1024]{1,0:T(8,128)(2,1)}, u32[]{:S(2)}, u32[]{:S(2)}) collective-permute-start(bf16[256,1024]{1,0:T(8,128)(2,1)} %rest_0_.1), channel_id=1, source_target_pairs={{0,8},{1,9},{2,10},{3,11},{4,12},{5,13},{6,14},{7,15},{8,16},{9,17... | collective-permute-start | bytes 1572872 | tf_op jit(solution)/shard_map/ppermute | solution.py:36
  8.8 14.2 %collective-permute-start.5 = (bf16[128,2048]{1,0:T(8,128)(2,1)S(1)}, bf16[128,2048]{1,0:T(8,128)(2,1)S(1)}, u32[]{:S(2)}, u32[]{:S(2)}) collective-permute-start(bf16[128,2048]{1,0:T(8,128)(2,1)S(1)} %join.4.refs_0_), channel_id=1, source_target_pairs={{0,1},{1,0},{2,3},{3,2},{4,5},{5,4},{6,7},{7,6},{8,9},{9,8},{10,11... | collective-permute-start | bytes 1572872 | tf_op jit(solution)/shard_map/ppermute | solution.py:36
  10.4 14.2 %collective-permute-start.7 = (bf16[128,2048]{1,0:T(8,128)(2,1)S(1)}, bf16[128,2048]{1,0:T(8,128)(2,1)S(1)}, u32[]{:S(2)}, u32[]{:S(2)}) collective-permute-start(bf16[128,2048]{1,0:T(8,128)(2,1)S(1)} %join.6.refs_0_), channel_id=1, source_target_pairs={{0,2},{1,3},{2,0},{3,1},{4,6},{5,7},{6,4},{7,5},{8,10},{9,11},{10,... | collective-permute-start | bytes 1572872 | tf_op jit(solution)/shard_map/ppermute | solution.py:36
  17.7 14.5 %collective-permute-start.1 = (bf16[256,1024]{1,0:T(8,128)(2,1)}, bf16[256,1024]{1,0:T(8,128)(2,1)}, u32[]{:S(2)}, u32[]{:S(2)}) collective-permute-start(bf16[256,1024]{1,0:T(8,128)(2,1)} %collective-permute-done.rest_1_), channel_id=1, source_target_pairs={{0,8},{1,9},{2,10},{3,11},{4,12},{5,13},{6,14},{7,15},{8,16},{9,17... | collective-permute-start | bytes 1572872 | tf_op jit(solution)/shard_map/ppermute | solution.py:36
  23.0 23.3 %collective-permute-start.6 = (bf16[256,2048]{1,0:T(8,128)(2,1)S(1)}, bf16[256,2048]{1,0:T(8,128)(2,1)S(1)}, u32[]{:S(2)}, u32[]{:S(2)}) collective-permute-start(bf16[256,2048]{1,0:T(8,128)(2,1)S(1)} %join.5.refs_0_), channel_id=1, source_target_pairs={{0,2},{1,3},{2,0},{3,1},{4,6},{5,7},{6,4},{7,5},{8,10},{9,11},{10,... | collective-permute-start | bytes 3145736 | tf_op jit(solution)/shard_map/ppermute | solution.py:36
  24.7 23.1 %collective-permute-start.8 = (bf16[256,2048]{1,0:T(8,128)(2,1)S(1)}, bf16[256,2048]{1,0:T(8,128)(2,1)}, u32[]{:S(2)}, u32[]{:S(2)}) collective-permute-start(bf16[256,2048]{1,0:T(8,128)(2,1)S(1)} %join.7.refs_2_), channel_id=1, source_target_pairs={{0,1},{1,0},{2,3},{3,2},{4,5},{5,4},{6,7},{7,6},{8,9},{9,8},{10,11... | collective-permute-start | bytes 3145736 | tf_op jit(solution)/shard_map/ppermute | solution.py:36
  49.7 10.2 %collective-permute-start.9 = (bf16[256,2048]{1,0:T(8,128)(2,1)S(1)}, bf16[256,2048]{1,0:T(8,128)(2,1)S(1)}, u32[]{:S(2)}, u32[]{:S(2)}) collective-permute-start(bf16[256,2048]{1,0:T(8,128)(2,1)S(1)} %get-tuple-element.28.refs_4_), channel_id=1, source_target_pairs={{0,4},{1,5},{2,6},{3,7},{4,0},{5,1},{6,2},{7,3},{8,12},{9,13},{10,... | collective-permute-start | bytes 3145736 | tf_op jit(solution)/shard_map/ppermute | solution.py:36
  49.7 10.2 %collective-permute-start.10 = (bf16[256,2048]{1,0:T(8,128)(2,1)}, bf16[256,2048]{1,0:T(8,128)(2,1)}, u32[]{:S(2)}, u32[]{:S(2)}) collective-permute-start(bf16[256,2048]{1,0:T(8,128)(2,1)} %copy-done), channel_id=1, source_target_pairs={{0,4},{1,5},{2,6},{3,7},{4,0},{5,1},{6,2},{7,3},{8,12},{9,13},{10,... | collective-permute-start | bytes 3145736 | tf_op jit(solution)/shard_map/ppermute | solution.py:36
  50.2 9.7 %collective-permute-start.11 = (bf16[256,2048]{1,0:T(8,128)(2,1)S(1)}, bf16[256,2048]{1,0:T(8,128)(2,1)}, u32[]{:S(2)}, u32[]{:S(2)}) collective-permute-start(bf16[256,2048]{1,0:T(8,128)(2,1)S(1)} %get-tuple-element.30.refs_4_), channel_id=1, source_target_pairs={{0,4},{1,5},{2,6},{3,7},{4,0},{5,1},{6,2},{7,3},{8,12},{9,13},{10,... | collective-permute-start | bytes 3145736 | tf_op jit(solution)/shard_map/ppermute | solution.py:36
  50.2 9.7 %collective-permute-start.12 = (bf16[256,2048]{1,0:T(8,128)(2,1)}, bf16[256,2048]{1,0:T(8,128)(2,1)}, u32[]{:S(2)}, u32[]{:S(2)}) collective-permute-start(bf16[256,2048]{1,0:T(8,128)(2,1)} %get-tuple-element.31.refs_5_), channel_id=1, source_target_pairs={{0,4},{1,5},{2,6},{3,7},{4,0},{5,1},{6,2},{7,3},{8,12},{9,13},{10,... | collective-permute-start | bytes 3145736 | tf_op jit(solution)/shard_map/ppermute | solution.py:36
  50.7 9.2 %all-to-all-start.1 = ((bf16[4,32,1024]{2,1,0:T(8,128)(2,1)}), bf16[4,32,1024]{2,1,0:T(8,128)(2,1)S(1)}, u32[]{:S(2)}, u32[]{:S(2)}) async-start(bf16[4,32,1024]{2,1,0:T(8,128)(2,1)} %get-tuple-element.40), calls=%async_computation.1 | async-start | bytes 524288 | tf_op jit(solution)/shard_map/all_to_all | solution.py:320
  61.2 7.8 %collective-permute-start.20 = (bf16[32,1024]{1,0:T(8,128)(2,1)}, bf16[32,1024]{1,0:T(8,128)(2,1)S(1)}, u32[]{:S(2)}, u32[]{:S(2)}) collective-permute-start(bf16[32,1024]{1,0:T(8,128)(2,1)} %get-tuple-element.41), channel_id=1, source_target_pairs={{0,24},{1,25},{2,26},{3,27},{4,28},{5,29},{6,30},{7,31},{8,16},{9,... | collective-permute-start | bytes 196616 | tf_op jit(solution)/shard_map/ppermute | solution.py:36
  65.6 9.8 %all-to-all-start = ((bf16[4,32,1024]{2,1,0:T(8,128)(2,1)}), bf16[4,32,1024]{2,1,0:T(8,128)(2,1)S(1)}, u32[]{:S(2)}, u32[]{:S(2)}) async-start(bf16[4,32,1024]{2,1,0:T(8,128)(2,1)} %get-tuple-element.27.refs_4_), calls=%async_computation | async-start | bytes 524288 | tf_op jit(solution)/shard_map/all_to_all | solution.py:320
  73.4 20.3 %collective-permute-start.25 = (bf16[64,2048]{1,0:T(8,128)(2,1)}, bf16[64,2048]{1,0:T(8,128)(2,1)}, u32[]{:S(2)}, u32[]{:S(2)}) collective-permute-start(bf16[64,2048]{1,0:T(8,128)(2,1)} %get-tuple-element.48), channel_id=1, source_target_pairs={{0,8},{1,9},{2,10},{3,11},{4,12},{5,13},{6,14},{7,15},{8,0},{9,1},... | collective-permute-start | bytes 786440 | tf_op jit(solution)/shard_map/ppermute | solution.py:36
  76.0 9.6 %collective-permute-start.13 = (bf16[32,1024]{1,0:T(8,128)(2,1)S(1)}, bf16[32,1024]{1,0:T(8,128)(2,1)S(1)}, u32[]{:S(2)}, u32[]{:S(2)}) collective-permute-start(bf16[32,1024]{1,0:T(8,128)(2,1)S(1)} %get-tuple-element.32), channel_id=1, source_target_pairs={{0,24},{1,25},{2,26},{3,27},{4,28},{5,29},{6,30},{7,31},{8,16},{9,... | collective-permute-start | bytes 196616 | tf_op jit(solution)/shard_map/ppermute | solution.py:36
  77.6 8.0 %collective-permute-start.14 = (bf16[32,1024]{1,0:T(8,128)(2,1)S(1)}, bf16[32,1024]{1,0:T(8,128)(2,1)S(1)}, u32[]{:S(2)}, u32[]{:S(2)}) collective-permute-start(bf16[32,1024]{1,0:T(8,128)(2,1)S(1)} %get-tuple-element.33), channel_id=1, source_target_pairs={{0,8},{1,9},{2,10},{3,11},{4,12},{5,13},{6,14},{7,15},{8,0},{9,1},... | collective-permute-start | bytes 196616 | tf_op jit(solution)/shard_map/ppermute | solution.py:36
  78.2 8.0 %collective-permute-start.15 = (bf16[32,1024]{1,0:T(8,128)(2,1)S(1)}, bf16[32,1024]{1,0:T(8,128)(2,1)S(1)}, u32[]{:S(2)}, u32[]{:S(2)}) collective-permute-start(bf16[32,1024]{1,0:T(8,128)(2,1)S(1)} %get-tuple-element.34), channel_id=1, source_target_pairs={{0,16},{1,17},{2,18},{3,19},{4,20},{5,21},{6,22},{7,23},{8,24},{9,... | collective-permute-start | bytes 196616 | tf_op jit(solution)/shard_map/ppermute | solution.py:36
  82.5 14.9 %collective-permute-start.23 = (bf16[64,2048]{1,0:T(8,128)(2,1)S(1)}, bf16[64,2048]{1,0:T(8,128)(2,1)S(1)}, u32[]{:S(2)}, u32[]{:S(2)}) collective-permute-start(bf16[64,2048]{1,0:T(8,128)(2,1)S(1)} %get-tuple-element.46), channel_id=1, source_target_pairs={{0,8},{1,9},{2,10},{3,11},{4,12},{5,13},{6,14},{7,15},{8,0},{9,1},... | collective-permute-start | bytes 786440 | tf_op jit(solution)/shard_map/ppermute | solution.py:36
  88.8 15.0 %collective-permute-start.18 = (bf16[64,2048]{1,0:T(8,128)(2,1)S(1)}, bf16[64,2048]{1,0:T(8,128)(2,1)S(1)}, u32[]{:S(2)}, u32[]{:S(2)}) collective-permute-start(bf16[64,2048]{1,0:T(8,128)(2,1)S(1)} %get-tuple-element.39), channel_id=1, source_target_pairs={{0,8},{1,9},{2,10},{3,11},{4,12},{5,13},{6,14},{7,15},{8,0},{9,1},... | collective-permute-start | bytes 786440 | tf_op jit(solution)/shard_map/ppermute | solution.py:36
  93.6 14.5 %collective-permute-start.16 = (bf16[64,2048]{1,0:T(8,128)(2,1)S(1)}, bf16[64,2048]{1,0:T(8,128)(2,1)S(1)}, u32[]{:S(2)}, u32[]{:S(2)}) collective-permute-start(bf16[64,2048]{1,0:T(8,128)(2,1)S(1)} %get-tuple-element.37), channel_id=1, source_target_pairs={{0,8},{1,9},{2,10},{3,11},{4,12},{5,13},{6,14},{7,15},{8,0},{9,1},... | collective-permute-start | bytes 786440 | tf_op jit(solution)/shard_map/ppermute | solution.py:36
  94.7 13.9 %collective-permute-start.26 = (bf16[32,2048]{1,0:T(8,128)(2,1)S(1)}, bf16[32,2048]{1,0:T(8,128)(2,1)S(1)}, u32[]{:S(2)}, u32[]{:S(2)}) collective-permute-start(bf16[32,2048]{1,0:T(8,128)(2,1)S(1)} %fusion), channel_id=1, source_target_pairs={{0,16},{1,17},{2,18},{3,19},{4,20},{5,21},{6,22},{7,23},{8,24},{9,... | collective-permute-start | bytes 393224 | tf_op jit(solution)/shard_map/ppermute | solution.py:36
  97.5 16.5 %collective-permute-start.24 = (bf16[32,2048]{1,0:T(8,128)(2,1)S(1)}, bf16[32,2048]{1,0:T(8,128)(2,1)S(1)}, u32[]{:S(2)}, u32[]{:S(2)}) collective-permute-start(bf16[32,2048]{1,0:T(8,128)(2,1)S(1)} %fusion.3), channel_id=1, source_target_pairs={{0,16},{1,17},{2,18},{3,19},{4,20},{5,21},{6,22},{7,23},{8,24},{9,... | collective-permute-start | bytes 393224 | tf_op jit(solution)/shard_map/ppermute | solution.py:36
  103.9 12.8 %collective-permute-start.19 = (bf16[32,2048]{1,0:T(8,128)(2,1)S(1)}, bf16[32,2048]{1,0:T(8,128)(2,1)S(1)}, u32[]{:S(2)}, u32[]{:S(2)}) collective-permute-start(bf16[32,2048]{1,0:T(8,128)(2,1)S(1)} %fusion.6), channel_id=1, source_target_pairs={{0,16},{1,17},{2,18},{3,19},{4,20},{5,21},{6,22},{7,23},{8,24},{9,... | collective-permute-start | bytes 393224 | tf_op jit(solution)/shard_map/ppermute | solution.py:36
  108.2 10.0 %collective-permute-start.17 = (bf16[32,2048]{1,0:T(8,128)(2,1)S(1)}, bf16[32,2048]{1,0:T(8,128)(2,1)S(1)}, u32[]{:S(2)}, u32[]{:S(2)}) collective-permute-start(bf16[32,2048]{1,0:T(8,128)(2,1)S(1)} %fusion.9), channel_id=1, source_target_pairs={{0,16},{1,17},{2,18},{3,19},{4,20},{5,21},{6,22},{7,23},{8,24},{9,... | collective-permute-start | bytes 393224 | tf_op jit(solution)/shard_map/ppermute | solution.py:36
  (12 other events, 46.3 us)

commit v4 on v3

--- a/solution.py
+++ b/solution.py
@@ -225,7 +225,7 @@
 
 
 def project_kernel(count, firsts, tile, spots, width, *refs):
-    act_refs, piece_refs = refs[:count], refs[count:-2]
+    act_refs, piece_refs = refs[:count], refs[count : count + len(firsts)]
     send_ref, keep_ref = refs[-2:]
     rows, cols = send_ref.shape
     acts = jnp.concatenate([act[...] for act in act_refs], axis=0)
@@ -245,7 +245,7 @@
         keep_ref[:, start : start + tile] = total[rows:]
 
 
-def project(acts, pieces, spots, width, cols):
+def project(acts, pieces, spots, width, cols, deps):
     rows, depth = acts[0].shape
     count = rows * len(acts)
     tile = min(cols, 512)
@@ -253,7 +253,8 @@
     held = pl.BlockSpec(memory_space=pltpu.VMEM)
     return pl.pallas_call(
         functools.partial(project_kernel, len(acts), firsts, tile, spots, width),
-        in_specs=[held] * (len(acts) + len(pieces)),
+        in_specs=[held] * (len(acts) + len(pieces))
+        + [pl.BlockSpec(memory_space=pl.ANY)] * len(deps),
         out_specs=[held] * 2,
         out_shape=[
             jax.ShapeDtypeStruct((count // 2, cols), BF16),
@@ -266,7 +267,7 @@
             transcendentals=0,
         ),
         name="project",
-    )(*acts, *[piece for piece, _ in pieces])
+    )(*acts, *[piece for piece, _ in pieces], *deps)
 
 
 def body(values, gates, filters, skip, out_weight):
@@ -338,21 +339,29 @@
     acts = [[some[rank] for rank in ranks] for some in acts]
 
     outs = []
+    passed = []
     for some in acts:
-        row = []
+        row, sent = [], []
         for which in range(2):
             send, keep = project(
-                some, [(piece, 0) for piece in parts[which]], spots[which], own_rows, half
+                some,
+                [(piece, 0) for piece in parts[which]],
+                spots[which],
+                own_rows,
+                half,
+                passed[:1] if which == 0 else [],
             )
             for index, step in enumerate(steps):
                 got = permute(send, lambda p, k, c, step=step: (p ^ step, k, c)).astype(F32)
                 many = got.shape[0] // 2
                 if index + 1 < count:
                     send = (keep[:many] + got[:many]).astype(BF16)
+                    sent.append(send)
                     keep = keep[many:] + got[many:]
                 else:
                     keep = keep + got
             row.append(keep.astype(BF16))
+        passed = sent
         outs.append(jnp.concatenate(row, axis=1))
     return jnp.concatenate(outs, axis=0)
 

time: 120 us -> 119 us (level)
  waiting for transfers between devices: 48 us -> 42.7 us
  starting transfers between devices: 45.4 us -> 49.8 us
    ppermute x27, waiting for transfers between devices: 42.3 us -> 37.1 us  [permute(): return lax.ppermute(value, AXES, route)]
    ppermute x27, starting transfers between devices: 38.6 us -> 43 us  [permute(): return lax.ppermute(value, AXES, route)]
where the time goes in v4:
time: 119 us; the launch traced here: 118 us
  starting transfers between devices  49.8 us (42%)
  waiting for transfers between devices  42.7 us (36%)
  Pallas kernels  19.1 us (16%)
  local copies, waits for them, and re-layouts  4.04 us (3%)
  other arithmetic  2.18 us (2%)
    ppermute x27, starting transfers between devices, permute(): return lax.ppermute(value, AXES, route)  43 us
    ppermute x27, waiting for transfers between devices, permute(): return lax.ppermute(value, AXES, route)  37.1 us
    pallas_call x4, Pallas kernels, project(): pl.pallas_call(functools.partial(project_kernel, len(acts), firsts, tile,...  9.92 us
    pallas_call x1, Pallas kernels, convolve(): pl.pallas_call(functools.partial(conv_kernel, lags), grid_spec=pltpu.Pref...  7.13 us
    all_to_all x2, starting transfers between devices, body(): lax.all_to_all(some, 'chan', split_axis=0, concat_axis=0)  6.81 us
    all_to_all x2, waiting for transfers between devices, body(): lax.all_to_all(some, 'chan', split_axis=0, concat_axis=0)  5.66 us
    unnamed x14, local copies, waits for them, and re-layouts  3.95 us
  transfers between devices with their start and end apart: 29, of which 14 were waited for; matrix products, arithmetic and copies ran while one was open for 1% of the time, Pallas kernels for 15%

profile of v4, /device:TPU:0, one launch (start us, length us, event | category | flops | bytes accessed | tf_op | source)
XLA Modules:
  0.0 118.2 jit_solution(7242310476430780255)
XLA Ops:
  0.0 2.4 %collective-permute-start.2 = (bf16[256,1024]{1,0:T(8,128)(2,1)}, bf16[256,1024]{1,0:T(8,128)(2,1)S(1)}, u32[]{:S(2)}, u32[]{:S(2)}) collective-permute-start(bf16[256,1024]{1,0:T(8,128)(2,1)} %rest_0_.1), channel_id=1, source_target_pairs={{0,4},{1,5},{2,6},{3,7},{8,12},{9,13},{10,14},{11,15},{16,20},{17,... | collective-permute-start | bytes 1572872 | tf_op jit(solution)/shard_map/ppermute | solution.py:36
  2.4 5.1 %collective-permute-start = (bf16[256,1024]{1,0:T(8,128)(2,1)}, bf16[256,1024]{1,0:T(8,128)(2,1)}, u32[]{:S(2)}, u32[]{:S(2)}) collective-permute-start(bf16[256,1024]{1,0:T(8,128)(2,1)} %rest_0_.1), channel_id=1, source_target_pairs={{0,8},{1,9},{2,10},{3,11},{4,12},{5,13},{6,14},{7,15},{8,16},{9,17... | collective-permute-start | bytes 1572872 | tf_op jit(solution)/shard_map/ppermute | solution.py:36
  12.0 5.7 %collective-permute-done.rest_1_ = bf16[256,1024]{1,0:T(8,128)(2,1)} collective-permute-done((bf16[256,1024]{1,0:T(8,128)(2,1)}, bf16[256,1024]{1,0:T(8,128)(2,1)}, u32[]{:S(2)}, u32[]{:S(2)}) %collective-permute-start) | collective-permute-done | bytes 524320 | tf_op jit(solution)/shard_map/ppermute | solution.py:36
  17.7 5.2 %collective-permute-start.1 = (bf16[256,1024]{1,0:T(8,128)(2,1)}, bf16[256,1024]{1,0:T(8,128)(2,1)}, u32[]{:S(2)}, u32[]{:S(2)}) collective-permute-start(bf16[256,1024]{1,0:T(8,128)(2,1)} %collective-permute-done.rest_1_), channel_id=1, source_target_pairs={{0,8},{1,9},{2,10},{3,11},{4,12},{5,13},{6,14},{7,15},{8,16},{9,17... | collective-permute-start | bytes 1572872 | tf_op jit(solution)/shard_map/ppermute | solution.py:36
  26.2 5.9 %collective-permute-done.1.rest_2_ = bf16[256,1024]{1,0:T(8,128)(2,1)} collective-permute-done((bf16[256,1024]{1,0:T(8,128)(2,1)}, bf16[256,1024]{1,0:T(8,128)(2,1)}, u32[]{:S(2)}, u32[]{:S(2)}) %collective-permute-start.1) | collective-permute-done | bytes 524320 | tf_op jit(solution)/shard_map/ppermute | solution.py:36
  33.5 2.8 %collective-permute-done.4.rest_5_ = bf16[256,1024]{1,0:T(8,128)(2,1)} collective-permute-done((bf16[256,1024]{1,0:T(8,128)(2,1)}, bf16[256,1024]{1,0:T(8,128)(2,1)}, u32[]{:S(2)}, u32[]{:S(2)}) %collective-permute-start.4) | collective-permute-done | bytes 524320 | tf_op jit(solution)/shard_map/ppermute | solution.py:36
  36.3 7.1 %conv.1 = (bf16[4,32,1024]{2,1,0:T(8,128)(2,1)}, bf16[4,32,1024]{2,1,0:T(8,128)(2,1)}) custom-call(s32[1]{0:T(128)} %bitcast.9.core_ref, bf16[512,256]{1,0:T(8,128)(2,1)} %constant.42.clone.table_ref, bf16[256,512]{1,0:T(8,128)(2,1)} %constant.43.clone.back_ref, f32[1,1024]{1,0:T(1,128)} %bitcast.11, bf16[256,1024]{1,0:T(8,128)(2,1)} %gates_ref.1, ...), custom_call_target="tpu_custom_call" | custom-call | flops 4026531840 | bytes 6291456 | tf_op jit(solution)/shard_map/conv/pallas_call | solution.py:108
  43.4 2.9 %collective-permute-done.6.refs_1_ = bf16[256,2048]{1,0:T(8,128)(2,1)} collective-permute-done((bf16[256,2048]{1,0:T(8,128)(2,1)S(1)}, bf16[256,2048]{1,0:T(8,128)(2,1)}, u32[]{:S(2)}, u32[]{:S(2)}) %collective-permute-start.6) | collective-permute-done | bytes 1048608 | tf_op jit(solution)/shard_map/ppermute | solution.py:36
  50.6 3.4 %all-to-all-start = ((bf16[4,32,1024]{2,1,0:T(8,128)(2,1)}), bf16[4,32,1024]{2,1,0:T(8,128)(2,1)S(1)}, u32[]{:S(2)}, u32[]{:S(2)}) async-start(bf16[4,32,1024]{2,1,0:T(8,128)(2,1)} %get-tuple-element.27.refs_4_), calls=%async_computation | async-start | bytes 524288 | tf_op jit(solution)/shard_map/all_to_all | solution.py:321
  54.1 5.7 %all-to-all-done.refs_0_ = bf16[4,32,1024]{2,1,0:T(8,128)(2,1)S(1)} async-done(((bf16[4,32,1024]{2,1,0:T(8,128)(2,1)}), bf16[4,32,1024]{2,1,0:T(8,128)(2,1)S(1)}, u32[]{:S(2)}, u32[]{:S(2)}) %all-to-all-start) | async-done | bytes 262176 | tf_op jit(solution)/shard_map/all_to_all | solution.py:321
  61.1 2.5 %collective-permute-start.13 = (bf16[32,1024]{1,0:T(8,128)(2,1)}, bf16[32,1024]{1,0:T(8,128)(2,1)S(1)}, u32[]{:S(2)}, u32[]{:S(2)}) collective-permute-start(bf16[32,1024]{1,0:T(8,128)(2,1)} %get-tuple-element.32), channel_id=1, source_target_pairs={{0,24},{1,25},{2,26},{3,27},{4,28},{5,29},{6,30},{7,31},{8,16},{9,... | collective-permute-start | bytes 196616 | tf_op jit(solution)/shard_map/ppermute | solution.py:36
  65.5 3.4 %all-to-all-start.1 = ((bf16[4,32,1024]{2,1,0:T(8,128)(2,1)}), bf16[4,32,1024]{2,1,0:T(8,128)(2,1)S(1)}, u32[]{:S(2)}, u32[]{:S(2)}) async-start(bf16[4,32,1024]{2,1,0:T(8,128)(2,1)} %get-tuple-element.40), calls=%async_computation.1 | async-start | bytes 524288 | tf_op jit(solution)/shard_map/all_to_all | solution.py:321
  69.2 3.3 %project.4 = (bf16[64,2048]{1,0:T(8,128)(2,1)}, f32[64,2048]{1,0:T(8,128)S(1)}) custom-call(bf16[32,1024]{1,0:T(8,128)(2,1)S(1)} %collective-permute-done.13.refs_0_, bf16[32,1024]{1,0:T(8,128)(2,1)} %collective-permute-done.14.refs_1_, bf16[32,1024]{1,0:T(8,128)(2,1)} %collective-permute-done.15.refs_2_, bf16[32,1024]{1,0:T(8,128)(2,1)S(1)} %get-tuple-element.35.refs_3_, ...), custom_call_target="tpu_custom_call" | custom-call | flops 536870912 | bytes 5767168 | tf_op jit(solution)/shard_map/project/pallas_call | solution.py:254
  78.1 2.2 %collective-permute-start.22 = (bf16[32,1024]{1,0:T(8,128)(2,1)S(1)}, bf16[32,1024]{1,0:T(8,128)(2,1)S(1)}, u32[]{:S(2)}, u32[]{:S(2)}) collective-permute-start(bf16[32,1024]{1,0:T(8,128)(2,1)S(1)} %get-tuple-element.43), channel_id=1, source_target_pairs={{0,16},{1,17},{2,18},{3,19},{4,20},{5,21},{6,22},{7,23},{8,24},{9,... | collective-permute-start | bytes 196616 | tf_op jit(solution)/shard_map/ppermute | solution.py:36
  80.3 2.0 %project.5 = (bf16[64,2048]{1,0:T(8,128)(2,1)S(1)}, f32[64,2048]{1,0:T(8,128)S(1)}) custom-call(bf16[32,1024]{1,0:T(8,128)(2,1)S(1)} %collective-permute-done.13.refs_0_, bf16[32,1024]{1,0:T(8,128)(2,1)} %collective-permute-done.14.refs_1_, bf16[32,1024]{1,0:T(8,128)(2,1)} %collective-permute-done.15.refs_2_, ...), custom_call_target="tpu_custom_call" | custom-call | flops 536870912 | bytes 5767168 | tf_op jit(solution)/shard_map/project/pallas_call | solution.py:254
  82.4 3.1 %collective-permute-done.20.refs_0_ = bf16[32,1024]{1,0:T(8,128)(2,1)S(1)} collective-permute-done((bf16[32,1024]{1,0:T(8,128)(2,1)S(1)}, bf16[32,1024]{1,0:T(8,128)(2,1)S(1)}, u32[]{:S(2)}, u32[]{:S(2)}) %collective-permute-start.20) | collective-permute-done | bytes 65568 | tf_op jit(solution)/shard_map/ppermute | solution.py:36
  88.4 2.5 %collective-permute-start.25 = (bf16[64,2048]{1,0:T(8,128)(2,1)S(1)}, bf16[64,2048]{1,0:T(8,128)(2,1)S(1)}, u32[]{:S(2)}, u32[]{:S(2)}) collective-permute-start(bf16[64,2048]{1,0:T(8,128)(2,1)S(1)} %get-tuple-element.48), channel_id=1, source_target_pairs={{0,8},{1,9},{2,10},{3,11},{4,12},{5,13},{6,14},{7,15},{8,0},{9,1},... | collective-permute-start | bytes 786440 | tf_op jit(solution)/shard_map/ppermute | solution.py:36
  96.2 2.6 %project.6 = (bf16[64,2048]{1,0:T(8,128)(2,1)S(1)}, f32[64,2048]{1,0:T(8,128)S(1)}) custom-call(bf16[32,1024]{1,0:T(8,128)(2,1)S(1)} %collective-permute-done.20.refs_0_, bf16[32,1024]{1,0:T(8,128)(2,1)S(1)} %collective-permute-done.21.refs_1_, bf16[32,1024]{1,0:T(8,128)(2,1)S(1)} %collective-permute-done.22.refs_2_, ...), custom_call_target="tpu_custom_call" | custom-call | flops 536870912 | bytes 5767168 | tf_op jit(solution)/shard_map/project/pallas_call | solution.py:254
  98.8 2.5 %collective-permute-start.23 = (bf16[64,2048]{1,0:T(8,128)(2,1)S(1)}, bf16[64,2048]{1,0:T(8,128)(2,1)S(1)}, u32[]{:S(2)}, u32[]{:S(2)}) collective-permute-start(bf16[64,2048]{1,0:T(8,128)(2,1)S(1)} %get-tuple-element.46), channel_id=1, source_target_pairs={{0,8},{1,9},{2,10},{3,11},{4,12},{5,13},{6,14},{7,15},{8,0},{9,1},... | collective-permute-start | bytes 786440 | tf_op jit(solution)/shard_map/ppermute | solution.py:36
  101.3 3.0 %collective-permute-done.25 = bf16[64,2048]{1,0:T(8,128)(2,1)S(1)} collective-permute-done((bf16[64,2048]{1,0:T(8,128)(2,1)S(1)}, bf16[64,2048]{1,0:T(8,128)(2,1)S(1)}, u32[]{:S(2)}, u32[]{:S(2)}) %collective-permute-start.25) | collective-permute-done | bytes 262176 | tf_op jit(solution)/shard_map/ppermute | solution.py:36
  105.3 2.8 %collective-permute-done.23 = bf16[64,2048]{1,0:T(8,128)(2,1)S(1)} collective-permute-done((bf16[64,2048]{1,0:T(8,128)(2,1)S(1)}, bf16[64,2048]{1,0:T(8,128)(2,1)S(1)}, u32[]{:S(2)}, u32[]{:S(2)}) %collective-permute-start.23) | collective-permute-done | bytes 262176 | tf_op jit(solution)/shard_map/ppermute | solution.py:36
  108.1 2.1 %collective-permute-start.24 = (bf16[32,2048]{1,0:T(8,128)(2,1)S(1)}, bf16[32,2048]{1,0:T(8,128)(2,1)S(1)}, u32[]{:S(2)}, u32[]{:S(2)}) collective-permute-start(bf16[32,2048]{1,0:T(8,128)(2,1)S(1)} %fusion.3), channel_id=1, source_target_pairs={{0,16},{1,17},{2,18},{3,19},{4,20},{5,21},{6,22},{7,23},{8,24},{9,... | collective-permute-start | bytes 393224 | tf_op jit(solution)/shard_map/ppermute | solution.py:36
  110.2 5.1 %collective-permute-done.26 = bf16[32,2048]{1,0:T(8,128)(2,1)S(1)} collective-permute-done((bf16[32,2048]{1,0:T(8,128)(2,1)S(1)}, bf16[32,2048]{1,0:T(8,128)(2,1)S(1)}, u32[]{:S(2)}, u32[]{:S(2)}) %collective-permute-start.26) | collective-permute-done | bytes 131104 | tf_op jit(solution)/shard_map/ppermute | solution.py:36
  115.3 2.0 %collective-permute-done.24 = bf16[32,2048]{1,0:T(8,128)(2,1)S(1)} collective-permute-done((bf16[32,2048]{1,0:T(8,128)(2,1)S(1)}, bf16[32,2048]{1,0:T(8,128)(2,1)S(1)}, u32[]{:S(2)}, u32[]{:S(2)}) %collective-permute-start.24) | collective-permute-done | bytes 131104 | tf_op jit(solution)/shard_map/ppermute | solution.py:36
  (76 shorter events, 32.5 us)
Async XLA Ops:
  2.4 15.3 %collective-permute-start = (bf16[256,1024]{1,0:T(8,128)(2,1)}, bf16[256,1024]{1,0:T(8,128)(2,1)}, u32[]{:S(2)}, u32[]{:S(2)}) collective-permute-start(bf16[256,1024]{1,0:T(8,128)(2,1)} %rest_0_.1), channel_id=1, source_target_pairs={{0,8},{1,9},{2,10},{3,11},{4,12},{5,13},{6,14},{7,15},{8,16},{9,17... | collective-permute-start | bytes 1572872 | tf_op jit(solution)/shard_map/ppermute | solution.py:36
  8.8 14.2 %collective-permute-start.5 = (bf16[128,2048]{1,0:T(8,128)(2,1)S(1)}, bf16[128,2048]{1,0:T(8,128)(2,1)S(1)}, u32[]{:S(2)}, u32[]{:S(2)}) collective-permute-start(bf16[128,2048]{1,0:T(8,128)(2,1)S(1)} %join.4.refs_0_), channel_id=1, source_target_pairs={{0,1},{1,0},{2,3},{3,2},{4,5},{5,4},{6,7},{7,6},{8,9},{9,8},{10,11... | collective-permute-start | bytes 1572872 | tf_op jit(solution)/shard_map/ppermute | solution.py:36
  10.4 14.2 %collective-permute-start.7 = (bf16[128,2048]{1,0:T(8,128)(2,1)S(1)}, bf16[128,2048]{1,0:T(8,128)(2,1)S(1)}, u32[]{:S(2)}, u32[]{:S(2)}) collective-permute-start(bf16[128,2048]{1,0:T(8,128)(2,1)S(1)} %join.6.refs_0_), channel_id=1, source_target_pairs={{0,2},{1,3},{2,0},{3,1},{4,6},{5,7},{6,4},{7,5},{8,10},{9,11},{10,... | collective-permute-start | bytes 1572872 | tf_op jit(solution)/shard_map/ppermute | solution.py:36
  17.7 14.5 %collective-permute-start.1 = (bf16[256,1024]{1,0:T(8,128)(2,1)}, bf16[256,1024]{1,0:T(8,128)(2,1)}, u32[]{:S(2)}, u32[]{:S(2)}) collective-permute-start(bf16[256,1024]{1,0:T(8,128)(2,1)} %collective-permute-done.rest_1_), channel_id=1, source_target_pairs={{0,8},{1,9},{2,10},{3,11},{4,12},{5,13},{6,14},{7,15},{8,16},{9,17... | collective-permute-start | bytes 1572872 | tf_op jit(solution)/shard_map/ppermute | solution.py:36
  23.0 23.4 %collective-permute-start.6 = (bf16[256,2048]{1,0:T(8,128)(2,1)S(1)}, bf16[256,2048]{1,0:T(8,128)(2,1)}, u32[]{:S(2)}, u32[]{:S(2)}) collective-permute-start(bf16[256,2048]{1,0:T(8,128)(2,1)S(1)} %join.5.refs_0_), channel_id=1, source_target_pairs={{0,2},{1,3},{2,0},{3,1},{4,6},{5,7},{6,4},{7,5},{8,10},{9,11},{10,... | collective-permute-start | bytes 3145736 | tf_op jit(solution)/shard_map/ppermute | solution.py:36
  24.7 23.0 %collective-permute-start.8 = (bf16[256,2048]{1,0:T(8,128)(2,1)S(1)}, bf16[256,2048]{1,0:T(8,128)(2,1)S(1)}, u32[]{:S(2)}, u32[]{:S(2)}) collective-permute-start(bf16[256,2048]{1,0:T(8,128)(2,1)S(1)} %join.7.refs_2_), channel_id=1, source_target_pairs={{0,1},{1,0},{2,3},{3,2},{4,5},{5,4},{6,7},{7,6},{8,9},{9,8},{10,11... | collective-permute-start | bytes 3145736 | tf_op jit(solution)/shard_map/ppermute | solution.py:36
  49.6 10.2 %collective-permute-start.10 = (bf16[256,2048]{1,0:T(8,128)(2,1)}, bf16[256,2048]{1,0:T(8,128)(2,1)}, u32[]{:S(2)}, u32[]{:S(2)}) collective-permute-start(bf16[256,2048]{1,0:T(8,128)(2,1)} %get-tuple-element.29.refs_5_), channel_id=1, source_target_pairs={{0,4},{1,5},{2,6},{3,7},{4,0},{5,1},{6,2},{7,3},{8,12},{9,13},{10,... | collective-permute-start | bytes 3145736 | tf_op jit(solution)/shard_map/ppermute | solution.py:36
  49.6 10.2 %collective-permute-start.11 = (bf16[256,2048]{1,0:T(8,128)(2,1)S(1)}, bf16[256,2048]{1,0:T(8,128)(2,1)S(1)}, u32[]{:S(2)}, u32[]{:S(2)}) collective-permute-start(bf16[256,2048]{1,0:T(8,128)(2,1)S(1)} %get-tuple-element.30.refs_4_), channel_id=1, source_target_pairs={{0,4},{1,5},{2,6},{3,7},{4,0},{5,1},{6,2},{7,3},{8,12},{9,13},{10,... | collective-permute-start | bytes 3145736 | tf_op jit(solution)/shard_map/ppermute | solution.py:36
  50.1 9.7 %collective-permute-start.12 = (bf16[256,2048]{1,0:T(8,128)(2,1)}, bf16[256,2048]{1,0:T(8,128)(2,1)}, u32[]{:S(2)}, u32[]{:S(2)}) collective-permute-start(bf16[256,2048]{1,0:T(8,128)(2,1)} %copy-done), channel_id=1, source_target_pairs={{0,4},{1,5},{2,6},{3,7},{4,0},{5,1},{6,2},{7,3},{8,12},{9,13},{10,... | collective-permute-start | bytes 3145736 | tf_op jit(solution)/shard_map/ppermute | solution.py:36
  50.1 9.7 %collective-permute-start.9 = (bf16[256,2048]{1,0:T(8,128)(2,1)S(1)}, bf16[256,2048]{1,0:T(8,128)(2,1)}, u32[]{:S(2)}, u32[]{:S(2)}) collective-permute-start(bf16[256,2048]{1,0:T(8,128)(2,1)S(1)} %get-tuple-element.28.refs_4_), channel_id=1, source_target_pairs={{0,4},{1,5},{2,6},{3,7},{4,0},{5,1},{6,2},{7,3},{8,12},{9,13},{10,... | collective-permute-start | bytes 3145736 | tf_op jit(solution)/shard_map/ppermute | solution.py:36
  50.6 9.2 %all-to-all-start = ((bf16[4,32,1024]{2,1,0:T(8,128)(2,1)}), bf16[4,32,1024]{2,1,0:T(8,128)(2,1)S(1)}, u32[]{:S(2)}, u32[]{:S(2)}) async-start(bf16[4,32,1024]{2,1,0:T(8,128)(2,1)} %get-tuple-element.27.refs_4_), calls=%async_computation | async-start | bytes 524288 | tf_op jit(solution)/shard_map/all_to_all | solution.py:321
  61.1 7.8 %collective-permute-start.13 = (bf16[32,1024]{1,0:T(8,128)(2,1)}, bf16[32,1024]{1,0:T(8,128)(2,1)S(1)}, u32[]{:S(2)}, u32[]{:S(2)}) collective-permute-start(bf16[32,1024]{1,0:T(8,128)(2,1)} %get-tuple-element.32), channel_id=1, source_target_pairs={{0,24},{1,25},{2,26},{3,27},{4,28},{5,29},{6,30},{7,31},{8,16},{9,... | collective-permute-start | bytes 196616 | tf_op jit(solution)/shard_map/ppermute | solution.py:36
  65.5 9.8 %all-to-all-start.1 = ((bf16[4,32,1024]{2,1,0:T(8,128)(2,1)}), bf16[4,32,1024]{2,1,0:T(8,128)(2,1)S(1)}, u32[]{:S(2)}, u32[]{:S(2)}) async-start(bf16[4,32,1024]{2,1,0:T(8,128)(2,1)} %get-tuple-element.40), calls=%async_computation.1 | async-start | bytes 524288 | tf_op jit(solution)/shard_map/all_to_all | solution.py:321
  73.3 17.6 %collective-permute-start.16 = (bf16[64,2048]{1,0:T(8,128)(2,1)}, bf16[64,2048]{1,0:T(8,128)(2,1)}, u32[]{:S(2)}, u32[]{:S(2)}) collective-permute-start(bf16[64,2048]{1,0:T(8,128)(2,1)} %get-tuple-element.37), channel_id=1, source_target_pairs={{0,8},{1,9},{2,10},{3,11},{4,12},{5,13},{6,14},{7,15},{8,0},{9,1},... | collective-permute-start | bytes 786440 | tf_op jit(solution)/shard_map/ppermute | solution.py:36
  75.9 9.6 %collective-permute-start.20 = (bf16[32,1024]{1,0:T(8,128)(2,1)S(1)}, bf16[32,1024]{1,0:T(8,128)(2,1)S(1)}, u32[]{:S(2)}, u32[]{:S(2)}) collective-permute-start(bf16[32,1024]{1,0:T(8,128)(2,1)S(1)} %get-tuple-element.41), channel_id=1, source_target_pairs={{0,24},{1,25},{2,26},{3,27},{4,28},{5,29},{6,30},{7,31},{8,16},{9,... | collective-permute-start | bytes 196616 | tf_op jit(solution)/shard_map/ppermute | solution.py:36
  77.4 8.0 %collective-permute-start.21 = (bf16[32,1024]{1,0:T(8,128)(2,1)S(1)}, bf16[32,1024]{1,0:T(8,128)(2,1)S(1)}, u32[]{:S(2)}, u32[]{:S(2)}) collective-permute-start(bf16[32,1024]{1,0:T(8,128)(2,1)S(1)} %get-tuple-element.42), channel_id=1, source_target_pairs={{0,8},{1,9},{2,10},{3,11},{4,12},{5,13},{6,14},{7,15},{8,0},{9,1},... | collective-permute-start | bytes 196616 | tf_op jit(solution)/shard_map/ppermute | solution.py:36
  78.1 8.3 %collective-permute-start.22 = (bf16[32,1024]{1,0:T(8,128)(2,1)S(1)}, bf16[32,1024]{1,0:T(8,128)(2,1)S(1)}, u32[]{:S(2)}, u32[]{:S(2)}) collective-permute-start(bf16[32,1024]{1,0:T(8,128)(2,1)S(1)} %get-tuple-element.43), channel_id=1, source_target_pairs={{0,16},{1,17},{2,18},{3,19},{4,20},{5,21},{6,22},{7,23},{8,24},{9,... | collective-permute-start | bytes 196616 | tf_op jit(solution)/shard_map/ppermute | solution.py:36
  82.4 12.1 %collective-permute-start.18 = (bf16[64,2048]{1,0:T(8,128)(2,1)S(1)}, bf16[64,2048]{1,0:T(8,128)(2,1)S(1)}, u32[]{:S(2)}, u32[]{:S(2)}) collective-permute-start(bf16[64,2048]{1,0:T(8,128)(2,1)S(1)} %get-tuple-element.39), channel_id=1, source_target_pairs={{0,8},{1,9},{2,10},{3,11},{4,12},{5,13},{6,14},{7,15},{8,0},{9,1},... | collective-permute-start | bytes 786440 | tf_op jit(solution)/shard_map/ppermute | solution.py:36
  88.4 15.9 %collective-permute-start.25 = (bf16[64,2048]{1,0:T(8,128)(2,1)S(1)}, bf16[64,2048]{1,0:T(8,128)(2,1)S(1)}, u32[]{:S(2)}, u32[]{:S(2)}) collective-permute-start(bf16[64,2048]{1,0:T(8,128)(2,1)S(1)} %get-tuple-element.48), channel_id=1, source_target_pairs={{0,8},{1,9},{2,10},{3,11},{4,12},{5,13},{6,14},{7,15},{8,0},{9,1},... | collective-permute-start | bytes 786440 | tf_op jit(solution)/shard_map/ppermute | solution.py:36
  92.0 13.2 %collective-permute-start.17 = (bf16[32,2048]{1,0:T(8,128)(2,1)S(1)}, bf16[32,2048]{1,0:T(8,128)(2,1)S(1)}, u32[]{:S(2)}, u32[]{:S(2)}) collective-permute-start(bf16[32,2048]{1,0:T(8,128)(2,1)S(1)} %fusion.9.refs_8_), channel_id=1, source_target_pairs={{0,16},{1,17},{2,18},{3,19},{4,20},{5,21},{6,22},{7,23},{8,24},{9,... | collective-permute-start | bytes 393224 | tf_op jit(solution)/shard_map/ppermute | solution.py:36
  94.5 10.7 %collective-permute-start.19 = (bf16[32,2048]{1,0:T(8,128)(2,1)S(1)}, bf16[32,2048]{1,0:T(8,128)(2,1)S(1)}, u32[]{:S(2)}, u32[]{:S(2)}) collective-permute-start(bf16[32,2048]{1,0:T(8,128)(2,1)S(1)} %fusion.6), channel_id=1, source_target_pairs={{0,16},{1,17},{2,18},{3,19},{4,20},{5,21},{6,22},{7,23},{8,24},{9,... | collective-permute-start | bytes 393224 | tf_op jit(solution)/shard_map/ppermute | solution.py:36
  98.8 9.2 %collective-permute-start.23 = (bf16[64,2048]{1,0:T(8,128)(2,1)S(1)}, bf16[64,2048]{1,0:T(8,128)(2,1)S(1)}, u32[]{:S(2)}, u32[]{:S(2)}) collective-permute-start(bf16[64,2048]{1,0:T(8,128)(2,1)S(1)} %get-tuple-element.46), channel_id=1, source_target_pairs={{0,8},{1,9},{2,10},{3,11},{4,12},{5,13},{6,14},{7,15},{8,0},{9,1},... | collective-permute-start | bytes 786440 | tf_op jit(solution)/shard_map/ppermute | solution.py:36
  104.4 10.9 %collective-permute-start.26 = (bf16[32,2048]{1,0:T(8,128)(2,1)S(1)}, bf16[32,2048]{1,0:T(8,128)(2,1)S(1)}, u32[]{:S(2)}, u32[]{:S(2)}) collective-permute-start(bf16[32,2048]{1,0:T(8,128)(2,1)S(1)} %fusion), channel_id=1, source_target_pairs={{0,16},{1,17},{2,18},{3,19},{4,20},{5,21},{6,22},{7,23},{8,24},{9,... | collective-permute-start | bytes 393224 | tf_op jit(solution)/shard_map/ppermute | solution.py:36
  108.1 9.2 %collective-permute-start.24 = (bf16[32,2048]{1,0:T(8,128)(2,1)S(1)}, bf16[32,2048]{1,0:T(8,128)(2,1)S(1)}, u32[]{:S(2)}, u32[]{:S(2)}) collective-permute-start(bf16[32,2048]{1,0:T(8,128)(2,1)S(1)} %fusion.3), channel_id=1, source_target_pairs={{0,16},{1,17},{2,18},{3,19},{4,20},{5,21},{6,22},{7,23},{8,24},{9,... | collective-permute-start | bytes 393224 | tf_op jit(solution)/shard_map/ppermute | solution.py:36
  (12 other events, 45.9 us)

commit v5 on v4

--- a/solution.py
+++ b/solution.py
@@ -299,7 +299,7 @@
     bits = [1 << index for index in range(chans.bit_length() - 1)]
     parts, spots = [], []
     for which, order in enumerate((bits, bits[::-1])):
-        held = join([(out_weight, which)], half, [crossed[0]])
+        held = join([(out_weight, which)], half)
         found = [0]
         for step, bit in enumerate(order):
             if step:

time: 119 us -> 118 us (level)
  starting transfers between devices: 49.8 us -> 43.3 us
  waiting for transfers between devices: 42.7 us -> 48.2 us
    ppermute x27, starting transfers between devices: 43 us -> 36.5 us  [permute(): return lax.ppermute(value, AXES, route)]
    ppermute x27, waiting for transfers between devices: 37.1 us -> 42.1 us  [permute(): return lax.ppermute(value, AXES, route)]
    unnamed x14 -> x12, local copies, waits for them, and re-layouts: 3.95 us -> 3.95 us
  transfers between devices with their start and end apart: 29 -> 29, of which waited for: 14 -> 16; matrix products, arithmetic and copies ran while one was open for 1% -> 1% of each run, Pallas kernels for 15% -> 15%
where the time goes in v5:
time: 118 us; the launch traced here: 117 us
  waiting for transfers between devices  48.2 us (41%)
  starting transfers between devices  43.3 us (37%)
  Pallas kernels  19.1 us (16%)
  local copies, waits for them, and re-layouts  4.04 us (3%)
  other arithmetic  2.18 us (2%)
    ppermute x27, waiting for transfers between devices, permute(): return lax.ppermute(value, AXES, route)  42.1 us
    ppermute x27, starting transfers between devices, permute(): return lax.ppermute(value, AXES, route)  36.5 us
    pallas_call x4, Pallas kernels, project(): pl.pallas_call(functools.partial(project_kernel, len(acts), firsts, tile,...  9.92 us
    pallas_call x1, Pallas kernels, convolve(): pl.pallas_call(functools.partial(conv_kernel, lags), grid_spec=pltpu.Pref...  7.09 us
    all_to_all x2, starting transfers between devices, body(): lax.all_to_all(some, 'chan', split_axis=0, concat_axis=0)  6.81 us
    all_to_all x2, waiting for transfers between devices, body(): lax.all_to_all(some, 'chan', split_axis=0, concat_axis=0)  6.11 us
    unnamed x12, local copies, waits for them, and re-layouts  3.95 us
  transfers between devices with their start and end apart: 29, of which 16 were waited for; matrix products, arithmetic and copies ran while one was open for 1% of the time, Pallas kernels for 15%

profile of v5, /device:TPU:0, one launch (start us, length us, event | category | flops | bytes accessed | tf_op | source)
XLA Modules:
  0.0 117.2 jit_solution(11947753423308831842)
XLA Ops:
  0.0 5.7 %collective-permute-start = (bf16[256,1024]{1,0:T(8,128)(2,1)}, bf16[256,1024]{1,0:T(8,128)(2,1)}, u32[]{:S(2)}, u32[]{:S(2)}) collective-permute-start(bf16[256,1024]{1,0:T(8,128)(2,1)} %rest_0_.1), channel_id=1, source_target_pairs={{0,8},{1,9},{2,10},{3,11},{4,12},{5,13},{6,14},{7,15},{8,16},{9,17... | collective-permute-start | bytes 1572872 | tf_op jit(solution)/shard_map/ppermute | solution.py:36
  10.2 6.2 %collective-permute-done.rest_1_ = bf16[256,1024]{1,0:T(8,128)(2,1)} collective-permute-done((bf16[256,1024]{1,0:T(8,128)(2,1)}, bf16[256,1024]{1,0:T(8,128)(2,1)}, u32[]{:S(2)}, u32[]{:S(2)}) %collective-permute-start) | collective-permute-done | bytes 524320 | tf_op jit(solution)/shard_map/ppermute | solution.py:36
  16.4 5.2 %collective-permute-start.1 = (bf16[256,1024]{1,0:T(8,128)(2,1)}, bf16[256,1024]{1,0:T(8,128)(2,1)}, u32[]{:S(2)}, u32[]{:S(2)}) collective-permute-start(bf16[256,1024]{1,0:T(8,128)(2,1)} %collective-permute-done.rest_1_), channel_id=1, source_target_pairs={{0,8},{1,9},{2,10},{3,11},{4,12},{5,13},{6,14},{7,15},{8,16},{9,17... | collective-permute-start | bytes 1572872 | tf_op jit(solution)/shard_map/ppermute | solution.py:36
  24.9 2.1 %collective-permute-start.2 = (bf16[256,1024]{1,0:T(8,128)(2,1)}, bf16[256,1024]{1,0:T(8,128)(2,1)}, u32[]{:S(2)}, u32[]{:S(2)}) collective-permute-start(bf16[256,1024]{1,0:T(8,128)(2,1)} %rest_0_.1), channel_id=1, source_target_pairs={{0,4},{1,5},{2,6},{3,7},{8,12},{9,13},{10,14},{11,15},{16,20},{17,... | collective-permute-start | bytes 1572872 | tf_op jit(solution)/shard_map/ppermute | solution.py:36
  27.0 4.4 %collective-permute-done.1.rest_2_ = bf16[256,1024]{1,0:T(8,128)(2,1)} collective-permute-done((bf16[256,1024]{1,0:T(8,128)(2,1)}, bf16[256,1024]{1,0:T(8,128)(2,1)}, u32[]{:S(2)}, u32[]{:S(2)}) %collective-permute-start.1) | collective-permute-done | bytes 524320 | tf_op jit(solution)/shard_map/ppermute | solution.py:36
  32.7 2.8 %collective-permute-done.4.rest_5_ = bf16[256,1024]{1,0:T(8,128)(2,1)} collective-permute-done((bf16[256,1024]{1,0:T(8,128)(2,1)}, bf16[256,1024]{1,0:T(8,128)(2,1)}, u32[]{:S(2)}, u32[]{:S(2)}) %collective-permute-start.4) | collective-permute-done | bytes 524320 | tf_op jit(solution)/shard_map/ppermute | solution.py:36
  35.5 7.1 %conv.1 = (bf16[4,32,1024]{2,1,0:T(8,128)(2,1)}, bf16[4,32,1024]{2,1,0:T(8,128)(2,1)}) custom-call(s32[1]{0:T(128)} %bitcast.9.core_ref, bf16[512,256]{1,0:T(8,128)(2,1)} %constant.42.clone.table_ref, bf16[256,512]{1,0:T(8,128)(2,1)} %constant.43.clone.back_ref, f32[1,1024]{1,0:T(1,128)} %bitcast.11, bf16[256,1024]{1,0:T(8,128)(2,1)} %gates_ref.1, ...), custom_call_target="tpu_custom_call" | custom-call | flops 4026531840 | bytes 6291456 | tf_op jit(solution)/shard_map/conv/pallas_call | solution.py:108
  42.6 3.0 %collective-permute-done.6.refs_1_ = bf16[256,2048]{1,0:T(8,128)(2,1)} collective-permute-done((bf16[256,2048]{1,0:T(8,128)(2,1)S(1)}, bf16[256,2048]{1,0:T(8,128)(2,1)}, u32[]{:S(2)}, u32[]{:S(2)}) %collective-permute-start.6) | collective-permute-done | bytes 1048608 | tf_op jit(solution)/shard_map/ppermute | solution.py:36
  49.8 3.4 %all-to-all-start = ((bf16[4,32,1024]{2,1,0:T(8,128)(2,1)}), bf16[4,32,1024]{2,1,0:T(8,128)(2,1)S(1)}, u32[]{:S(2)}, u32[]{:S(2)}) async-start(bf16[4,32,1024]{2,1,0:T(8,128)(2,1)} %get-tuple-element.27.refs_4_), calls=%async_computation | async-start | bytes 524288 | tf_op jit(solution)/shard_map/all_to_all | solution.py:321
  53.4 5.7 %all-to-all-done.refs_0_ = bf16[4,32,1024]{2,1,0:T(8,128)(2,1)S(1)} async-done(((bf16[4,32,1024]{2,1,0:T(8,128)(2,1)}), bf16[4,32,1024]{2,1,0:T(8,128)(2,1)S(1)}, u32[]{:S(2)}, u32[]{:S(2)}) %all-to-all-start) | async-done | bytes 262176 | tf_op jit(solution)/shard_map/all_to_all | solution.py:321
  62.7 2.0 %collective-permute-start.15 = (bf16[32,1024]{1,0:T(8,128)(2,1)}, bf16[32,1024]{1,0:T(8,128)(2,1)}, u32[]{:S(2)}, u32[]{:S(2)}) collective-permute-start(bf16[32,1024]{1,0:T(8,128)(2,1)} %get-tuple-element.34), channel_id=1, source_target_pairs={{0,16},{1,17},{2,18},{3,19},{4,20},{5,21},{6,22},{7,23},{8,24},{9,... | collective-permute-start | bytes 196616 | tf_op jit(solution)/shard_map/ppermute | solution.py:36
  64.7 3.4 %all-to-all-start.1 = ((bf16[4,32,1024]{2,1,0:T(8,128)(2,1)}), bf16[4,32,1024]{2,1,0:T(8,128)(2,1)S(1)}, u32[]{:S(2)}, u32[]{:S(2)}) async-start(bf16[4,32,1024]{2,1,0:T(8,128)(2,1)} %get-tuple-element.40), calls=%async_computation.1 | async-start | bytes 524288 | tf_op jit(solution)/shard_map/all_to_all | solution.py:321
  68.9 3.3 %project.4 = (bf16[64,2048]{1,0:T(8,128)(2,1)}, f32[64,2048]{1,0:T(8,128)S(1)}) custom-call(bf16[32,1024]{1,0:T(8,128)(2,1)S(1)} %collective-permute-done.13.refs_0_, bf16[32,1024]{1,0:T(8,128)(2,1)} %collective-permute-done.14.refs_1_, bf16[32,1024]{1,0:T(8,128)(2,1)} %collective-permute-done.15.refs_2_, bf16[32,1024]{1,0:T(8,128)(2,1)S(1)} %get-tuple-element.35.refs_3_, ...), custom_call_target="tpu_custom_call" | custom-call | flops 536870912 | bytes 5767168 | tf_op jit(solution)/shard_map/project/pallas_call | solution.py:254
  74.1 2.4 %collective-permute-start.20 = (bf16[32,1024]{1,0:T(8,128)(2,1)S(1)}, bf16[32,1024]{1,0:T(8,128)(2,1)S(1)}, u32[]{:S(2)}, u32[]{:S(2)}) collective-permute-start(bf16[32,1024]{1,0:T(8,128)(2,1)S(1)} %get-tuple-element.41), channel_id=1, source_target_pairs={{0,24},{1,25},{2,26},{3,27},{4,28},{5,29},{6,30},{7,31},{8,16},{9,... | collective-permute-start | bytes 196616 | tf_op jit(solution)/shard_map/ppermute | solution.py:36
  76.5 2.1 %collective-permute-start.22 = (bf16[32,1024]{1,0:T(8,128)(2,1)S(1)}, bf16[32,1024]{1,0:T(8,128)(2,1)S(1)}, u32[]{:S(2)}, u32[]{:S(2)}) collective-permute-start(bf16[32,1024]{1,0:T(8,128)(2,1)S(1)} %get-tuple-element.43), channel_id=1, source_target_pairs={{0,16},{1,17},{2,18},{3,19},{4,20},{5,21},{6,22},{7,23},{8,24},{9,... | collective-permute-start | bytes 196616 | tf_op jit(solution)/shard_map/ppermute | solution.py:36
  78.5 2.0 %project.5 = (bf16[64,2048]{1,0:T(8,128)(2,1)S(1)}, f32[64,2048]{1,0:T(8,128)S(1)}) custom-call(bf16[32,1024]{1,0:T(8,128)(2,1)S(1)} %collective-permute-done.13.refs_0_, bf16[32,1024]{1,0:T(8,128)(2,1)} %collective-permute-done.14.refs_1_, bf16[32,1024]{1,0:T(8,128)(2,1)} %collective-permute-done.15.refs_2_, ...), custom_call_target="tpu_custom_call" | custom-call | flops 536870912 | bytes 5767168 | tf_op jit(solution)/shard_map/project/pallas_call | solution.py:254
  81.3 2.9 %collective-permute-done.20.refs_0_ = bf16[32,1024]{1,0:T(8,128)(2,1)S(1)} collective-permute-done((bf16[32,1024]{1,0:T(8,128)(2,1)S(1)}, bf16[32,1024]{1,0:T(8,128)(2,1)S(1)}, u32[]{:S(2)}, u32[]{:S(2)}) %collective-permute-start.20) | collective-permute-done | bytes 65568 | tf_op jit(solution)/shard_map/ppermute | solution.py:36
  84.2 2.0 %collective-permute-done.21.refs_1_ = bf16[32,1024]{1,0:T(8,128)(2,1)S(1)} collective-permute-done((bf16[32,1024]{1,0:T(8,128)(2,1)S(1)}, bf16[32,1024]{1,0:T(8,128)(2,1)S(1)}, u32[]{:S(2)}, u32[]{:S(2)}) %collective-permute-start.21) | collective-permute-done | bytes 65568 | tf_op jit(solution)/shard_map/ppermute | solution.py:36
  91.7 3.0 %collective-permute-done.18 = bf16[64,2048]{1,0:T(8,128)(2,1)S(1)} collective-permute-done((bf16[64,2048]{1,0:T(8,128)(2,1)S(1)}, bf16[64,2048]{1,0:T(8,128)(2,1)S(1)}, u32[]{:S(2)}, u32[]{:S(2)}) %collective-permute-start.18) | collective-permute-done | bytes 262176 | tf_op jit(solution)/shard_map/ppermute | solution.py:36
  94.8 2.6 %project.6 = (bf16[64,2048]{1,0:T(8,128)(2,1)S(1)}, f32[64,2048]{1,0:T(8,128)S(1)}) custom-call(bf16[32,1024]{1,0:T(8,128)(2,1)S(1)} %collective-permute-done.20.refs_0_, bf16[32,1024]{1,0:T(8,128)(2,1)S(1)} %collective-permute-done.21.refs_1_, bf16[32,1024]{1,0:T(8,128)(2,1)S(1)} %collective-permute-done.22.refs_2_, ...), custom_call_target="tpu_custom_call" | custom-call | flops 536870912 | bytes 5767168 | tf_op jit(solution)/shard_map/project/pallas_call | solution.py:254
  97.4 2.3 %collective-permute-start.23 = (bf16[64,2048]{1,0:T(8,128)(2,1)S(1)}, bf16[64,2048]{1,0:T(8,128)(2,1)S(1)}, u32[]{:S(2)}, u32[]{:S(2)}) collective-permute-start(bf16[64,2048]{1,0:T(8,128)(2,1)S(1)} %get-tuple-element.46), channel_id=1, source_target_pairs={{0,8},{1,9},{2,10},{3,11},{4,12},{5,13},{6,14},{7,15},{8,0},{9,1},... | collective-permute-start | bytes 786440 | tf_op jit(solution)/shard_map/ppermute | solution.py:36
  99.7 4.1 %collective-permute-done.25 = bf16[64,2048]{1,0:T(8,128)(2,1)S(1)} collective-permute-done((bf16[64,2048]{1,0:T(8,128)(2,1)S(1)}, bf16[64,2048]{1,0:T(8,128)(2,1)S(1)}, u32[]{:S(2)}, u32[]{:S(2)}) %collective-permute-start.25) | collective-permute-done | bytes 262176 | tf_op jit(solution)/shard_map/ppermute | solution.py:36
  104.3 3.6 %collective-permute-done.23 = bf16[64,2048]{1,0:T(8,128)(2,1)S(1)} collective-permute-done((bf16[64,2048]{1,0:T(8,128)(2,1)S(1)}, bf16[64,2048]{1,0:T(8,128)(2,1)S(1)}, u32[]{:S(2)}, u32[]{:S(2)}) %collective-permute-start.23) | collective-permute-done | bytes 262176 | tf_op jit(solution)/shard_map/ppermute | solution.py:36
  108.6 6.2 %collective-permute-done.26 = bf16[32,2048]{1,0:T(8,128)(2,1)S(1)} collective-permute-done((bf16[32,2048]{1,0:T(8,128)(2,1)S(1)}, bf16[32,2048]{1,0:T(8,128)(2,1)S(1)}, u32[]{:S(2)}, u32[]{:S(2)}) %collective-permute-start.26) | collective-permute-done | bytes 131104 | tf_op jit(solution)/shard_map/ppermute | solution.py:36
  (74 shorter events, 29.2 us)
Async XLA Ops:
  0.0 16.4 %collective-permute-start = (bf16[256,1024]{1,0:T(8,128)(2,1)}, bf16[256,1024]{1,0:T(8,128)(2,1)}, u32[]{:S(2)}, u32[]{:S(2)}) collective-permute-start(bf16[256,1024]{1,0:T(8,128)(2,1)} %rest_0_.1), channel_id=1, source_target_pairs={{0,8},{1,9},{2,10},{3,11},{4,12},{5,13},{6,14},{7,15},{8,16},{9,17... | collective-permute-start | bytes 1572872 | tf_op jit(solution)/shard_map/ppermute | solution.py:36
  7.0 14.6 %collective-permute-start.5 = (bf16[128,2048]{1,0:T(8,128)(2,1)S(1)}, bf16[128,2048]{1,0:T(8,128)(2,1)S(1)}, u32[]{:S(2)}, u32[]{:S(2)}) collective-permute-start(bf16[128,2048]{1,0:T(8,128)(2,1)S(1)} %join.4.refs_0_), channel_id=1, source_target_pairs={{0,1},{1,0},{2,3},{3,2},{4,5},{5,4},{6,7},{7,6},{8,9},{9,8},{10,11... | collective-permute-start | bytes 1572872 | tf_op jit(solution)/shard_map/ppermute | solution.py:36
  8.6 14.7 %collective-permute-start.7 = (bf16[128,2048]{1,0:T(8,128)(2,1)S(1)}, bf16[128,2048]{1,0:T(8,128)(2,1)S(1)}, u32[]{:S(2)}, u32[]{:S(2)}) collective-permute-start(bf16[128,2048]{1,0:T(8,128)(2,1)S(1)} %join.6.refs_0_), channel_id=1, source_target_pairs={{0,2},{1,3},{2,0},{3,1},{4,6},{5,7},{6,4},{7,5},{8,10},{9,11},{10,... | collective-permute-start | bytes 1572872 | tf_op jit(solution)/shard_map/ppermute | solution.py:36
  16.4 15.0 %collective-permute-start.1 = (bf16[256,1024]{1,0:T(8,128)(2,1)}, bf16[256,1024]{1,0:T(8,128)(2,1)}, u32[]{:S(2)}, u32[]{:S(2)}) collective-permute-start(bf16[256,1024]{1,0:T(8,128)(2,1)} %collective-permute-done.rest_1_), channel_id=1, source_target_pairs={{0,8},{1,9},{2,10},{3,11},{4,12},{5,13},{6,14},{7,15},{8,16},{9,17... | collective-permute-start | bytes 1572872 | tf_op jit(solution)/shard_map/ppermute | solution.py:36
  21.7 23.9 %collective-permute-start.6 = (bf16[256,2048]{1,0:T(8,128)(2,1)S(1)}, bf16[256,2048]{1,0:T(8,128)(2,1)}, u32[]{:S(2)}, u32[]{:S(2)}) collective-permute-start(bf16[256,2048]{1,0:T(8,128)(2,1)S(1)} %join.5.refs_0_), channel_id=1, source_target_pairs={{0,2},{1,3},{2,0},{3,1},{4,6},{5,7},{6,4},{7,5},{8,10},{9,11},{10,... | collective-permute-start | bytes 3145736 | tf_op jit(solution)/shard_map/ppermute | solution.py:36
  23.3 23.5 %collective-permute-start.8 = (bf16[256,2048]{1,0:T(8,128)(2,1)S(1)}, bf16[256,2048]{1,0:T(8,128)(2,1)S(1)}, u32[]{:S(2)}, u32[]{:S(2)}) collective-permute-start(bf16[256,2048]{1,0:T(8,128)(2,1)S(1)} %join.7.refs_2_), channel_id=1, source_target_pairs={{0,1},{1,0},{2,3},{3,2},{4,5},{5,4},{6,7},{7,6},{8,9},{9,8},{10,11... | collective-permute-start | bytes 3145736 | tf_op jit(solution)/shard_map/ppermute | solution.py:36
  24.9 7.8 %collective-permute-start.2 = (bf16[256,1024]{1,0:T(8,128)(2,1)}, bf16[256,1024]{1,0:T(8,128)(2,1)}, u32[]{:S(2)}, u32[]{:S(2)}) collective-permute-start(bf16[256,1024]{1,0:T(8,128)(2,1)} %rest_0_.1), channel_id=1, source_target_pairs={{0,4},{1,5},{2,6},{3,7},{8,12},{9,13},{10,14},{11,15},{16,20},{17,... | collective-permute-start | bytes 1572872 | tf_op jit(solution)/shard_map/ppermute | solution.py:36
  48.8 10.2 %collective-permute-start.10 = (bf16[256,2048]{1,0:T(8,128)(2,1)}, bf16[256,2048]{1,0:T(8,128)(2,1)}, u32[]{:S(2)}, u32[]{:S(2)}) collective-permute-start(bf16[256,2048]{1,0:T(8,128)(2,1)} %get-tuple-element.29.refs_5_), channel_id=1, source_target_pairs={{0,4},{1,5},{2,6},{3,7},{4,0},{5,1},{6,2},{7,3},{8,12},{9,13},{10,... | collective-permute-start | bytes 3145736 | tf_op jit(solution)/shard_map/ppermute | solution.py:36
  48.8 10.2 %collective-permute-start.11 = (bf16[256,2048]{1,0:T(8,128)(2,1)S(1)}, bf16[256,2048]{1,0:T(8,128)(2,1)S(1)}, u32[]{:S(2)}, u32[]{:S(2)}) collective-permute-start(bf16[256,2048]{1,0:T(8,128)(2,1)S(1)} %get-tuple-element.30.refs_4_), channel_id=1, source_target_pairs={{0,4},{1,5},{2,6},{3,7},{4,0},{5,1},{6,2},{7,3},{8,12},{9,13},{10,... | collective-permute-start | bytes 3145736 | tf_op jit(solution)/shard_map/ppermute | solution.py:36
  49.3 9.7 %collective-permute-start.12 = (bf16[256,2048]{1,0:T(8,128)(2,1)}, bf16[256,2048]{1,0:T(8,128)(2,1)}, u32[]{:S(2)}, u32[]{:S(2)}) collective-permute-start(bf16[256,2048]{1,0:T(8,128)(2,1)} %copy-done), channel_id=1, source_target_pairs={{0,4},{1,5},{2,6},{3,7},{4,0},{5,1},{6,2},{7,3},{8,12},{9,13},{10,... | collective-permute-start | bytes 3145736 | tf_op jit(solution)/shard_map/ppermute | solution.py:36
  49.3 9.7 %collective-permute-start.9 = (bf16[256,2048]{1,0:T(8,128)(2,1)S(1)}, bf16[256,2048]{1,0:T(8,128)(2,1)}, u32[]{:S(2)}, u32[]{:S(2)}) collective-permute-start(bf16[256,2048]{1,0:T(8,128)(2,1)S(1)} %get-tuple-element.28.refs_4_), channel_id=1, source_target_pairs={{0,4},{1,5},{2,6},{3,7},{4,0},{5,1},{6,2},{7,3},{8,12},{9,13},{10,... | collective-permute-start | bytes 3145736 | tf_op jit(solution)/shard_map/ppermute | solution.py:36
  49.8 9.2 %all-to-all-start = ((bf16[4,32,1024]{2,1,0:T(8,128)(2,1)}), bf16[4,32,1024]{2,1,0:T(8,128)(2,1)S(1)}, u32[]{:S(2)}, u32[]{:S(2)}) async-start(bf16[4,32,1024]{2,1,0:T(8,128)(2,1)} %get-tuple-element.27.refs_4_), calls=%async_computation | async-start | bytes 524288 | tf_op jit(solution)/shard_map/all_to_all | solution.py:321
  64.7 8.8 %all-to-all-start.1 = ((bf16[4,32,1024]{2,1,0:T(8,128)(2,1)}), bf16[4,32,1024]{2,1,0:T(8,128)(2,1)S(1)}, u32[]{:S(2)}, u32[]{:S(2)}) async-start(bf16[4,32,1024]{2,1,0:T(8,128)(2,1)} %get-tuple-element.40), calls=%async_computation.1 | async-start | bytes 524288 | tf_op jit(solution)/shard_map/all_to_all | solution.py:321
  73.0 16.4 %collective-permute-start.16 = (bf16[64,2048]{1,0:T(8,128)(2,1)}, bf16[64,2048]{1,0:T(8,128)(2,1)}, u32[]{:S(2)}, u32[]{:S(2)}) collective-permute-start(bf16[64,2048]{1,0:T(8,128)(2,1)} %get-tuple-element.37), channel_id=1, source_target_pairs={{0,8},{1,9},{2,10},{3,11},{4,12},{5,13},{6,14},{7,15},{8,0},{9,1},... | collective-permute-start | bytes 786440 | tf_op jit(solution)/shard_map/ppermute | solution.py:36
  74.1 10.2 %collective-permute-start.20 = (bf16[32,1024]{1,0:T(8,128)(2,1)S(1)}, bf16[32,1024]{1,0:T(8,128)(2,1)S(1)}, u32[]{:S(2)}, u32[]{:S(2)}) collective-permute-start(bf16[32,1024]{1,0:T(8,128)(2,1)S(1)} %get-tuple-element.41), channel_id=1, source_target_pairs={{0,24},{1,25},{2,26},{3,27},{4,28},{5,29},{6,30},{7,31},{8,16},{9,... | collective-permute-start | bytes 196616 | tf_op jit(solution)/shard_map/ppermute | solution.py:36
  76.5 9.8 %collective-permute-start.21 = (bf16[32,1024]{1,0:T(8,128)(2,1)S(1)}, bf16[32,1024]{1,0:T(8,128)(2,1)S(1)}, u32[]{:S(2)}, u32[]{:S(2)}) collective-permute-start(bf16[32,1024]{1,0:T(8,128)(2,1)S(1)} %get-tuple-element.42), channel_id=1, source_target_pairs={{0,8},{1,9},{2,10},{3,11},{4,12},{5,13},{6,14},{7,15},{8,0},{9,1},... | collective-permute-start | bytes 196616 | tf_op jit(solution)/shard_map/ppermute | solution.py:36
  76.5 9.8 %collective-permute-start.22 = (bf16[32,1024]{1,0:T(8,128)(2,1)S(1)}, bf16[32,1024]{1,0:T(8,128)(2,1)S(1)}, u32[]{:S(2)}, u32[]{:S(2)}) collective-permute-start(bf16[32,1024]{1,0:T(8,128)(2,1)S(1)} %get-tuple-element.43), channel_id=1, source_target_pairs={{0,16},{1,17},{2,18},{3,19},{4,20},{5,21},{6,22},{7,23},{8,24},{9,... | collective-permute-start | bytes 196616 | tf_op jit(solution)/shard_map/ppermute | solution.py:36
  80.6 14.1 %collective-permute-start.18 = (bf16[64,2048]{1,0:T(8,128)(2,1)S(1)}, bf16[64,2048]{1,0:T(8,128)(2,1)S(1)}, u32[]{:S(2)}, u32[]{:S(2)}) collective-permute-start(bf16[64,2048]{1,0:T(8,128)(2,1)S(1)} %get-tuple-element.39), channel_id=1, source_target_pairs={{0,8},{1,9},{2,10},{3,11},{4,12},{5,13},{6,14},{7,15},{8,0},{9,1},... | collective-permute-start | bytes 786440 | tf_op jit(solution)/shard_map/ppermute | solution.py:36
  88.3 15.6 %collective-permute-start.25 = (bf16[64,2048]{1,0:T(8,128)(2,1)S(1)}, bf16[64,2048]{1,0:T(8,128)(2,1)S(1)}, u32[]{:S(2)}, u32[]{:S(2)}) collective-permute-start(bf16[64,2048]{1,0:T(8,128)(2,1)S(1)} %get-tuple-element.48), channel_id=1, source_target_pairs={{0,8},{1,9},{2,10},{3,11},{4,12},{5,13},{6,14},{7,15},{8,0},{9,1},... | collective-permute-start | bytes 786440 | tf_op jit(solution)/shard_map/ppermute | solution.py:36
  90.5 13.5 %collective-permute-start.17 = (bf16[32,2048]{1,0:T(8,128)(2,1)S(1)}, bf16[32,2048]{1,0:T(8,128)(2,1)S(1)}, u32[]{:S(2)}, u32[]{:S(2)}) collective-permute-start(bf16[32,2048]{1,0:T(8,128)(2,1)S(1)} %fusion.9.refs_8_), channel_id=1, source_target_pairs={{0,16},{1,17},{2,18},{3,19},{4,20},{5,21},{6,22},{7,23},{8,24},{9,... | collective-permute-start | bytes 393224 | tf_op jit(solution)/shard_map/ppermute | solution.py:36
  94.8 9.5 %collective-permute-start.19 = (bf16[32,2048]{1,0:T(8,128)(2,1)S(1)}, bf16[32,2048]{1,0:T(8,128)(2,1)S(1)}, u32[]{:S(2)}, u32[]{:S(2)}) collective-permute-start(bf16[32,2048]{1,0:T(8,128)(2,1)S(1)} %fusion.6), channel_id=1, source_target_pairs={{0,16},{1,17},{2,18},{3,19},{4,20},{5,21},{6,22},{7,23},{8,24},{9,... | collective-permute-start | bytes 393224 | tf_op jit(solution)/shard_map/ppermute | solution.py:36
  97.4 10.5 %collective-permute-start.23 = (bf16[64,2048]{1,0:T(8,128)(2,1)S(1)}, bf16[64,2048]{1,0:T(8,128)(2,1)S(1)}, u32[]{:S(2)}, u32[]{:S(2)}) collective-permute-start(bf16[64,2048]{1,0:T(8,128)(2,1)S(1)} %get-tuple-element.46), channel_id=1, source_target_pairs={{0,8},{1,9},{2,10},{3,11},{4,12},{5,13},{6,14},{7,15},{8,0},{9,1},... | collective-permute-start | bytes 786440 | tf_op jit(solution)/shard_map/ppermute | solution.py:36
  103.9 10.9 %collective-permute-start.26 = (bf16[32,2048]{1,0:T(8,128)(2,1)S(1)}, bf16[32,2048]{1,0:T(8,128)(2,1)S(1)}, u32[]{:S(2)}, u32[]{:S(2)}) collective-permute-start(bf16[32,2048]{1,0:T(8,128)(2,1)S(1)} %fusion), channel_id=1, source_target_pairs={{0,16},{1,17},{2,18},{3,19},{4,20},{5,21},{6,22},{7,23},{8,24},{9,... | collective-permute-start | bytes 393224 | tf_op jit(solution)/shard_map/ppermute | solution.py:36
  108.0 8.3 %collective-permute-start.24 = (bf16[32,2048]{1,0:T(8,128)(2,1)S(1)}, bf16[32,2048]{1,0:T(8,128)(2,1)S(1)}, u32[]{:S(2)}, u32[]{:S(2)}) collective-permute-start(bf16[32,2048]{1,0:T(8,128)(2,1)S(1)} %fusion.3), channel_id=1, source_target_pairs={{0,16},{1,17},{2,18},{3,19},{4,20},{5,21},{6,22},{7,23},{8,24},{9,... | collective-permute-start | bytes 393224 | tf_op jit(solution)/shard_map/ppermute | solution.py:36
  (11 other events, 44.0 us)

commit v6 on v5

--- a/solution.py
+++ b/solution.py
@@ -340,27 +340,29 @@
 
     outs = []
     passed = []
-    for some in acts:
+    for turn, some in enumerate(acts):
         row, sent = [], []
         for which in range(2):
-            send, keep = project(
-                some,
-                [(piece, 0) for piece in parts[which]],
-                spots[which],
-                own_rows,
-                half,
-                passed[:1] if which == 0 else [],
-            )
-            for index, step in enumerate(steps):
-                got = permute(send, lambda p, k, c, step=step: (p ^ step, k, c)).astype(F32)
-                many = got.shape[0] // 2
-                if index + 1 < count:
-                    send = (keep[:many] + got[:many]).astype(BF16)
-                    sent.append(send)
-                    keep = keep[many:] + got[many:]
-                else:
-                    keep = keep + got
-            row.append(keep.astype(BF16))
+            chunks = 2 if turn == 1 and which == 0 else 1
+            for chunk in range(chunks):
+                send, keep = project(
+                    some,
+                    [(piece, chunk) for piece in parts[which]],
+                    spots[which],
+                    own_rows,
+                    half // chunks,
+                    passed[:1] if which == 0 else [],
+                )
+                for index, step in enumerate(steps):
+                    got = permute(send, lambda p, k, c, step=step: (p ^ step, k, c)).astype(F32)
+                    many = got.shape[0] // 2
+                    if index + 1 < count:
+                        send = (keep[:many] + got[:many]).astype(BF16)
+                        sent.append(send)
+                        keep = keep[many:] + got[many:]
+                    else:
+                        keep = keep + got
+                row.append(keep.astype(BF16))
         passed = sent
         outs.append(jnp.concatenate(row, axis=1))
     return jnp.concatenate(outs, axis=0)

time: 118 us -> 115 us (0.975)
  waiting for transfers between devices: 48.2 us -> 42.4 us
  Pallas kernels: 19.1 us -> 22.2 us
  starting transfers between devices: 43.3 us -> 44.6 us
    ppermute x27 -> x29, waiting for transfers between devices: 42.1 us -> 36.4 us  [permute(): return lax.ppermute(value, AXES, route)]
    pallas_call x4 -> x5, Pallas kernels: 9.92 us -> 12 us  [project(): pl.pallas_call(functools.partial(project_kernel, len(acts), firsts, tile,...]
    ppermute x27 -> x29, starting transfers between devices: 36.5 us -> 37.8 us  [permute(): return lax.ppermute(value, AXES, route)]
    unnamed x12 -> x16, local copies, waits for them, and re-layouts: 3.95 us -> 2.98 us
  transfers between devices with their start and end apart: 29 -> 31, of which waited for: 16 -> 17; matrix products, arithmetic and copies ran while one was open for 1% -> 1% of each run, Pallas kernels for 15% -> 18%
where the time goes in v6:
time: 115 us
  starting transfers between devices  44.6 us (39%)
  waiting for transfers between devices  42.4 us (37%)
  Pallas kernels  22.2 us (19%)
  local copies, waits for them, and re-layouts  3.07 us (3%)
  other arithmetic  2.2 us (2%)
    ppermute x29, starting transfers between devices, permute(): return lax.ppermute(value, AXES, route)  37.8 us
    ppermute x29, waiting for transfers between devices, permute(): return lax.ppermute(value, AXES, route)  36.4 us
    pallas_call x5, Pallas kernels, project(): pl.pallas_call(functools.partial(project_kernel, len(acts), firsts, tile,...  12 us
    pallas_call x1, Pallas kernels, convolve(): pl.pallas_call(functools.partial(conv_kernel, lags), grid_spec=pltpu.Pref...  7.13 us
    all_to_all x2, starting transfers between devices, body(): lax.all_to_all(some, 'chan', split_axis=0, concat_axis=0)  6.81 us
    all_to_all x2, waiting for transfers between devices, body(): lax.all_to_all(some, 'chan', split_axis=0, concat_axis=0)  5.97 us
    unnamed x16, local copies, waits for them, and re-layouts  2.98 us
  transfers between devices with their start and end apart: 31, of which 17 were waited for; matrix products, arithmetic and copies ran while one was open for 1% of the time, Pallas kernels for 18%

profile of v6, /device:TPU:0, one launch (start us, length us, event | category | flops | bytes accessed | tf_op | source)
XLA Modules:
  0.0 114.8 jit_solution(9637989817310870494)
XLA Ops:
  0.0 5.0 %collective-permute-start = (bf16[256,1024]{1,0:T(8,128)(2,1)}, bf16[256,1024]{1,0:T(8,128)(2,1)S(1)}, u32[]{:S(2)}, u32[]{:S(2)}) collective-permute-start(bf16[256,1024]{1,0:T(8,128)(2,1)} %rest_0_.1), channel_id=1, source_target_pairs={{0,8},{1,9},{2,10},{3,11},{4,12},{5,13},{6,14},{7,15},{8,16},{9,17... | collective-permute-start | bytes 1572872 | tf_op jit(solution)/shard_map/ppermute | solution.py:36
  9.4 7.0 %collective-permute-done.rest_1_ = bf16[256,1024]{1,0:T(8,128)(2,1)S(1)} collective-permute-done((bf16[256,1024]{1,0:T(8,128)(2,1)}, bf16[256,1024]{1,0:T(8,128)(2,1)S(1)}, u32[]{:S(2)}, u32[]{:S(2)}) %collective-permute-start) | collective-permute-done | bytes 524320 | tf_op jit(solution)/shard_map/ppermute | solution.py:36
  16.4 4.3 %collective-permute-start.1 = (bf16[256,1024]{1,0:T(8,128)(2,1)S(1)}, bf16[256,1024]{1,0:T(8,128)(2,1)S(1)}, u32[]{:S(2)}, u32[]{:S(2)}) collective-permute-start(bf16[256,1024]{1,0:T(8,128)(2,1)S(1)} %collective-permute-done.rest_1_), channel_id=1, source_target_pairs={{0,8},{1,9},{2,10},{3,11},{4,12},{5,13},{6,14},{7,15},{8,16},{9,17... | collective-permute-start | bytes 1572872 | tf_op jit(solution)/shard_map/ppermute | solution.py:36
  26.3 4.6 %collective-permute-done.1.rest_2_ = bf16[256,1024]{1,0:T(8,128)(2,1)S(1)} collective-permute-done((bf16[256,1024]{1,0:T(8,128)(2,1)S(1)}, bf16[256,1024]{1,0:T(8,128)(2,1)S(1)}, u32[]{:S(2)}, u32[]{:S(2)}) %collective-permute-start.1) | collective-permute-done | bytes 524320 | tf_op jit(solution)/shard_map/ppermute | solution.py:36
  32.3 2.6 %collective-permute-done.4.rest_5_ = bf16[256,1024]{1,0:T(8,128)(2,1)} collective-permute-done((bf16[256,1024]{1,0:T(8,128)(2,1)S(1)}, bf16[256,1024]{1,0:T(8,128)(2,1)}, u32[]{:S(2)}, u32[]{:S(2)}) %collective-permute-start.4) | collective-permute-done | bytes 524320 | tf_op jit(solution)/shard_map/ppermute | solution.py:36
  34.9 7.1 %conv.1 = (bf16[4,32,1024]{2,1,0:T(8,128)(2,1)}, bf16[4,32,1024]{2,1,0:T(8,128)(2,1)}) custom-call(s32[1]{0:T(128)} %bitcast.9.core_ref, bf16[512,256]{1,0:T(8,128)(2,1)} %constant.42.clone.table_ref, bf16[256,512]{1,0:T(8,128)(2,1)} %constant.43.clone.back_ref, f32[1,1024]{1,0:T(1,128)} %bitcast.11, bf16[256,1024]{1,0:T(8,128)(2,1)} %gates_ref.1, ...), custom_call_target="tpu_custom_call" | custom-call | flops 4026531840 | bytes 6291456 | tf_op jit(solution)/shard_map/conv/pallas_call | solution.py:108
  42.0 2.7 %collective-permute-done.6.refs_1_ = bf16[256,2048]{1,0:T(8,128)(2,1)} collective-permute-done((bf16[256,2048]{1,0:T(8,128)(2,1)S(1)}, bf16[256,2048]{1,0:T(8,128)(2,1)}, u32[]{:S(2)}, u32[]{:S(2)}) %collective-permute-start.6) | collective-permute-done | bytes 1048608 | tf_op jit(solution)/shard_map/ppermute | solution.py:36
  44.7 2.5 %collective-permute-done.8.refs_3_ = bf16[256,2048]{1,0:T(8,128)(2,1)} collective-permute-done((bf16[256,2048]{1,0:T(8,128)(2,1)}, bf16[256,2048]{1,0:T(8,128)(2,1)}, u32[]{:S(2)}, u32[]{:S(2)}) %collective-permute-start.8) | collective-permute-done | bytes 1048608 | tf_op jit(solution)/shard_map/ppermute | solution.py:36
  49.2 3.4 %all-to-all-start = ((bf16[4,32,1024]{2,1,0:T(8,128)(2,1)}), bf16[4,32,1024]{2,1,0:T(8,128)(2,1)S(1)}, u32[]{:S(2)}, u32[]{:S(2)}) async-start(bf16[4,32,1024]{2,1,0:T(8,128)(2,1)} %get-tuple-element.29.refs_4_), calls=%async_computation | async-start | bytes 524288 | tf_op jit(solution)/shard_map/all_to_all | solution.py:321
  52.7 5.7 %all-to-all-done.refs_0_ = bf16[4,32,1024]{2,1,0:T(8,128)(2,1)S(1)} async-done(((bf16[4,32,1024]{2,1,0:T(8,128)(2,1)}), bf16[4,32,1024]{2,1,0:T(8,128)(2,1)S(1)}, u32[]{:S(2)}, u32[]{:S(2)}) %all-to-all-start) | async-done | bytes 262176 | tf_op jit(solution)/shard_map/all_to_all | solution.py:321
  64.1 3.4 %all-to-all-start.1 = ((bf16[4,32,1024]{2,1,0:T(8,128)(2,1)}), bf16[4,32,1024]{2,1,0:T(8,128)(2,1)S(1)}, u32[]{:S(2)}, u32[]{:S(2)}) async-start(bf16[4,32,1024]{2,1,0:T(8,128)(2,1)} %get-tuple-element.42), calls=%async_computation.1 | async-start | bytes 524288 | tf_op jit(solution)/shard_map/all_to_all | solution.py:321
  69.0 2.7 %project.5 = (bf16[64,2048]{1,0:T(8,128)(2,1)}, f32[64,2048]{1,0:T(8,128)S(1)}) custom-call(bf16[32,1024]{1,0:T(8,128)(2,1)S(1)} %collective-permute-done.13.refs_0_, bf16[32,1024]{1,0:T(8,128)(2,1)} %collective-permute-done.14.refs_1_, bf16[32,1024]{1,0:T(8,128)(2,1)} %collective-permute-done.15.refs_2_, bf16[32,1024]{1,0:T(8,128)(2,1)S(1)} %get-tuple-element.37.refs_3_, ...), custom_call_target="tpu_custom_call" | custom-call | flops 536870912 | bytes 5767168 | tf_op jit(solution)/shard_map/project/pallas_call | solution.py:254
  73.4 1.9 %collective-permute-start.20 = (bf16[32,1024]{1,0:T(8,128)(2,1)S(1)}, bf16[32,1024]{1,0:T(8,128)(2,1)S(1)}, u32[]{:S(2)}, u32[]{:S(2)}) collective-permute-start(bf16[32,1024]{1,0:T(8,128)(2,1)S(1)} %get-tuple-element.43), channel_id=1, source_target_pairs={{0,24},{1,25},{2,26},{3,27},{4,28},{5,29},{6,30},{7,31},{8,16},{9,... | collective-permute-start | bytes 196616 | tf_op jit(solution)/shard_map/ppermute | solution.py:36
  76.0 1.9 %collective-permute-start.22 = (bf16[32,1024]{1,0:T(8,128)(2,1)S(1)}, bf16[32,1024]{1,0:T(8,128)(2,1)S(1)}, u32[]{:S(2)}, u32[]{:S(2)}) collective-permute-start(bf16[32,1024]{1,0:T(8,128)(2,1)S(1)} %get-tuple-element.45), channel_id=1, source_target_pairs={{0,16},{1,17},{2,18},{3,19},{4,20},{5,21},{6,22},{7,23},{8,24},{9,... | collective-permute-start | bytes 196616 | tf_op jit(solution)/shard_map/ppermute | solution.py:36
  77.9 3.0 %project.6 = (bf16[64,2048]{1,0:T(8,128)(2,1)S(1)}, f32[64,2048]{1,0:T(8,128)S(1)}) custom-call(bf16[32,1024]{1,0:T(8,128)(2,1)S(1)} %collective-permute-done.13.refs_0_, bf16[32,1024]{1,0:T(8,128)(2,1)} %collective-permute-done.14.refs_1_, bf16[32,1024]{1,0:T(8,128)(2,1)} %collective-permute-done.15.refs_2_, ...), custom_call_target="tpu_custom_call" | custom-call | flops 536870912 | bytes 5767168 | tf_op jit(solution)/shard_map/project/pallas_call | solution.py:254
  82.6 2.1 %collective-permute-done.21.refs_1_ = bf16[32,1024]{1,0:T(8,128)(2,1)S(1)} collective-permute-done((bf16[32,1024]{1,0:T(8,128)(2,1)S(1)}, bf16[32,1024]{1,0:T(8,128)(2,1)S(1)}, u32[]{:S(2)}, u32[]{:S(2)}) %collective-permute-start.21) | collective-permute-done | bytes 65568 | tf_op jit(solution)/shard_map/ppermute | solution.py:36
  84.7 3.0 %project.9 = (bf16[64,2048]{1,0:T(8,128)(2,1)S(1)}, f32[64,2048]{1,0:T(8,128)S(1)}) custom-call(bf16[32,1024]{1,0:T(8,128)(2,1)S(1)} %collective-permute-done.20.refs_0_, bf16[32,1024]{1,0:T(8,128)(2,1)S(1)} %collective-permute-done.21.refs_1_, bf16[32,1024]{1,0:T(8,128)(2,1)S(1)} %collective-permute-done.22.refs_2_, ...), custom_call_target="tpu_custom_call" | custom-call | flops 536870912 | bytes 5767168 | tf_op jit(solution)/shard_map/project/pallas_call | solution.py:254
  93.1 1.7 %project.7 = (bf16[64,1024]{1,0:T(8,128)(2,1)S(1)}, f32[64,1024]{1,0:T(8,128)S(1)}) custom-call(bf16[32,1024]{1,0:T(8,128)(2,1)S(1)} %collective-permute-done.20.refs_0_, bf16[32,1024]{1,0:T(8,128)(2,1)S(1)} %collective-permute-done.21.refs_1_, bf16[32,1024]{1,0:T(8,128)(2,1)S(1)} %collective-permute-done.22.refs_2_, ...), custom_call_target="tpu_custom_call" | custom-call | flops 268435456 | bytes 2883584 | tf_op jit(solution)/shard_map/project/pallas_call | solution.py:254
  94.8 2.4 %collective-permute-start.23 = (bf16[64,1024]{1,0:T(8,128)(2,1)S(1)}, bf16[64,1024]{1,0:T(8,128)(2,1)S(1)}, u32[]{:S(2)}, u32[]{:S(2)}) collective-permute-start(bf16[64,1024]{1,0:T(8,128)(2,1)S(1)} %get-tuple-element.48), channel_id=1, source_target_pairs={{0,8},{1,9},{2,10},{3,11},{4,12},{5,13},{6,14},{7,15},{8,0},{9,1},... | collective-permute-start | bytes 393224 | tf_op jit(solution)/shard_map/ppermute | solution.py:36
  99.0 2.5 %collective-permute-done.27 = bf16[64,2048]{1,0:T(8,128)(2,1)S(1)} collective-permute-done((bf16[64,2048]{1,0:T(8,128)(2,1)S(1)}, bf16[64,2048]{1,0:T(8,128)(2,1)S(1)}, u32[]{:S(2)}, u32[]{:S(2)}) %collective-permute-start.27) | collective-permute-done | bytes 262176 | tf_op jit(solution)/shard_map/ppermute | solution.py:36
  102.6 2.2 %collective-permute-done.23 = bf16[64,1024]{1,0:T(8,128)(2,1)S(1)} collective-permute-done((bf16[64,1024]{1,0:T(8,128)(2,1)S(1)}, bf16[64,1024]{1,0:T(8,128)(2,1)S(1)}, u32[]{:S(2)}, u32[]{:S(2)}) %collective-permute-start.23) | collective-permute-done | bytes 131104 | tf_op jit(solution)/shard_map/ppermute | solution.py:36
  104.8 2.1 %collective-permute-start.24 = (bf16[32,1024]{1,0:T(8,128)(2,1)S(1)}, bf16[32,1024]{1,0:T(8,128)(2,1)S(1)}, u32[]{:S(2)}, u32[]{:S(2)}) collective-permute-start(bf16[32,1024]{1,0:T(8,128)(2,1)S(1)} %fusion.12), channel_id=1, source_target_pairs={{0,16},{1,17},{2,18},{3,19},{4,20},{5,21},{6,22},{7,23},{8,24},{9,... | collective-permute-start | bytes 196616 | tf_op jit(solution)/shard_map/ppermute | solution.py:36
  106.9 1.8 %collective-permute-done.25 = bf16[64,1024]{1,0:T(8,128)(2,1)S(1)} collective-permute-done((bf16[64,1024]{1,0:T(8,128)(2,1)S(1)}, bf16[64,1024]{1,0:T(8,128)(2,1)S(1)}, u32[]{:S(2)}, u32[]{:S(2)}) %collective-permute-start.25) | collective-permute-done | bytes 131104 | tf_op jit(solution)/shard_map/ppermute | solution.py:36
  108.9 2.8 %collective-permute-done.28 = bf16[32,2048]{1,0:T(8,128)(2,1)S(1)} collective-permute-done((bf16[32,2048]{1,0:T(8,128)(2,1)S(1)}, bf16[32,2048]{1,0:T(8,128)(2,1)S(1)}, u32[]{:S(2)}, u32[]{:S(2)}) %collective-permute-start.28) | collective-permute-done | bytes 131104 | tf_op jit(solution)/shard_map/ppermute | solution.py:36
  (86 shorter events, 36.2 us)
Async XLA Ops:
  0.0 16.4 %collective-permute-start = (bf16[256,1024]{1,0:T(8,128)(2,1)}, bf16[256,1024]{1,0:T(8,128)(2,1)S(1)}, u32[]{:S(2)}, u32[]{:S(2)}) collective-permute-start(bf16[256,1024]{1,0:T(8,128)(2,1)} %rest_0_.1), channel_id=1, source_target_pairs={{0,8},{1,9},{2,10},{3,11},{4,12},{5,13},{6,14},{7,15},{8,16},{9,17... | collective-permute-start | bytes 1572872 | tf_op jit(solution)/shard_map/ppermute | solution.py:36
  6.2 14.5 %collective-permute-start.5 = (bf16[128,2048]{1,0:T(8,128)(2,1)S(1)}, bf16[128,2048]{1,0:T(8,128)(2,1)S(1)}, u32[]{:S(2)}, u32[]{:S(2)}) collective-permute-start(bf16[128,2048]{1,0:T(8,128)(2,1)S(1)} %join.4.refs_0_), channel_id=1, source_target_pairs={{0,1},{1,0},{2,3},{3,2},{4,5},{5,4},{6,7},{7,6},{8,9},{9,8},{10,11... | collective-permute-start | bytes 1572872 | tf_op jit(solution)/shard_map/ppermute | solution.py:36
  7.8 14.6 %collective-permute-start.7 = (bf16[128,2048]{1,0:T(8,128)(2,1)S(1)}, bf16[128,2048]{1,0:T(8,128)(2,1)S(1)}, u32[]{:S(2)}, u32[]{:S(2)}) collective-permute-start(bf16[128,2048]{1,0:T(8,128)(2,1)S(1)} %join.6.refs_0_), channel_id=1, source_target_pairs={{0,2},{1,3},{2,0},{3,1},{4,6},{5,7},{6,4},{7,5},{8,10},{9,11},{10,... | collective-permute-start | bytes 1572872 | tf_op jit(solution)/shard_map/ppermute | solution.py:36
  16.4 14.6 %collective-permute-start.1 = (bf16[256,1024]{1,0:T(8,128)(2,1)S(1)}, bf16[256,1024]{1,0:T(8,128)(2,1)S(1)}, u32[]{:S(2)}, u32[]{:S(2)}) collective-permute-start(bf16[256,1024]{1,0:T(8,128)(2,1)S(1)} %collective-permute-done.rest_1_), channel_id=1, source_target_pairs={{0,8},{1,9},{2,10},{3,11},{4,12},{5,13},{6,14},{7,15},{8,16},{9,17... | collective-permute-start | bytes 1572872 | tf_op jit(solution)/shard_map/ppermute | solution.py:36
  20.8 23.9 %collective-permute-start.6 = (bf16[256,2048]{1,0:T(8,128)(2,1)S(1)}, bf16[256,2048]{1,0:T(8,128)(2,1)}, u32[]{:S(2)}, u32[]{:S(2)}) collective-permute-start(bf16[256,2048]{1,0:T(8,128)(2,1)S(1)} %join.5.refs_0_), channel_id=1, source_target_pairs={{0,2},{1,3},{2,0},{3,1},{4,6},{5,7},{6,4},{7,5},{8,10},{9,11},{10,... | collective-permute-start | bytes 3145736 | tf_op jit(solution)/shard_map/ppermute | solution.py:36
  23.4 23.8 %collective-permute-start.8 = (bf16[256,2048]{1,0:T(8,128)(2,1)}, bf16[256,2048]{1,0:T(8,128)(2,1)}, u32[]{:S(2)}, u32[]{:S(2)}) collective-permute-start(bf16[256,2048]{1,0:T(8,128)(2,1)} %join.7.refs_2_), channel_id=1, source_target_pairs={{0,1},{1,0},{2,3},{3,2},{4,5},{5,4},{6,7},{7,6},{8,9},{9,8},{10,11... | collective-permute-start | bytes 3145736 | tf_op jit(solution)/shard_map/ppermute | solution.py:36
  48.2 10.2 %collective-permute-start.10 = (bf16[256,2048]{1,0:T(8,128)(2,1)}, bf16[256,2048]{1,0:T(8,128)(2,1)S(1)}, u32[]{:S(2)}, u32[]{:S(2)}) collective-permute-start(bf16[256,2048]{1,0:T(8,128)(2,1)} %get-tuple-element.31.refs_5_), channel_id=1, source_target_pairs={{0,4},{1,5},{2,6},{3,7},{4,0},{5,1},{6,2},{7,3},{8,12},{9,13},{10,... | collective-permute-start | bytes 3145736 | tf_op jit(solution)/shard_map/ppermute | solution.py:36
  48.2 10.2 %collective-permute-start.11 = (bf16[256,2048]{1,0:T(8,128)(2,1)}, bf16[256,2048]{1,0:T(8,128)(2,1)}, u32[]{:S(2)}, u32[]{:S(2)}) collective-permute-start(bf16[256,2048]{1,0:T(8,128)(2,1)} %get-tuple-element.32.refs_4_), channel_id=1, source_target_pairs={{0,4},{1,5},{2,6},{3,7},{4,0},{5,1},{6,2},{7,3},{8,12},{9,13},{10,... | collective-permute-start | bytes 3145736 | tf_op jit(solution)/shard_map/ppermute | solution.py:36
  48.7 9.7 %collective-permute-start.12 = (bf16[256,2048]{1,0:T(8,128)(2,1)}, bf16[256,2048]{1,0:T(8,128)(2,1)}, u32[]{:S(2)}, u32[]{:S(2)}) collective-permute-start(bf16[256,2048]{1,0:T(8,128)(2,1)} %get-tuple-element.33.refs_5_), channel_id=1, source_target_pairs={{0,4},{1,5},{2,6},{3,7},{4,0},{5,1},{6,2},{7,3},{8,12},{9,13},{10,... | collective-permute-start | bytes 3145736 | tf_op jit(solution)/shard_map/ppermute | solution.py:36
  48.7 9.7 %collective-permute-start.9 = (bf16[256,2048]{1,0:T(8,128)(2,1)S(1)}, bf16[256,2048]{1,0:T(8,128)(2,1)S(1)}, u32[]{:S(2)}, u32[]{:S(2)}) collective-permute-start(bf16[256,2048]{1,0:T(8,128)(2,1)S(1)} %get-tuple-element.30.refs_4_), channel_id=1, source_target_pairs={{0,4},{1,5},{2,6},{3,7},{4,0},{5,1},{6,2},{7,3},{8,12},{9,13},{10,... | collective-permute-start | bytes 3145736 | tf_op jit(solution)/shard_map/ppermute | solution.py:36
  49.2 9.2 %all-to-all-start = ((bf16[4,32,1024]{2,1,0:T(8,128)(2,1)}), bf16[4,32,1024]{2,1,0:T(8,128)(2,1)S(1)}, u32[]{:S(2)}, u32[]{:S(2)}) async-start(bf16[4,32,1024]{2,1,0:T(8,128)(2,1)} %get-tuple-element.29.refs_4_), calls=%async_computation | async-start | bytes 524288 | tf_op jit(solution)/shard_map/all_to_all | solution.py:321
  64.1 8.8 %all-to-all-start.1 = ((bf16[4,32,1024]{2,1,0:T(8,128)(2,1)}), bf16[4,32,1024]{2,1,0:T(8,128)(2,1)S(1)}, u32[]{:S(2)}, u32[]{:S(2)}) async-start(bf16[4,32,1024]{2,1,0:T(8,128)(2,1)} %get-tuple-element.42), calls=%async_computation.1 | async-start | bytes 524288 | tf_op jit(solution)/shard_map/all_to_all | solution.py:321
  72.5 16.5 %collective-permute-start.16 = (bf16[64,2048]{1,0:T(8,128)(2,1)}, bf16[64,2048]{1,0:T(8,128)(2,1)}, u32[]{:S(2)}, u32[]{:S(2)}) collective-permute-start(bf16[64,2048]{1,0:T(8,128)(2,1)} %get-tuple-element.39), channel_id=1, source_target_pairs={{0,8},{1,9},{2,10},{3,11},{4,12},{5,13},{6,14},{7,15},{8,0},{9,1},... | collective-permute-start | bytes 786440 | tf_op jit(solution)/shard_map/ppermute | solution.py:36
  73.4 9.1 %collective-permute-start.20 = (bf16[32,1024]{1,0:T(8,128)(2,1)S(1)}, bf16[32,1024]{1,0:T(8,128)(2,1)S(1)}, u32[]{:S(2)}, u32[]{:S(2)}) collective-permute-start(bf16[32,1024]{1,0:T(8,128)(2,1)S(1)} %get-tuple-element.43), channel_id=1, source_target_pairs={{0,24},{1,25},{2,26},{3,27},{4,28},{5,29},{6,30},{7,31},{8,16},{9,... | collective-permute-start | bytes 196616 | tf_op jit(solution)/shard_map/ppermute | solution.py:36
  75.3 9.4 %collective-permute-start.21 = (bf16[32,1024]{1,0:T(8,128)(2,1)S(1)}, bf16[32,1024]{1,0:T(8,128)(2,1)S(1)}, u32[]{:S(2)}, u32[]{:S(2)}) collective-permute-start(bf16[32,1024]{1,0:T(8,128)(2,1)S(1)} %get-tuple-element.44), channel_id=1, source_target_pairs={{0,8},{1,9},{2,10},{3,11},{4,12},{5,13},{6,14},{7,15},{8,0},{9,1},... | collective-permute-start | bytes 196616 | tf_op jit(solution)/shard_map/ppermute | solution.py:36
  76.0 8.7 %collective-permute-start.22 = (bf16[32,1024]{1,0:T(8,128)(2,1)S(1)}, bf16[32,1024]{1,0:T(8,128)(2,1)S(1)}, u32[]{:S(2)}, u32[]{:S(2)}) collective-permute-start(bf16[32,1024]{1,0:T(8,128)(2,1)S(1)} %get-tuple-element.45), channel_id=1, source_target_pairs={{0,16},{1,17},{2,18},{3,19},{4,20},{5,21},{6,22},{7,23},{8,24},{9,... | collective-permute-start | bytes 196616 | tf_op jit(solution)/shard_map/ppermute | solution.py:36
  80.9 11.1 %collective-permute-start.18 = (bf16[64,2048]{1,0:T(8,128)(2,1)S(1)}, bf16[64,2048]{1,0:T(8,128)(2,1)S(1)}, u32[]{:S(2)}, u32[]{:S(2)}) collective-permute-start(bf16[64,2048]{1,0:T(8,128)(2,1)S(1)} %get-tuple-element.41), channel_id=1, source_target_pairs={{0,8},{1,9},{2,10},{3,11},{4,12},{5,13},{6,14},{7,15},{8,0},{9,1},... | collective-permute-start | bytes 786440 | tf_op jit(solution)/shard_map/ppermute | solution.py:36
  87.6 13.9 %collective-permute-start.27 = (bf16[64,2048]{1,0:T(8,128)(2,1)S(1)}, bf16[64,2048]{1,0:T(8,128)(2,1)S(1)}, u32[]{:S(2)}, u32[]{:S(2)}) collective-permute-start(bf16[64,2048]{1,0:T(8,128)(2,1)S(1)} %get-tuple-element.52), channel_id=1, source_target_pairs={{0,8},{1,9},{2,10},{3,11},{4,12},{5,13},{6,14},{7,15},{8,0},{9,1},... | collective-permute-start | bytes 786440 | tf_op jit(solution)/shard_map/ppermute | solution.py:36
  90.0 18.8 %collective-permute-start.17 = (bf16[32,2048]{1,0:T(8,128)(2,1)S(1)}, bf16[32,2048]{1,0:T(8,128)(2,1)S(1)}, u32[]{:S(2)}, u32[]{:S(2)}) collective-permute-start(bf16[32,2048]{1,0:T(8,128)(2,1)S(1)} %fusion.6.refs_8_), channel_id=1, source_target_pairs={{0,16},{1,17},{2,18},{3,19},{4,20},{5,21},{6,22},{7,23},{8,24},{9,... | collective-permute-start | bytes 393224 | tf_op jit(solution)/shard_map/ppermute | solution.py:36
  92.0 16.9 %collective-permute-start.19 = (bf16[32,2048]{1,0:T(8,128)(2,1)S(1)}, bf16[32,2048]{1,0:T(8,128)(2,1)S(1)}, u32[]{:S(2)}, u32[]{:S(2)}) collective-permute-start(bf16[32,2048]{1,0:T(8,128)(2,1)S(1)} %fusion.3), channel_id=1, source_target_pairs={{0,16},{1,17},{2,18},{3,19},{4,20},{5,21},{6,22},{7,23},{8,24},{9,... | collective-permute-start | bytes 393224 | tf_op jit(solution)/shard_map/ppermute | solution.py:36
  94.8 9.9 %collective-permute-start.23 = (bf16[64,1024]{1,0:T(8,128)(2,1)S(1)}, bf16[64,1024]{1,0:T(8,128)(2,1)S(1)}, u32[]{:S(2)}, u32[]{:S(2)}) collective-permute-start(bf16[64,1024]{1,0:T(8,128)(2,1)S(1)} %get-tuple-element.48), channel_id=1, source_target_pairs={{0,8},{1,9},{2,10},{3,11},{4,12},{5,13},{6,14},{7,15},{8,0},{9,1},... | collective-permute-start | bytes 393224 | tf_op jit(solution)/shard_map/ppermute | solution.py:36
  98.9 9.8 %collective-permute-start.25 = (bf16[64,1024]{1,0:T(8,128)(2,1)S(1)}, bf16[64,1024]{1,0:T(8,128)(2,1)S(1)}, u32[]{:S(2)}, u32[]{:S(2)}) collective-permute-start(bf16[64,1024]{1,0:T(8,128)(2,1)S(1)} %get-tuple-element.50), channel_id=1, source_target_pairs={{0,8},{1,9},{2,10},{3,11},{4,12},{5,13},{6,14},{7,15},{8,0},{9,1},... | collective-permute-start | bytes 393224 | tf_op jit(solution)/shard_map/ppermute | solution.py:36
  101.6 10.1 %collective-permute-start.28 = (bf16[32,2048]{1,0:T(8,128)(2,1)S(1)}, bf16[32,2048]{1,0:T(8,128)(2,1)S(1)}, u32[]{:S(2)}, u32[]{:S(2)}) collective-permute-start(bf16[32,2048]{1,0:T(8,128)(2,1)S(1)} %fusion), channel_id=1, source_target_pairs={{0,16},{1,17},{2,18},{3,19},{4,20},{5,21},{6,22},{7,23},{8,24},{9,... | collective-permute-start | bytes 393224 | tf_op jit(solution)/shard_map/ppermute | solution.py:36
  104.8 8.5 %collective-permute-start.24 = (bf16[32,1024]{1,0:T(8,128)(2,1)S(1)}, bf16[32,1024]{1,0:T(8,128)(2,1)S(1)}, u32[]{:S(2)}, u32[]{:S(2)}) collective-permute-start(bf16[32,1024]{1,0:T(8,128)(2,1)S(1)} %fusion.12), channel_id=1, source_target_pairs={{0,16},{1,17},{2,18},{3,19},{4,20},{5,21},{6,22},{7,23},{8,24},{9,... | collective-permute-start | bytes 196616 | tf_op jit(solution)/shard_map/ppermute | solution.py:36
  (15 other events, 84.5 us)

commit v7 on v6

--- a/solution.py
+++ b/solution.py
@@ -248,7 +248,7 @@
 def project(acts, pieces, spots, width, cols, deps):
     rows, depth = acts[0].shape
     count = rows * len(acts)
-    tile = min(cols, 512)
+    tile = min(cols, 1024)
     firsts = [first for _, first in pieces]
     held = pl.BlockSpec(memory_space=pltpu.VMEM)
     return pl.pallas_call(

time: 115 us -> 115 us (level)
  no operation moved by 1% of the time
where the time goes in v7:
time: 115 us
  starting transfers between devices  44.6 us (39%)
  waiting for transfers between devices  42.4 us (37%)
  Pallas kernels  22.2 us (19%)
  local copies, waits for them, and re-layouts  3.07 us (3%)
  other arithmetic  2.2 us (2%)
    ppermute x29, starting transfers between devices, permute(): return lax.ppermute(value, AXES, route)  37.8 us
    ppermute x29, waiting for transfers between devices, permute(): return lax.ppermute(value, AXES, route)  36.4 us
    pallas_call x5, Pallas kernels, project(): pl.pallas_call(functools.partial(project_kernel, len(acts), firsts, tile,...  12 us
    pallas_call x1, Pallas kernels, convolve(): pl.pallas_call(functools.partial(conv_kernel, lags), grid_spec=pltpu.Pref...  7.13 us
    all_to_all x2, starting transfers between devices, body(): lax.all_to_all(some, 'chan', split_axis=0, concat_axis=0)  6.81 us
    all_to_all x2, waiting for transfers between devices, body(): lax.all_to_all(some, 'chan', split_axis=0, concat_axis=0)  5.97 us
    unnamed x16, local copies, waits for them, and re-layouts  2.98 us
  transfers between devices with their start and end apart: 31, of which 17 were waited for; matrix products, arithmetic and copies ran while one was open for 1% of the time, Pallas kernels for 18%

profile of v7, /device:TPU:0, one launch (start us, length us, event | category | flops | bytes accessed | tf_op | source)
XLA Modules:
  0.0 114.8 jit_solution(9637989817310870494)
XLA Ops:
  0.0 5.0 %collective-permute-start = (bf16[256,1024]{1,0:T(8,128)(2,1)}, bf16[256,1024]{1,0:T(8,128)(2,1)S(1)}, u32[]{:S(2)}, u32[]{:S(2)}) collective-permute-start(bf16[256,1024]{1,0:T(8,128)(2,1)} %rest_0_.1), channel_id=1, source_target_pairs={{0,8},{1,9},{2,10},{3,11},{4,12},{5,13},{6,14},{7,15},{8,16},{9,17... | collective-permute-start | bytes 1572872 | tf_op jit(solution)/shard_map/ppermute | solution.py:36
  9.4 7.0 %collective-permute-done.rest_1_ = bf16[256,1024]{1,0:T(8,128)(2,1)S(1)} collective-permute-done((bf16[256,1024]{1,0:T(8,128)(2,1)}, bf16[256,1024]{1,0:T(8,128)(2,1)S(1)}, u32[]{:S(2)}, u32[]{:S(2)}) %collective-permute-start) | collective-permute-done | bytes 524320 | tf_op jit(solution)/shard_map/ppermute | solution.py:36
  16.4 4.3 %collective-permute-start.1 = (bf16[256,1024]{1,0:T(8,128)(2,1)S(1)}, bf16[256,1024]{1,0:T(8,128)(2,1)S(1)}, u32[]{:S(2)}, u32[]{:S(2)}) collective-permute-start(bf16[256,1024]{1,0:T(8,128)(2,1)S(1)} %collective-permute-done.rest_1_), channel_id=1, source_target_pairs={{0,8},{1,9},{2,10},{3,11},{4,12},{5,13},{6,14},{7,15},{8,16},{9,17... | collective-permute-start | bytes 1572872 | tf_op jit(solution)/shard_map/ppermute | solution.py:36
  26.3 4.6 %collective-permute-done.1.rest_2_ = bf16[256,1024]{1,0:T(8,128)(2,1)S(1)} collective-permute-done((bf16[256,1024]{1,0:T(8,128)(2,1)S(1)}, bf16[256,1024]{1,0:T(8,128)(2,1)S(1)}, u32[]{:S(2)}, u32[]{:S(2)}) %collective-permute-start.1) | collective-permute-done | bytes 524320 | tf_op jit(solution)/shard_map/ppermute | solution.py:36
  32.3 2.6 %collective-permute-done.4.rest_5_ = bf16[256,1024]{1,0:T(8,128)(2,1)} collective-permute-done((bf16[256,1024]{1,0:T(8,128)(2,1)S(1)}, bf16[256,1024]{1,0:T(8,128)(2,1)}, u32[]{:S(2)}, u32[]{:S(2)}) %collective-permute-start.4) | collective-permute-done | bytes 524320 | tf_op jit(solution)/shard_map/ppermute | solution.py:36
  34.9 7.1 %conv.1 = (bf16[4,32,1024]{2,1,0:T(8,128)(2,1)}, bf16[4,32,1024]{2,1,0:T(8,128)(2,1)}) custom-call(s32[1]{0:T(128)} %bitcast.9.core_ref, bf16[512,256]{1,0:T(8,128)(2,1)} %constant.42.clone.table_ref, bf16[256,512]{1,0:T(8,128)(2,1)} %constant.43.clone.back_ref, f32[1,1024]{1,0:T(1,128)} %bitcast.11, bf16[256,1024]{1,0:T(8,128)(2,1)} %gates_ref.1, ...), custom_call_target="tpu_custom_call" | custom-call | flops 4026531840 | bytes 6291456 | tf_op jit(solution)/shard_map/conv/pallas_call | solution.py:108
  42.0 2.7 %collective-permute-done.6.refs_1_ = bf16[256,2048]{1,0:T(8,128)(2,1)} collective-permute-done((bf16[256,2048]{1,0:T(8,128)(2,1)S(1)}, bf16[256,2048]{1,0:T(8,128)(2,1)}, u32[]{:S(2)}, u32[]{:S(2)}) %collective-permute-start.6) | collective-permute-done | bytes 1048608 | tf_op jit(solution)/shard_map/ppermute | solution.py:36
  44.7 2.5 %collective-permute-done.8.refs_3_ = bf16[256,2048]{1,0:T(8,128)(2,1)} collective-permute-done((bf16[256,2048]{1,0:T(8,128)(2,1)}, bf16[256,2048]{1,0:T(8,128)(2,1)}, u32[]{:S(2)}, u32[]{:S(2)}) %collective-permute-start.8) | collective-permute-done | bytes 1048608 | tf_op jit(solution)/shard_map/ppermute | solution.py:36
  49.2 3.4 %all-to-all-start = ((bf16[4,32,1024]{2,1,0:T(8,128)(2,1)}), bf16[4,32,1024]{2,1,0:T(8,128)(2,1)S(1)}, u32[]{:S(2)}, u32[]{:S(2)}) async-start(bf16[4,32,1024]{2,1,0:T(8,128)(2,1)} %get-tuple-element.29.refs_4_), calls=%async_computation | async-start | bytes 524288 | tf_op jit(solution)/shard_map/all_to_all | solution.py:321
  52.7 5.7 %all-to-all-done.refs_0_ = bf16[4,32,1024]{2,1,0:T(8,128)(2,1)S(1)} async-done(((bf16[4,32,1024]{2,1,0:T(8,128)(2,1)}), bf16[4,32,1024]{2,1,0:T(8,128)(2,1)S(1)}, u32[]{:S(2)}, u32[]{:S(2)}) %all-to-all-start) | async-done | bytes 262176 | tf_op jit(solution)/shard_map/all_to_all | solution.py:321
  64.1 3.4 %all-to-all-start.1 = ((bf16[4,32,1024]{2,1,0:T(8,128)(2,1)}), bf16[4,32,1024]{2,1,0:T(8,128)(2,1)S(1)}, u32[]{:S(2)}, u32[]{:S(2)}) async-start(bf16[4,32,1024]{2,1,0:T(8,128)(2,1)} %get-tuple-element.42), calls=%async_computation.1 | async-start | bytes 524288 | tf_op jit(solution)/shard_map/all_to_all | solution.py:321
  69.0 2.7 %project.5 = (bf16[64,2048]{1,0:T(8,128)(2,1)}, f32[64,2048]{1,0:T(8,128)S(1)}) custom-call(bf16[32,1024]{1,0:T(8,128)(2,1)S(1)} %collective-permute-done.13.refs_0_, bf16[32,1024]{1,0:T(8,128)(2,1)} %collective-permute-done.14.refs_1_, bf16[32,1024]{1,0:T(8,128)(2,1)} %collective-permute-done.15.refs_2_, bf16[32,1024]{1,0:T(8,128)(2,1)S(1)} %get-tuple-element.37.refs_3_, ...), custom_call_target="tpu_custom_call" | custom-call | flops 536870912 | bytes 5767168 | tf_op jit(solution)/shard_map/project/pallas_call | solution.py:254
  73.4 1.9 %collective-permute-start.20 = (bf16[32,1024]{1,0:T(8,128)(2,1)S(1)}, bf16[32,1024]{1,0:T(8,128)(2,1)S(1)}, u32[]{:S(2)}, u32[]{:S(2)}) collective-permute-start(bf16[32,1024]{1,0:T(8,128)(2,1)S(1)} %get-tuple-element.43), channel_id=1, source_target_pairs={{0,24},{1,25},{2,26},{3,27},{4,28},{5,29},{6,30},{7,31},{8,16},{9,... | collective-permute-start | bytes 196616 | tf_op jit(solution)/shard_map/ppermute | solution.py:36
  76.0 1.9 %collective-permute-start.22 = (bf16[32,1024]{1,0:T(8,128)(2,1)S(1)}, bf16[32,1024]{1,0:T(8,128)(2,1)S(1)}, u32[]{:S(2)}, u32[]{:S(2)}) collective-permute-start(bf16[32,1024]{1,0:T(8,128)(2,1)S(1)} %get-tuple-element.45), channel_id=1, source_target_pairs={{0,16},{1,17},{2,18},{3,19},{4,20},{5,21},{6,22},{7,23},{8,24},{9,... | collective-permute-start | bytes 196616 | tf_op jit(solution)/shard_map/ppermute | solution.py:36
  77.9 3.0 %project.6 = (bf16[64,2048]{1,0:T(8,128)(2,1)S(1)}, f32[64,2048]{1,0:T(8,128)S(1)}) custom-call(bf16[32,1024]{1,0:T(8,128)(2,1)S(1)} %collective-permute-done.13.refs_0_, bf16[32,1024]{1,0:T(8,128)(2,1)} %collective-permute-done.14.refs_1_, bf16[32,1024]{1,0:T(8,128)(2,1)} %collective-permute-done.15.refs_2_, ...), custom_call_target="tpu_custom_call" | custom-call | flops 536870912 | bytes 5767168 | tf_op jit(solution)/shard_map/project/pallas_call | solution.py:254
  82.6 2.1 %collective-permute-done.21.refs_1_ = bf16[32,1024]{1,0:T(8,128)(2,1)S(1)} collective-permute-done((bf16[32,1024]{1,0:T(8,128)(2,1)S(1)}, bf16[32,1024]{1,0:T(8,128)(2,1)S(1)}, u32[]{:S(2)}, u32[]{:S(2)}) %collective-permute-start.21) | collective-permute-done | bytes 65568 | tf_op jit(solution)/shard_map/ppermute | solution.py:36
  84.7 3.0 %project.9 = (bf16[64,2048]{1,0:T(8,128)(2,1)S(1)}, f32[64,2048]{1,0:T(8,128)S(1)}) custom-call(bf16[32,1024]{1,0:T(8,128)(2,1)S(1)} %collective-permute-done.20.refs_0_, bf16[32,1024]{1,0:T(8,128)(2,1)S(1)} %collective-permute-done.21.refs_1_, bf16[32,1024]{1,0:T(8,128)(2,1)S(1)} %collective-permute-done.22.refs_2_, ...), custom_call_target="tpu_custom_call" | custom-call | flops 536870912 | bytes 5767168 | tf_op jit(solution)/shard_map/project/pallas_call | solution.py:254
  93.1 1.7 %project.7 = (bf16[64,1024]{1,0:T(8,128)(2,1)S(1)}, f32[64,1024]{1,0:T(8,128)S(1)}) custom-call(bf16[32,1024]{1,0:T(8,128)(2,1)S(1)} %collective-permute-done.20.refs_0_, bf16[32,1024]{1,0:T(8,128)(2,1)S(1)} %collective-permute-done.21.refs_1_, bf16[32,1024]{1,0:T(8,128)(2,1)S(1)} %collective-permute-done.22.refs_2_, ...), custom_call_target="tpu_custom_call" | custom-call | flops 268435456 | bytes 2883584 | tf_op jit(solution)/shard_map/project/pallas_call | solution.py:254
  94.8 2.4 %collective-permute-start.23 = (bf16[64,1024]{1,0:T(8,128)(2,1)S(1)}, bf16[64,1024]{1,0:T(8,128)(2,1)S(1)}, u32[]{:S(2)}, u32[]{:S(2)}) collective-permute-start(bf16[64,1024]{1,0:T(8,128)(2,1)S(1)} %get-tuple-element.48), channel_id=1, source_target_pairs={{0,8},{1,9},{2,10},{3,11},{4,12},{5,13},{6,14},{7,15},{8,0},{9,1},... | collective-permute-start | bytes 393224 | tf_op jit(solution)/shard_map/ppermute | solution.py:36
  99.0 2.5 %collective-permute-done.27 = bf16[64,2048]{1,0:T(8,128)(2,1)S(1)} collective-permute-done((bf16[64,2048]{1,0:T(8,128)(2,1)S(1)}, bf16[64,2048]{1,0:T(8,128)(2,1)S(1)}, u32[]{:S(2)}, u32[]{:S(2)}) %collective-permute-start.27) | collective-permute-done | bytes 262176 | tf_op jit(solution)/shard_map/ppermute | solution.py:36
  102.6 2.2 %collective-permute-done.23 = bf16[64,1024]{1,0:T(8,128)(2,1)S(1)} collective-permute-done((bf16[64,1024]{1,0:T(8,128)(2,1)S(1)}, bf16[64,1024]{1,0:T(8,128)(2,1)S(1)}, u32[]{:S(2)}, u32[]{:S(2)}) %collective-permute-start.23) | collective-permute-done | bytes 131104 | tf_op jit(solution)/shard_map/ppermute | solution.py:36
  104.8 2.1 %collective-permute-start.24 = (bf16[32,1024]{1,0:T(8,128)(2,1)S(1)}, bf16[32,1024]{1,0:T(8,128)(2,1)S(1)}, u32[]{:S(2)}, u32[]{:S(2)}) collective-permute-start(bf16[32,1024]{1,0:T(8,128)(2,1)S(1)} %fusion.12), channel_id=1, source_target_pairs={{0,16},{1,17},{2,18},{3,19},{4,20},{5,21},{6,22},{7,23},{8,24},{9,... | collective-permute-start | bytes 196616 | tf_op jit(solution)/shard_map/ppermute | solution.py:36
  106.9 1.8 %collective-permute-done.25 = bf16[64,1024]{1,0:T(8,128)(2,1)S(1)} collective-permute-done((bf16[64,1024]{1,0:T(8,128)(2,1)S(1)}, bf16[64,1024]{1,0:T(8,128)(2,1)S(1)}, u32[]{:S(2)}, u32[]{:S(2)}) %collective-permute-start.25) | collective-permute-done | bytes 131104 | tf_op jit(solution)/shard_map/ppermute | solution.py:36
  108.9 2.8 %collective-permute-done.28 = bf16[32,2048]{1,0:T(8,128)(2,1)S(1)} collective-permute-done((bf16[32,2048]{1,0:T(8,128)(2,1)S(1)}, bf16[32,2048]{1,0:T(8,128)(2,1)S(1)}, u32[]{:S(2)}, u32[]{:S(2)}) %collective-permute-start.28) | collective-permute-done | bytes 131104 | tf_op jit(solution)/shard_map/ppermute | solution.py:36
  (86 shorter events, 36.2 us)
Async XLA Ops:
  0.0 16.4 %collective-permute-start = (bf16[256,1024]{1,0:T(8,128)(2,1)}, bf16[256,1024]{1,0:T(8,128)(2,1)S(1)}, u32[]{:S(2)}, u32[]{:S(2)}) collective-permute-start(bf16[256,1024]{1,0:T(8,128)(2,1)} %rest_0_.1), channel_id=1, source_target_pairs={{0,8},{1,9},{2,10},{3,11},{4,12},{5,13},{6,14},{7,15},{8,16},{9,17... | collective-permute-start | bytes 1572872 | tf_op jit(solution)/shard_map/ppermute | solution.py:36
  6.2 14.5 %collective-permute-start.5 = (bf16[128,2048]{1,0:T(8,128)(2,1)S(1)}, bf16[128,2048]{1,0:T(8,128)(2,1)S(1)}, u32[]{:S(2)}, u32[]{:S(2)}) collective-permute-start(bf16[128,2048]{1,0:T(8,128)(2,1)S(1)} %join.4.refs_0_), channel_id=1, source_target_pairs={{0,1},{1,0},{2,3},{3,2},{4,5},{5,4},{6,7},{7,6},{8,9},{9,8},{10,11... | collective-permute-start | bytes 1572872 | tf_op jit(solution)/shard_map/ppermute | solution.py:36
  7.8 14.6 %collective-permute-start.7 = (bf16[128,2048]{1,0:T(8,128)(2,1)S(1)}, bf16[128,2048]{1,0:T(8,128)(2,1)S(1)}, u32[]{:S(2)}, u32[]{:S(2)}) collective-permute-start(bf16[128,2048]{1,0:T(8,128)(2,1)S(1)} %join.6.refs_0_), channel_id=1, source_target_pairs={{0,2},{1,3},{2,0},{3,1},{4,6},{5,7},{6,4},{7,5},{8,10},{9,11},{10,... | collective-permute-start | bytes 1572872 | tf_op jit(solution)/shard_map/ppermute | solution.py:36
  16.4 14.6 %collective-permute-start.1 = (bf16[256,1024]{1,0:T(8,128)(2,1)S(1)}, bf16[256,1024]{1,0:T(8,128)(2,1)S(1)}, u32[]{:S(2)}, u32[]{:S(2)}) collective-permute-start(bf16[256,1024]{1,0:T(8,128)(2,1)S(1)} %collective-permute-done.rest_1_), channel_id=1, source_target_pairs={{0,8},{1,9},{2,10},{3,11},{4,12},{5,13},{6,14},{7,15},{8,16},{9,17... | collective-permute-start | bytes 1572872 | tf_op jit(solution)/shard_map/ppermute | solution.py:36
  20.8 23.9 %collective-permute-start.6 = (bf16[256,2048]{1,0:T(8,128)(2,1)S(1)}, bf16[256,2048]{1,0:T(8,128)(2,1)}, u32[]{:S(2)}, u32[]{:S(2)}) collective-permute-start(bf16[256,2048]{1,0:T(8,128)(2,1)S(1)} %join.5.refs_0_), channel_id=1, source_target_pairs={{0,2},{1,3},{2,0},{3,1},{4,6},{5,7},{6,4},{7,5},{8,10},{9,11},{10,... | collective-permute-start | bytes 3145736 | tf_op jit(solution)/shard_map/ppermute | solution.py:36
  23.4 23.8 %collective-permute-start.8 = (bf16[256,2048]{1,0:T(8,128)(2,1)}, bf16[256,2048]{1,0:T(8,128)(2,1)}, u32[]{:S(2)}, u32[]{:S(2)}) collective-permute-start(bf16[256,2048]{1,0:T(8,128)(2,1)} %join.7.refs_2_), channel_id=1, source_target_pairs={{0,1},{1,0},{2,3},{3,2},{4,5},{5,4},{6,7},{7,6},{8,9},{9,8},{10,11... | collective-permute-start | bytes 3145736 | tf_op jit(solution)/shard_map/ppermute | solution.py:36
  48.2 10.2 %collective-permute-start.10 = (bf16[256,2048]{1,0:T(8,128)(2,1)}, bf16[256,2048]{1,0:T(8,128)(2,1)S(1)}, u32[]{:S(2)}, u32[]{:S(2)}) collective-permute-start(bf16[256,2048]{1,0:T(8,128)(2,1)} %get-tuple-element.31.refs_5_), channel_id=1, source_target_pairs={{0,4},{1,5},{2,6},{3,7},{4,0},{5,1},{6,2},{7,3},{8,12},{9,13},{10,... | collective-permute-start | bytes 3145736 | tf_op jit(solution)/shard_map/ppermute | solution.py:36
  48.2 10.2 %collective-permute-start.11 = (bf16[256,2048]{1,0:T(8,128)(2,1)}, bf16[256,2048]{1,0:T(8,128)(2,1)}, u32[]{:S(2)}, u32[]{:S(2)}) collective-permute-start(bf16[256,2048]{1,0:T(8,128)(2,1)} %get-tuple-element.32.refs_4_), channel_id=1, source_target_pairs={{0,4},{1,5},{2,6},{3,7},{4,0},{5,1},{6,2},{7,3},{8,12},{9,13},{10,... | collective-permute-start | bytes 3145736 | tf_op jit(solution)/shard_map/ppermute | solution.py:36
  48.7 9.7 %collective-permute-start.12 = (bf16[256,2048]{1,0:T(8,128)(2,1)}, bf16[256,2048]{1,0:T(8,128)(2,1)}, u32[]{:S(2)}, u32[]{:S(2)}) collective-permute-start(bf16[256,2048]{1,0:T(8,128)(2,1)} %get-tuple-element.33.refs_5_), channel_id=1, source_target_pairs={{0,4},{1,5},{2,6},{3,7},{4,0},{5,1},{6,2},{7,3},{8,12},{9,13},{10,... | collective-permute-start | bytes 3145736 | tf_op jit(solution)/shard_map/ppermute | solution.py:36
  48.7 9.7 %collective-permute-start.9 = (bf16[256,2048]{1,0:T(8,128)(2,1)S(1)}, bf16[256,2048]{1,0:T(8,128)(2,1)S(1)}, u32[]{:S(2)}, u32[]{:S(2)}) collective-permute-start(bf16[256,2048]{1,0:T(8,128)(2,1)S(1)} %get-tuple-element.30.refs_4_), channel_id=1, source_target_pairs={{0,4},{1,5},{2,6},{3,7},{4,0},{5,1},{6,2},{7,3},{8,12},{9,13},{10,... | collective-permute-start | bytes 3145736 | tf_op jit(solution)/shard_map/ppermute | solution.py:36
  49.2 9.2 %all-to-all-start = ((bf16[4,32,1024]{2,1,0:T(8,128)(2,1)}), bf16[4,32,1024]{2,1,0:T(8,128)(2,1)S(1)}, u32[]{:S(2)}, u32[]{:S(2)}) async-start(bf16[4,32,1024]{2,1,0:T(8,128)(2,1)} %get-tuple-element.29.refs_4_), calls=%async_computation | async-start | bytes 524288 | tf_op jit(solution)/shard_map/all_to_all | solution.py:321
  64.1 8.8 %all-to-all-start.1 = ((bf16[4,32,1024]{2,1,0:T(8,128)(2,1)}), bf16[4,32,1024]{2,1,0:T(8,128)(2,1)S(1)}, u32[]{:S(2)}, u32[]{:S(2)}) async-start(bf16[4,32,1024]{2,1,0:T(8,128)(2,1)} %get-tuple-element.42), calls=%async_computation.1 | async-start | bytes 524288 | tf_op jit(solution)/shard_map/all_to_all | solution.py:321
  72.5 16.5 %collective-permute-start.16 = (bf16[64,2048]{1,0:T(8,128)(2,1)}, bf16[64,2048]{1,0:T(8,128)(2,1)}, u32[]{:S(2)}, u32[]{:S(2)}) collective-permute-start(bf16[64,2048]{1,0:T(8,128)(2,1)} %get-tuple-element.39), channel_id=1, source_target_pairs={{0,8},{1,9},{2,10},{3,11},{4,12},{5,13},{6,14},{7,15},{8,0},{9,1},... | collective-permute-start | bytes 786440 | tf_op jit(solution)/shard_map/ppermute | solution.py:36
  73.4 9.1 %collective-permute-start.20 = (bf16[32,1024]{1,0:T(8,128)(2,1)S(1)}, bf16[32,1024]{1,0:T(8,128)(2,1)S(1)}, u32[]{:S(2)}, u32[]{:S(2)}) collective-permute-start(bf16[32,1024]{1,0:T(8,128)(2,1)S(1)} %get-tuple-element.43), channel_id=1, source_target_pairs={{0,24},{1,25},{2,26},{3,27},{4,28},{5,29},{6,30},{7,31},{8,16},{9,... | collective-permute-start | bytes 196616 | tf_op jit(solution)/shard_map/ppermute | solution.py:36
  75.3 9.4 %collective-permute-start.21 = (bf16[32,1024]{1,0:T(8,128)(2,1)S(1)}, bf16[32,1024]{1,0:T(8,128)(2,1)S(1)}, u32[]{:S(2)}, u32[]{:S(2)}) collective-permute-start(bf16[32,1024]{1,0:T(8,128)(2,1)S(1)} %get-tuple-element.44), channel_id=1, source_target_pairs={{0,8},{1,9},{2,10},{3,11},{4,12},{5,13},{6,14},{7,15},{8,0},{9,1},... | collective-permute-start | bytes 196616 | tf_op jit(solution)/shard_map/ppermute | solution.py:36
  76.0 8.7 %collective-permute-start.22 = (bf16[32,1024]{1,0:T(8,128)(2,1)S(1)}, bf16[32,1024]{1,0:T(8,128)(2,1)S(1)}, u32[]{:S(2)}, u32[]{:S(2)}) collective-permute-start(bf16[32,1024]{1,0:T(8,128)(2,1)S(1)} %get-tuple-element.45), channel_id=1, source_target_pairs={{0,16},{1,17},{2,18},{3,19},{4,20},{5,21},{6,22},{7,23},{8,24},{9,... | collective-permute-start | bytes 196616 | tf_op jit(solution)/shard_map/ppermute | solution.py:36
  80.9 11.1 %collective-permute-start.18 = (bf16[64,2048]{1,0:T(8,128)(2,1)S(1)}, bf16[64,2048]{1,0:T(8,128)(2,1)S(1)}, u32[]{:S(2)}, u32[]{:S(2)}) collective-permute-start(bf16[64,2048]{1,0:T(8,128)(2,1)S(1)} %get-tuple-element.41), channel_id=1, source_target_pairs={{0,8},{1,9},{2,10},{3,11},{4,12},{5,13},{6,14},{7,15},{8,0},{9,1},... | collective-permute-start | bytes 786440 | tf_op jit(solution)/shard_map/ppermute | solution.py:36
  87.6 13.9 %collective-permute-start.27 = (bf16[64,2048]{1,0:T(8,128)(2,1)S(1)}, bf16[64,2048]{1,0:T(8,128)(2,1)S(1)}, u32[]{:S(2)}, u32[]{:S(2)}) collective-permute-start(bf16[64,2048]{1,0:T(8,128)(2,1)S(1)} %get-tuple-element.52), channel_id=1, source_target_pairs={{0,8},{1,9},{2,10},{3,11},{4,12},{5,13},{6,14},{7,15},{8,0},{9,1},... | collective-permute-start | bytes 786440 | tf_op jit(solution)/shard_map/ppermute | solution.py:36
  90.0 18.8 %collective-permute-start.17 = (bf16[32,2048]{1,0:T(8,128)(2,1)S(1)}, bf16[32,2048]{1,0:T(8,128)(2,1)S(1)}, u32[]{:S(2)}, u32[]{:S(2)}) collective-permute-start(bf16[32,2048]{1,0:T(8,128)(2,1)S(1)} %fusion.6.refs_8_), channel_id=1, source_target_pairs={{0,16},{1,17},{2,18},{3,19},{4,20},{5,21},{6,22},{7,23},{8,24},{9,... | collective-permute-start | bytes 393224 | tf_op jit(solution)/shard_map/ppermute | solution.py:36
  92.0 16.9 %collective-permute-start.19 = (bf16[32,2048]{1,0:T(8,128)(2,1)S(1)}, bf16[32,2048]{1,0:T(8,128)(2,1)S(1)}, u32[]{:S(2)}, u32[]{:S(2)}) collective-permute-start(bf16[32,2048]{1,0:T(8,128)(2,1)S(1)} %fusion.3), channel_id=1, source_target_pairs={{0,16},{1,17},{2,18},{3,19},{4,20},{5,21},{6,22},{7,23},{8,24},{9,... | collective-permute-start | bytes 393224 | tf_op jit(solution)/shard_map/ppermute | solution.py:36
  94.8 9.9 %collective-permute-start.23 = (bf16[64,1024]{1,0:T(8,128)(2,1)S(1)}, bf16[64,1024]{1,0:T(8,128)(2,1)S(1)}, u32[]{:S(2)}, u32[]{:S(2)}) collective-permute-start(bf16[64,1024]{1,0:T(8,128)(2,1)S(1)} %get-tuple-element.48), channel_id=1, source_target_pairs={{0,8},{1,9},{2,10},{3,11},{4,12},{5,13},{6,14},{7,15},{8,0},{9,1},... | collective-permute-start | bytes 393224 | tf_op jit(solution)/shard_map/ppermute | solution.py:36
  98.9 9.8 %collective-permute-start.25 = (bf16[64,1024]{1,0:T(8,128)(2,1)S(1)}, bf16[64,1024]{1,0:T(8,128)(2,1)S(1)}, u32[]{:S(2)}, u32[]{:S(2)}) collective-permute-start(bf16[64,1024]{1,0:T(8,128)(2,1)S(1)} %get-tuple-element.50), channel_id=1, source_target_pairs={{0,8},{1,9},{2,10},{3,11},{4,12},{5,13},{6,14},{7,15},{8,0},{9,1},... | collective-permute-start | bytes 393224 | tf_op jit(solution)/shard_map/ppermute | solution.py:36
  101.6 10.1 %collective-permute-start.28 = (bf16[32,2048]{1,0:T(8,128)(2,1)S(1)}, bf16[32,2048]{1,0:T(8,128)(2,1)S(1)}, u32[]{:S(2)}, u32[]{:S(2)}) collective-permute-start(bf16[32,2048]{1,0:T(8,128)(2,1)S(1)} %fusion), channel_id=1, source_target_pairs={{0,16},{1,17},{2,18},{3,19},{4,20},{5,21},{6,22},{7,23},{8,24},{9,... | collective-permute-start | bytes 393224 | tf_op jit(solution)/shard_map/ppermute | solution.py:36
  104.8 8.5 %collective-permute-start.24 = (bf16[32,1024]{1,0:T(8,128)(2,1)S(1)}, bf16[32,1024]{1,0:T(8,128)(2,1)S(1)}, u32[]{:S(2)}, u32[]{:S(2)}) collective-permute-start(bf16[32,1024]{1,0:T(8,128)(2,1)S(1)} %fusion.12), channel_id=1, source_target_pairs={{0,16},{1,17},{2,18},{3,19},{4,20},{5,21},{6,22},{7,23},{8,24},{9,... | collective-permute-start | bytes 196616 | tf_op jit(solution)/shard_map/ppermute | solution.py:36
  (15 other events, 84.5 us)
